TPU v7x, 128 devices: a whole 4x4x4 slice. The times are simulated.
128 devices in a mesh: dom: 8 (over z, core), blk: 16 (over x, y).
Axes of the slice: x: 4, y: 4, z: 4, core: 2. Of those that a mesh axis runs over, the one named last changes fastest.
Arguments:
- node_owner: int32 [131072, 1], P(('dom', 'blk')), may hold values from 0 to 127; in each aligned block of 1024 rows (0 to 1023, 1024 to 2047, ...) at most 16 rows name the same one
- node_qrow: int32 [131072], P(('dom', 'blk')), may hold values from 0 to 1023
- node_rem: int32 [131072], P(('dom', 'blk')), may hold values from 0 to 1023
- quotient: bfloat16 [131072, 256], P(('dom', 'blk')), may hold values from -5 to 5
- remainder: bfloat16 [1024, 256], replicated, may hold values from -5 to 5
- edge_src: int32 [1024, 6144], P(('dom', 'blk')), may hold values from 0 to 16895, as said below
- edge_dst: int32 [1024, 6144], P(('dom', 'blk')), may hold values from 0 to 127
- block_count: int32 [1024], P(('dom', 'blk')), may hold values from 1024 to 6144, as said below
- w_self: bfloat16 [256, 256], replicated, may hold values from -0.375 to 0.375
- w_neigh: bfloat16 [256, 256], replicated, may hold values from -0.375 to 0.375
- bias: float32 [256], replicated, may hold values from -3 to 3
- cotangent: bfloat16 [131072, 256], P(('dom', 'blk')), may hold values from -6 to 6
Outputs:
- out: bfloat16 [131072, 256], P(('dom', 'blk'))
- d_quotient: float32 [131072, 256], P(('dom', 'blk'))
- d_remainder: float32 [1024, 256], replicated
- d_w_self: float32 [256, 256], replicated
- d_w_neigh: float32 [256, 256], replicated
- d_bias: float32 [256], replicated
Inputs may be any that keep to these rules, and one draw needn't show every extreme that they name: `node_owner`: among the nodes of one device no device is named more than 16 times, and exactly 16 times in some devices' nodes. `edge_src`: indexes the source rows of the block's device as the steps state. `block_count`: some block has all 6144 slots live.
All inputs are finite; a program needn't handle non-finite values.
Results may differ from a plain program's by a relative error of at most 0.008.
Values may be sent and summed in bfloat16 or wider, within the bound.
A program may use at most 128 MiB of HBM per device.

v0:
```python
import math

import jax
import jax.numpy as jnp
from jax import lax
from jax.sharding import PartitionSpec as P

ROWS_BLK = 128
HALO = 256


def padded(block, sides, width):
    for axis, dim in sides:
        count = lax.axis_size(axis)
        forward = [(i, i + 1) for i in range(count - 1)]
        forward.append((count - 1, 0))
        backward = [(target, source) for source, target in forward]
        low = lax.ppermute(
            lax.slice_in_dim(block, block.shape[dim] - width, None, axis=dim), axis, forward
        )
        high = lax.ppermute(lax.slice_in_dim(block, 0, width, axis=dim), axis, backward)
        block = jnp.concatenate([low, block, high], axis=dim)
    return block


def shifted(block, axis, distance):
    devices = range(lax.axis_size(axis))
    route = [((i - distance) % len(devices), i) for i in devices]
    return lax.ppermute(block, axis, route)


def block_adjacency(src_row, dst_row, filled, width):
    live_slot = (jnp.arange(src_row.shape[0], dtype=jnp.int32) < filled).astype(jnp.bfloat16)
    flat_index = dst_row * width + src_row
    adjacency = jnp.zeros((ROWS_BLK * width,), jnp.bfloat16).at[flat_index].add(live_slot)
    return adjacency.reshape(ROWS_BLK, width)


def send_ids(buffer):
    return lax.all_to_all(buffer, ("dom", "blk"), split_axis=0, concat_axis=0, tiled=True)


def send_rows(buffer):
    return lax.all_to_all(buffer, ("dom", "blk"), split_axis=0, concat_axis=0, tiled=True)


def send_grads(buffer):
    return lax.all_to_all(
        buffer.astype(jnp.bfloat16), ("dom", "blk"), split_axis=0, concat_axis=0, tiled=True
    ).astype(buffer.dtype)


def forward_block(source_rows, src_row, dst_row, filled):
    adjacency = block_adjacency(src_row, dst_row, filled, source_rows.shape[0])
    summed = jnp.dot(adjacency, source_rows, preferred_element_type=jnp.float32)
    return (summed, jnp.sum(adjacency.astype(jnp.float32), axis=1))


def backward_block(accum, src_row, dst_row, filled, scaled_blk):
    contract_rows = (((0,), (0,)), ((), ()))
    adjacency = block_adjacency(src_row, dst_row, filled, accum.shape[0])
    return accum + lax.dot_general(
        adjacency, scaled_blk, contract_rows, preferred_element_type=jnp.float32
    )


def per_device(
    node_owner,
    node_qrow,
    node_rem,
    quotient,
    remainder,
    edge_src,
    edge_dst,
    block_count,
    w_self,
    w_neigh,
    bias,
    cotangent,
):
    nodes_dev = node_qrow.shape[0]
    feature_dim = quotient.shape[1]
    devices = lax.axis_size("dom") * lax.axis_size("blk")
    slot_cap = 2 * nodes_dev // devices
    owner_dev = node_owner[:, 0]
    owner_hot = (owner_dev[:, None] == jnp.arange(devices, dtype=jnp.int32)[None, :]).astype(
        jnp.bfloat16
    )
    row_ids = jnp.arange(nodes_dev, dtype=jnp.int32)
    lower_mask = (row_ids[:, None] > row_ids[None, :]).astype(jnp.bfloat16)
    earlier = jnp.dot(lower_mask, owner_hot, preferred_element_type=jnp.float32)
    slot_rank = jnp.sum(earlier * owner_hot.astype(jnp.float32), axis=1).astype(jnp.int32)
    slot_index = owner_dev * slot_cap + slot_rank
    requests = jnp.zeros((devices * slot_cap,), jnp.int32).at[slot_index].set(node_qrow)
    asked_rows = send_ids(requests.reshape(devices, slot_cap)).reshape(devices * slot_cap)
    served = quotient[asked_rows].reshape(devices, slot_cap, feature_dim)
    returned = send_rows(served).reshape(devices * slot_cap, feature_dim)
    quot_rows = returned[slot_index].astype(jnp.float32)
    remain_rows = remainder[node_rem].astype(jnp.float32)
    features = (quot_rows * remain_rows).astype(jnp.bfloat16)
    part_gathered = lax.all_gather(features, "blk", axis=0, tiled=True)
    extended = padded(features, (("dom", 0),), HALO)
    source_rows = jnp.concatenate(
        [part_gathered, extended[:HALO], extended[extended.shape[0] - HALO :]], axis=0
    )

    def map_forward(inner):
        src_row, dst_row, filled = inner
        return forward_block(source_rows, src_row, dst_row, filled)

    agg_sum, degree = lax.map(map_forward, (edge_src, edge_dst, block_count))
    agg_sum = agg_sum.reshape(nodes_dev, feature_dim)
    divisor = jnp.maximum(degree.reshape(nodes_dev), 1.0)
    neighbour = (agg_sum / divisor[:, None]).astype(jnp.bfloat16)
    preact = (
        jnp.dot(features, w_self, preferred_element_type=jnp.float32)
        + jnp.dot(neighbour, w_neigh, preferred_element_type=jnp.float32)
        + bias
    )
    sigma = jax.nn.sigmoid(preact)
    out = (preact * sigma).astype(jnp.bfloat16)
    dpre = (cotangent.astype(jnp.float32) * sigma * (1.0 + preact * (1.0 - sigma))).astype(
        jnp.bfloat16
    )
    contract_rows = (((0,), (0,)), ((), ()))
    contract_cols = (((1,), (1,)), ((), ()))
    local_self = lax.dot_general(features, dpre, contract_rows, preferred_element_type=jnp.float32)
    local_neigh = lax.dot_general(
        neighbour, dpre, contract_rows, preferred_element_type=jnp.float32
    )
    local_bias = jnp.sum(dpre.astype(jnp.float32), axis=0)
    dagg = lax.dot_general(dpre, w_neigh, contract_cols, preferred_element_type=jnp.float32)
    dagg_scaled = (dagg / divisor[:, None]).astype(jnp.bfloat16)
    dx_self = lax.dot_general(dpre, w_self, contract_cols, preferred_element_type=jnp.float32)
    scaled_blocks = dagg_scaled.reshape(edge_src.shape[0], ROWS_BLK, feature_dim)

    def scan_backward(accum, inner):
        src_row, dst_row, filled, scaled_blk = inner
        return (backward_block(accum, src_row, dst_row, filled, scaled_blk), None)

    start_grad = jnp.zeros((source_rows.shape[0], feature_dim), jnp.float32)
    source_grad, unused = lax.scan(
        scan_backward, start_grad, (edge_src, edge_dst, block_count, scaled_blocks)
    )
    part_nodes = source_rows.shape[0] - 2 * HALO
    own_grads = lax.psum_scatter(
        source_grad[:part_nodes].astype(jnp.bfloat16), "blk", scatter_dimension=0, tiled=True
    ).astype(jnp.float32)
    tail_grad = shifted(source_grad[part_nodes : part_nodes + HALO].astype(jnp.bfloat16), "dom", -1)
    head_grad = shifted(source_grad[part_nodes + HALO :].astype(jnp.bfloat16), "dom", 1)
    grad_x = dx_self + own_grads
    grad_x = grad_x + jnp.pad(head_grad.astype(jnp.float32), ((0, nodes_dev - HALO), (0, 0)))
    grad_x = grad_x + jnp.pad(tail_grad.astype(jnp.float32), ((nodes_dev - HALO, 0), (0, 0)))
    outgoing = (
        jnp.zeros((devices * slot_cap, feature_dim), jnp.float32)
        .at[slot_index]
        .set(grad_x * remain_rows)
    )
    incoming = send_grads(outgoing.reshape(devices, slot_cap, feature_dim)).reshape(
        devices * slot_cap, feature_dim
    )
    d_quotient = jax.ops.segment_sum(incoming, asked_rows, num_segments=quotient.shape[0])
    local_remain = jax.ops.segment_sum(
        grad_x * quot_rows, node_rem, num_segments=remainder.shape[0]
    )
    summed_self, summed_neigh, summed_bias, summed_remain = lax.psum(
        (local_self, local_neigh, local_bias, local_remain), ("dom", "blk")
    )
    nodes_total = nodes_dev * devices
    weight_scale = 1.0 / math.sqrt(nodes_total)
    remain_scale = math.sqrt(remainder.shape[0] / nodes_total)
    return (
        out,
        d_quotient,
        summed_remain * remain_scale,
        summed_self * weight_scale,
        summed_neigh * weight_scale,
        summed_bias * weight_scale,
    )


def solution(mesh):
    placed = (
        P(("dom", "blk"), None),
        P(("dom", "blk")),
        P(("dom", "blk")),
        P(("dom", "blk"), None),
        P(),
        P(("dom", "blk"), None),
        P(("dom", "blk"), None),
        P(("dom", "blk")),
        P(),
        P(),
        P(),
        P(("dom", "blk"), None),
    )
    return jax.shard_map(
        per_device,
        mesh=mesh,
        in_specs=placed,
        out_specs=(P(("dom", "blk"), None), P(("dom", "blk"), None), P(), P(), P(), P()),
        check_vma=False,
    )
```

profile of v0, /device:TPU:1, one launch (start us, length us, event | category | flops | bytes accessed | tf_op | source)
XLA Modules:
  0.0 1554.4 jit_solution(238234375723441070)
XLA Ops:
  13.9 20.9 %all_to_all.19 = s32[128,1,16]{2,1,0:T(1,128)S(1)} all-to-all(s32[128,1,16]{2,1,0:T(1,128)S(1)} %bitcast.80), channel_id=1, replica_groups=mesh['dom'=8,'blk'=16] {'dom','blk'}, dimensions={0} | all-to-all | bytes 16384 | tf_op jit(solution)/shard_map/all_to_all | solution.py:40
  81.4 59.0 %all-gather.2.cloned.1.call-done = bf16[16384,256]{1,0:T(8,128)(2,1)} async-done(((bf16[1024,256]{1,0:T(8,128)(2,1)}), bf16[16384,256]{1,0:T(8,128)(2,1)}) %all-gather.2.cloned.1.call-update) | async-done | bytes 8388624 | tf_op jit(solution)/shard_map/all_gather | solution.py:101
  140.4 29.2 %pad_maximum_fusion = bf16[16896,256]{1,0:T(8,128)(2,1)} fusion(bf16[256,256]{1,0:T(8,128)(2,1)S(1)} %collective-permute-done.1, bf16[256,256]{1,0:T(8,128)(2,1)S(1)} %collective-permute-done, bf16[16384,256]{1,0:T(8,128)(2,1)} %all-gather.2.cloned.1.call-done), kind=kLoop, calls=%fused_computation.26 | loop fusion | flops 25952256 | bytes 17301504 | tf_op jit(solution)/shard_map/concatenate | solution.py:103
  169.7 520.9 %while.23 = (s32[]{:T(128)}, f32[8,128,256]{2,1,0:T(8,128)S(1)}, f32[8,128]{1,0:T(8,128)S(1)}, s32[8,6144]{1,0:T(8,128)}, s32[8,6144]{1,0:T(8,128)}, /*index=5*/...) while((s32[]{:T(128)}, f32[8,128,256]{2,1,0:T(8,128)S(1)}, ...), condition=%wide.region_5.6_spmd, body=%wide.region_2.5_spmd.sunk | while | flops 1111670656 | bytes 47797924 | solution.py:111
  172.6 45.6 %scatter_custom_fusion.18 = bf16[2162688]{0:T(1024)(128)(2,1)} fusion(s32[6144]{0:T(1024)S(1)} %bitcast.77, bf16[6144]{0:T(1024)(128)(2,1)S(1)} %fusion.63, bf16[]{:T(256)} %constant.41.clone.1..sunk), kind=kCustom, calls=%fused_computation.10.clone.1 | custom fusion | flops 6144 | bytes 4325378 | tf_op jit(solution)/shard_map/while/body/eval_jaxpr/scatter-add | solution.py:35
  237.6 45.6 %scatter_custom_fusion.18 = bf16[2162688]{0:T(1024)(128)(2,1)} fusion(s32[6144]{0:T(1024)S(1)} %bitcast.77, bf16[6144]{0:T(1024)(128)(2,1)S(1)} %fusion.63, bf16[]{:T(256)} %constant.41.clone.1..sunk), kind=kCustom, calls=%fused_computation.10.clone.1 | custom fusion | flops 6144 | bytes 4325378 | tf_op jit(solution)/shard_map/while/body/eval_jaxpr/scatter-add | solution.py:35
  302.7 45.6 %scatter_custom_fusion.18 = bf16[2162688]{0:T(1024)(128)(2,1)} fusion(s32[6144]{0:T(1024)S(1)} %bitcast.77, bf16[6144]{0:T(1024)(128)(2,1)S(1)} %fusion.63, bf16[]{:T(256)} %constant.41.clone.1..sunk), kind=kCustom, calls=%fused_computation.10.clone.1 | custom fusion | flops 6144 | bytes 4325378 | tf_op jit(solution)/shard_map/while/body/eval_jaxpr/scatter-add | solution.py:35
  367.7 45.6 %scatter_custom_fusion.18 = bf16[2162688]{0:T(1024)(128)(2,1)} fusion(s32[6144]{0:T(1024)S(1)} %bitcast.77, bf16[6144]{0:T(1024)(128)(2,1)S(1)} %fusion.63, bf16[]{:T(256)} %constant.41.clone.1..sunk), kind=kCustom, calls=%fused_computation.10.clone.1 | custom fusion | flops 6144 | bytes 4325378 | tf_op jit(solution)/shard_map/while/body/eval_jaxpr/scatter-add | solution.py:35
  432.8 45.6 %scatter_custom_fusion.18 = bf16[2162688]{0:T(1024)(128)(2,1)} fusion(s32[6144]{0:T(1024)S(1)} %bitcast.77, bf16[6144]{0:T(1024)(128)(2,1)S(1)} %fusion.63, bf16[]{:T(256)} %constant.41.clone.1..sunk), kind=kCustom, calls=%fused_computation.10.clone.1 | custom fusion | flops 6144 | bytes 4325378 | tf_op jit(solution)/shard_map/while/body/eval_jaxpr/scatter-add | solution.py:35
  497.8 45.6 %scatter_custom_fusion.18 = bf16[2162688]{0:T(1024)(128)(2,1)} fusion(s32[6144]{0:T(1024)S(1)} %bitcast.77, bf16[6144]{0:T(1024)(128)(2,1)S(1)} %fusion.63, bf16[]{:T(256)} %constant.41.clone.1..sunk), kind=kCustom, calls=%fused_computation.10.clone.1 | custom fusion | flops 6144 | bytes 4325378 | tf_op jit(solution)/shard_map/while/body/eval_jaxpr/scatter-add | solution.py:35
  562.9 45.6 %scatter_custom_fusion.18 = bf16[2162688]{0:T(1024)(128)(2,1)} fusion(s32[6144]{0:T(1024)S(1)} %bitcast.77, bf16[6144]{0:T(1024)(128)(2,1)S(1)} %fusion.63, bf16[]{:T(256)} %constant.41.clone.1..sunk), kind=kCustom, calls=%fused_computation.10.clone.1 | custom fusion | flops 6144 | bytes 4325378 | tf_op jit(solution)/shard_map/while/body/eval_jaxpr/scatter-add | solution.py:35
  627.9 45.6 %scatter_custom_fusion.18 = bf16[2162688]{0:T(1024)(128)(2,1)} fusion(s32[6144]{0:T(1024)S(1)} %bitcast.77, bf16[6144]{0:T(1024)(128)(2,1)S(1)} %fusion.63, bf16[]{:T(256)} %constant.41.clone.1..sunk), kind=kCustom, calls=%fused_computation.10.clone.1 | custom fusion | flops 6144 | bytes 4325378 | tf_op jit(solution)/shard_map/while/body/eval_jaxpr/scatter-add | solution.py:35
  694.0 572.9 %while.24 = (s32[]{:T(128)}, f32[16896,256]{1,0:T(8,128)}, s32[8,6144]{1,0:T(8,128)}, s32[8,6144]{1,0:T(8,128)}, s32[8]{0:T(128)S(1)}, /*index=5*/bf16[8,128,256...) while((s32[]{:T(128)}, f32[16896,256]{1,0:T(8,128)}, s32[8,6144]{1,0:T(8,128)}, ...), condition=%wide.region_8.9_spmd.clone, body=%wide.region_6.8_spmd.clone.sunk | while | flops 1115996160 | bytes 52056200 | solution.py:142
  696.5 45.5 %scatter_custom_fusion.20 = bf16[2162688]{0:T(1024)(128)(2,1)} fusion(s32[6144]{0:T(1024)S(1)} %bitcast.78, bf16[6144]{0:T(1024)(128)(2,1)S(1)} %fusion.68, bf16[]{:T(256)} %constant.41.clone.1..sunk.1), kind=kCustom, calls=%fused_computation.18.clone.1 | custom fusion | flops 6144 | bytes 4325378 | tf_op jit(solution)/shard_map/while/body/eval_jaxpr/scatter-add | solution.py:35
  763.7 45.5 %scatter_custom_fusion.20 = bf16[2162688]{0:T(1024)(128)(2,1)} fusion(s32[6144]{0:T(1024)S(1)} %bitcast.78, bf16[6144]{0:T(1024)(128)(2,1)S(1)} %fusion.68, bf16[]{:T(256)} %constant.41.clone.1..sunk.1), kind=kCustom, calls=%fused_computation.18.clone.1 | custom fusion | flops 6144 | bytes 4325378 | tf_op jit(solution)/shard_map/while/body/eval_jaxpr/scatter-add | solution.py:35
  835.9 45.5 %scatter_custom_fusion.20 = bf16[2162688]{0:T(1024)(128)(2,1)} fusion(s32[6144]{0:T(1024)S(1)} %bitcast.78, bf16[6144]{0:T(1024)(128)(2,1)S(1)} %fusion.68, bf16[]{:T(256)} %constant.41.clone.1..sunk.1), kind=kCustom, calls=%fused_computation.18.clone.1 | custom fusion | flops 6144 | bytes 4325378 | tf_op jit(solution)/shard_map/while/body/eval_jaxpr/scatter-add | solution.py:35
  908.1 45.5 %scatter_custom_fusion.20 = bf16[2162688]{0:T(1024)(128)(2,1)} fusion(s32[6144]{0:T(1024)S(1)} %bitcast.78, bf16[6144]{0:T(1024)(128)(2,1)S(1)} %fusion.68, bf16[]{:T(256)} %constant.41.clone.1..sunk.1), kind=kCustom, calls=%fused_computation.18.clone.1 | custom fusion | flops 6144 | bytes 4325378 | tf_op jit(solution)/shard_map/while/body/eval_jaxpr/scatter-add | solution.py:35
  980.4 45.5 %scatter_custom_fusion.20 = bf16[2162688]{0:T(1024)(128)(2,1)} fusion(s32[6144]{0:T(1024)S(1)} %bitcast.78, bf16[6144]{0:T(1024)(128)(2,1)S(1)} %fusion.68, bf16[]{:T(256)} %constant.41.clone.1..sunk.1), kind=kCustom, calls=%fused_computation.18.clone.1 | custom fusion | flops 6144 | bytes 4325378 | tf_op jit(solution)/shard_map/while/body/eval_jaxpr/scatter-add | solution.py:35
  1052.6 45.5 %scatter_custom_fusion.20 = bf16[2162688]{0:T(1024)(128)(2,1)} fusion(s32[6144]{0:T(1024)S(1)} %bitcast.78, bf16[6144]{0:T(1024)(128)(2,1)S(1)} %fusion.68, bf16[]{:T(256)} %constant.41.clone.1..sunk.1), kind=kCustom, calls=%fused_computation.18.clone.1 | custom fusion | flops 6144 | bytes 4325378 | tf_op jit(solution)/shard_map/while/body/eval_jaxpr/scatter-add | solution.py:35
  1124.8 45.5 %scatter_custom_fusion.20 = bf16[2162688]{0:T(1024)(128)(2,1)} fusion(s32[6144]{0:T(1024)S(1)} %bitcast.78, bf16[6144]{0:T(1024)(128)(2,1)S(1)} %fusion.68, bf16[]{:T(256)} %constant.41.clone.1..sunk.1), kind=kCustom, calls=%fused_computation.18.clone.1 | custom fusion | flops 6144 | bytes 4325378 | tf_op jit(solution)/shard_map/while/body/eval_jaxpr/scatter-add | solution.py:35
  1197.0 45.5 %scatter_custom_fusion.20 = bf16[2162688]{0:T(1024)(128)(2,1)} fusion(s32[6144]{0:T(1024)S(1)} %bitcast.78, bf16[6144]{0:T(1024)(128)(2,1)S(1)} %fusion.68, bf16[]{:T(256)} %constant.41.clone.1..sunk.1), kind=kCustom, calls=%fused_computation.18.clone.1 | custom fusion | flops 6144 | bytes 4325378 | tf_op jit(solution)/shard_map/while/body/eval_jaxpr/scatter-add | solution.py:35
  1286.1 77.7 %reduce-scatter.2.cloned.1.call-done = bf16[1024,256]{1,0:T(8,128)(2,1)} async-done(((bf16[16384,256]{1,0:T(8,128)(2,1)}), bf16[1024,256]{1,0:T(8,128)(2,1)}) %reduce-scatter.2.cloned.1.call-update) | async-done | bytes 524304 | tf_op jit(solution)/shard_map/reduce_scatter | solution.py:146
  1392.1 71.9 %psum.31 = f32[256]{0:T(256)S(1)} all-reduce(f32[256]{0:T(256)S(1)} %get-tuple-element.129), channel_id=1, replica_groups=mesh['dom'=8,'blk'=16] {'dom','blk'}, use_global_device_ids=true, to_apply=%region_17.18 | all-reduce | flops 256 | bytes 2048 | tf_op jit(solution)/shard_map/psum | solution.py:166
  1464.6 66.2 %all-reduce.5.cloned.1.call-done = (f32[1024,256]{1,0:T(8,128)}, f32[256,256]{1,0:T(8,128)}, f32[256,256]{1,0:T(8,128)}) async-done(((f32[1024,256]{1,0:T(8,128)}, f32[256,256]{1,0:T(8,128)}, f32[256,256]{1,0:T(8,128)}), (f32[1024,256]{1,0:T(8,128)}, f32[256,256]{1,0:T(8,128)}, f32[256,256]{1,0:T(8,128)})) %all-reduce.5.cloned.1.call-update) | async-done | bytes 1572880 | tf_op jit(solution)/shard_map/psum | solution.py:166
  (207 shorter events, 484.8 us)
Async XLA Ops:
  7.2 29.1 %copy-start = (bf16[1024,256]{1,0:T(8,128)(2,1)S(1)}, bf16[1024,256]{1,0:T(8,128)(2,1)}, u32[]{:S(2)}) copy-start(bf16[1024,256]{1,0:T(8,128)(2,1)} %param.19) | copy-start | bytes 1572868
  9.3 44.6 %copy-start.14 = (s32[1024,1]{0,1:T(1,128)}, s32[1024,1]{0,1:T(1,128)S(1)}, u32[]{:S(2)}) copy-start(s32[1024,1]{0,1:T(1,128)S(1)} %compare_select_fusion.3) | copy-start | bytes 12292
  36.2 13.6 copy-start.4
  45.3 23.1 %all-to-all-start.1 = ((bf16[128,16,256]{2,1,0:T(8,128)(2,1)}), bf16[128,16,256]{2,1,0:T(8,128)(2,1)S(1)}, u32[]{:S(2)}, u32[]{:S(2)}) async-start(bf16[128,16,256]{2,1,0:T(8,128)(2,1)} %bitcast.10), calls=%async_computation.1 | async-start | bytes 2097152 | tf_op jit(solution)/shard_map/all_to_all | solution.py:44
  49.8 90.6 %all-gather.2.cloned.1.call-start = ((), (), s32[]{:S(2)}) async-start(), calls=%async_computation.4 | async-start | bytes 8912896 | tf_op jit(solution)/shard_map/all_gather | solution.py:101
  53.9 25.2 %copy-start.6 = (bf16[1024,256]{1,0:T(8,128)(2,1)}, bf16[1024,256]{1,0:T(8,128)(2,1)S(1)}, u32[]{:S(2)}) copy-start(bf16[1024,256]{1,0:T(8,128)(2,1)S(1)} %gather_fusion.2) | copy-start | bytes 1572868
  53.9 22.9 %copy-start.12 = (bf16[256,256]{1,0:T(8,128)(2,1)S(1)}, bf16[256,256]{1,0:T(8,128)(2,1)}, u32[]{:S(2)}) copy-start(bf16[256,256]{1,0:T(8,128)(2,1)} %param.24) | copy-start | bytes 393220
  72.4 97.2 %copy-start.8 = (bf16[1024,256]{1,0:T(8,128)(2,1)}, bf16[1024,256]{1,0:T(8,128)(2,1)S(1)}, u32[]{:S(2)}) copy-start(bf16[1024,256]{1,0:T(8,128)(2,1)S(1)} %gather_fusion.1) | copy-start | bytes 1572868
  73.4 1290.4 %reduce-scatter.2.cloned.1.call-start = ((), (), s32[]{:S(2)}) async-start(), calls=%async_computation.5 | async-start | bytes 8912896 | tf_op jit(solution)/shard_map/reduce_scatter | solution.py:146
  74.8 4.3 collective-permute-start
  76.7 4.7 collective-permute-start.1
  79.0 90.6 %copy-start.19 = (s32[8]{0:T(128)S(1)}, s32[8]{0:T(128)}, u32[]{:S(2)}) copy-start(s32[8]{0:T(128)} %param.23) | copy-start | bytes 100
  169.7 521.2 %copy-start.16 = (bf16[1024,256]{1,0:T(8,128)(2,1)S(1)}, bf16[1024,256]{1,0:T(8,128)(2,1)}, u32[]{:S(2)}) copy-start(bf16[1024,256]{1,0:T(8,128)(2,1)} %param.27) | copy-start | bytes 1572868
  169.7 521.2 %copy-start.17 = (bf16[256,256]{1,0:T(8,128)(2,1)S(1)}, bf16[256,256]{1,0:T(8,128)(2,1)}, u32[]{:S(2)}) copy-start(bf16[256,256]{1,0:T(8,128)(2,1)} %param.25) | copy-start | bytes 393220
  169.7 521.2 %copy-start.18 = (f32[256]{0:T(256)S(1)}, f32[256]{0:T(256)}, u32[]{:S(2)}) copy-start(f32[256]{0:T(256)} %param.26) | copy-start | bytes 3076
  1280.3 83.5 %copy-start.13 = (bf16[256,256]{1,0:T(8,128)(2,1)S(1)}, bf16[256,256]{1,0:T(8,128)(2,1)}, u32[]{:S(2)}) copy-start(bf16[256,256]{1,0:T(8,128)(2,1)} %param.24) | copy-start | bytes 393220
  1280.3 84.8 %copy-start.9 = (bf16[1024,256]{1,0:T(8,128)(2,1)S(1)}, bf16[1024,256]{1,0:T(8,128)(2,1)}, u32[]{:S(2)}) copy-start(bf16[1024,256]{1,0:T(8,128)(2,1)} %copy-done.8) | copy-start | bytes 1572868
  1280.3 250.5 %all-reduce.5.cloned.1.call-start = ((), (), s32[]{:S(2)}) async-start(), calls=%async_computation.6 | async-start | bytes 3145728 | tf_op jit(solution)/shard_map/psum | solution.py:166
  1282.1 83.0 %collective-permute-start.2 = (bf16[256,256]{1,0:T(8,128)(2,1)}, bf16[256,256]{1,0:T(8,128)(2,1)S(1)}, u32[]{:S(2)}, u32[]{:S(2)}) collective-permute-start(bf16[256,256]{1,0:T(8,128)(2,1)} %get-tuple-element.131), channel_id=1, source_target_pairs={{112,0},{0,16},{16,32},{32,48},{48,64},{64,80},{80,96},{96,112},{1... | collective-permute-start | bytes 393224 | tf_op jit(solution)/shard_map/ppermute | solution.py:29
  1284.0 81.2 %collective-permute-start.3 = (bf16[256,256]{1,0:T(8,128)(2,1)}, bf16[256,256]{1,0:T(8,128)(2,1)S(1)}, u32[]{:S(2)}, u32[]{:S(2)}) collective-permute-start(bf16[256,256]{1,0:T(8,128)(2,1)} %get-tuple-element.132), channel_id=1, source_target_pairs={{16,0},{32,16},{48,32},{64,48},{80,64},{96,80},{112,96},{0,112},{1... | collective-permute-start | bytes 393224 | tf_op jit(solution)/shard_map/ppermute | solution.py:29
  1285.0 88.3 %copy-start.7 = (bf16[1024,256]{1,0:T(8,128)(2,1)S(1)}, bf16[1024,256]{1,0:T(8,128)(2,1)}, u32[]{:S(2)}) copy-start(bf16[1024,256]{1,0:T(8,128)(2,1)} %copy-done.6) | copy-start | bytes 1572868
  1373.3 18.7 %copy-start.11 = (s32[128,1,16]{2,1,0:T(1,128)S(1)}, s32[128,1,16]{2,1,0:T(1,128)}, u32[]{:S(2)}) copy-start(s32[128,1,16]{2,1,0:T(1,128)} %copy-done.10) | copy-start | bytes 24580
  1380.4 167.3 %copy-start.1 = (bf16[1024,256]{1,0:T(8,128)(2,1)S(1)}, bf16[1024,256]{1,0:T(8,128)(2,1)}, u32[]{:S(2)}) copy-start(bf16[1024,256]{1,0:T(8,128)(2,1)} %param.19) | copy-start | bytes 1572868
  1383.1 151.9 %all-to-all-start.2 = ((bf16[128,16,256]{2,1,0:T(8,128)(2,1)}), bf16[128,16,256]{2,1,0:T(8,128)(2,1)S(1)}, u32[]{:S(2)}, u32[]{:S(2)}) async-start(bf16[128,16,256]{2,1,0:T(8,128)(2,1)} %bitcast.15), calls=%async_computation.3 | async-start | bytes 2097152 | tf_op jit(solution)/shard_map/all_to_all | solution.py:48
  (12 other events, 51.3 us)
Sparse Core Ops, SparseCore 0:
  73.5 66.8 all-gather.1
  1280.4 83.2 reduce-scatter.1
  1373.4 157.3 all-reduce.4
where the time goes:
time: 1560 us; the launch traced here: 1550 us
  other arithmetic  855 us (55%)
  waiting for transfers between devices  220 us (14%)
  local copies, waits for them, and re-layouts  186 us (12%)
  matrix products  168 us (11%)
  blocking collectives  92.8 us (6%)
  starting transfers between devices  17.6 us (1%)
    scatter-add x16, other arithmetic, block_adjacency(): jnp.zeros((ROWS_BLK * width,), jnp.bfloat16).at[flat_index].add(live_slot)  729 us
    reshape x16, local copies, waits for them, and re-layouts, block_adjacency(): return adjacency.reshape(ROWS_BLK, width)  140 us
    dot_general x8, matrix products, backward_block(): lax.dot_general(adjacency, scaled_blk, contract_rows, preferred_element_t...  120 us
    reduce_scatter x1, waiting for transfers between devices, per_device(): lax.psum_scatter(source_grad[:part_nodes].astype(jnp.bfloat16), 'blk', sc...  77.7 us
    psum x1, blocking collectives, per_device(): lax.psum((local_self, local_neigh, local_bias, local_remain), ('dom', 'bl...  71.9 us
    psum x1, waiting for transfers between devices, per_device(): lax.psum((local_self, local_neigh, local_bias, local_remain), ('dom', 'bl...  66.2 us
    all_gather x1, waiting for transfers between devices, per_device(): part_gathered = lax.all_gather(features, 'blk', axis=0, tiled=True)  59 us
    dot_general x8, matrix products, forward_block(): summed = jnp.dot(adjacency, source_rows, preferred_element_type=jnp.float32)  37.9 us
  transfers between devices with their start and end apart: 9, of which 5 were waited for; matrix products, arithmetic and copies ran while one was open for 2% of the time, Pallas kernels for 0%

commit v1 on v0

v1 whole, which is shorter than its diff:
```python
import functools
import math

import jax
import jax.numpy as jnp
from jax import lax
from jax.experimental import pallas as pl
from jax.experimental.pallas import tpu as pltpu
from jax.sharding import PartitionSpec as P

ROWS_BLK = 128
HALO = 256
LANES = 128
BATCH = 16
AXES = ("dom", "blk")
ROWS = (((0,), (0,)), ((), ()))
COLS = (((1,), (1,)), ((), ()))


def prep_kernel(dump, src_ref, dst_ref, count_ref, fast_ref, slow_ref, flag_ref):
    blocks, slots = src_ref.shape
    src = src_ref[...]
    lane = lax.broadcasted_iota(jnp.int32, (blocks, slots), 1)
    cell = ((src >> 7) * ROWS_BLK + dst_ref[...]) * LANES + (src & 127)
    live = lane < count_ref[...]
    spare = dump * LANES
    cell = jnp.where(live, cell, spare)
    row = cell >> 7
    clash = jnp.zeros((blocks, slots), jnp.bool_)
    place = lane & (BATCH - 1)
    for s in range(1, BATCH):
        clash = clash | ((pltpu.roll(row, s, 1) == row) & (place >= s))
    clash = clash & live
    fast_ref[...] = jnp.where(clash, spare, cell)
    slow_ref[...] = jnp.where(clash, cell, spare)
    ones = jnp.where(clash, 1.0, 0.0)
    chunks = slots // LANES
    col = lax.broadcasted_iota(jnp.int32, (blocks, LANES), 1)
    flags = jnp.zeros((blocks, LANES), jnp.float32)
    for c in range(chunks):
        total = jnp.sum(ones[:, c * LANES : (c + 1) * LANES], axis=1, keepdims=True)
        flags = flags + jnp.where(col == c, total, 0.0)
    flag_ref[...] = flags.astype(jnp.int32)


def count_kernel(dump, count_ref, fast_ref, slow_ref, flag_ref, main_ref, halo_ref, deg_ref, cells):
    j = pl.program_id(0)
    his = dump // ROWS_BLK
    his_main = main_ref.shape[1] // LANES
    zero = jnp.zeros((ROWS_BLK, LANES), jnp.float32)

    @pl.when(j == 0)
    def _():
        def clear(i, carry):
            cells[pl.ds(pl.multiple_of(i * ROWS_BLK, ROWS_BLK), ROWS_BLK), :] = zero
            return carry

        lax.fori_loop(0, his, clear, 0)
        cells[pl.ds(dump, 8), :] = jnp.zeros((8, LANES), jnp.float32)

    count = count_ref[j]
    lanes = lax.broadcasted_iota(jnp.int32, (1, LANES), 1)

    def batch(t, carry):
        keys = [fast_ref[j, t * BATCH + i] for i in range(BATCH)]
        rows = [k >> 7 for k in keys]
        olds = [cells[pl.ds(r, 1), :] for r in rows]
        news = [old + jnp.where(lanes == (k & 127), 1.0, 0.0) for old, k in zip(olds, keys)]
        for r, new in zip(rows, news):
            cells[pl.ds(r, 1), :] = new
        return carry

    lax.fori_loop(0, (count + BATCH - 1) // BATCH, batch, 0)

    def chunk(c, carry):
        @pl.when(flag_ref[j, c] > 0)
        def _():
            def one(i, inner):
                k = slow_ref[j, c * LANES + i]

                @pl.when(k != dump * LANES)
                def _():
                    r = k >> 7
                    cells[pl.ds(r, 1), :] = cells[pl.ds(r, 1), :] + jnp.where(lanes == (k & 127), 1.0, 0.0)

                return inner

            lax.fori_loop(0, LANES, one, 0)

        return carry

    lax.fori_loop(0, (count + LANES - 1) // LANES, chunk, 0)

    def flush(ref, first):
        def step(h, total):
            at = pl.multiple_of((first + h) * ROWS_BLK, ROWS_BLK)
            value = cells[pl.ds(at, ROWS_BLK), :]
            ref[:, pl.ds(pl.multiple_of(h * LANES, LANES), LANES)] = value.astype(jnp.bfloat16)
            cells[pl.ds(at, ROWS_BLK), :] = zero
            return total + value

        return step

    total = lax.fori_loop(0, his_main, flush(main_ref, 0), zero, unroll=2)
    total = lax.fori_loop(0, his - his_main, flush(halo_ref, his_main), total, unroll=2)
    deg_ref[...] = jnp.sum(total, axis=1, keepdims=True)


def build_counts(edge_src, edge_dst, block_count, part_nodes):
    blocks, slots = edge_src.shape
    width = part_nodes + 2 * HALO
    dump = width // LANES * ROWS_BLK
    edge = jax.ShapeDtypeStruct((blocks, slots), jnp.int32)
    fast, slow, flags = pl.pallas_call(
        functools.partial(prep_kernel, dump),
        out_shape=(edge, edge, jax.ShapeDtypeStruct((blocks, LANES), jnp.int32)),
        compiler_params=pltpu.CompilerParams(vmem_limit_bytes=32 << 20),
        name="edge_prep",
    )(edge_src, edge_dst, block_count[:, None])
    smem = pl.BlockSpec(memory_space=pltpu.SMEM)
    nodes = blocks * ROWS_BLK
    return pl.pallas_call(
        functools.partial(count_kernel, dump),
        grid=(blocks,),
        out_shape=(
            jax.ShapeDtypeStruct((nodes, part_nodes), jnp.bfloat16),
            jax.ShapeDtypeStruct((nodes, 2 * HALO), jnp.bfloat16),
            jax.ShapeDtypeStruct((nodes, 1), jnp.float32),
        ),
        in_specs=[smem, smem, smem, smem],
        out_specs=(
            pl.BlockSpec((ROWS_BLK, part_nodes), lambda j: (j, 0)),
            pl.BlockSpec((ROWS_BLK, 2 * HALO), lambda j: (j, 0)),
            pl.BlockSpec((ROWS_BLK, 1), lambda j: (j, 0)),
        ),
        scratch_shapes=[pltpu.VMEM((dump + 8, LANES), jnp.float32)],
        compiler_params=pltpu.CompilerParams(vmem_limit_bytes=40 << 20),
        cost_estimate=pl.CostEstimate(flops=80_000_000_000, bytes_accessed=40_000_000, transcendentals=0),
        name="edge_counts",
    )(block_count, fast, slow, flags)


def shifted(block, axis, distance):
    devices = range(lax.axis_size(axis))
    route = [((i - distance) % len(devices), i) for i in devices]
    return lax.ppermute(block, axis, route)


def exchange(buffer):
    return lax.all_to_all(buffer, AXES, split_axis=0, concat_axis=0, tiled=True)


def hot(index, size):
    return (index[:, None] == jnp.arange(size, dtype=jnp.int32)[None, :]).astype(jnp.bfloat16)


def dot(a, b, dims=(((1,), (0,)), ((), ()))):
    return lax.dot_general(a, b, dims, preferred_element_type=jnp.float32)


def per_device(
    node_owner,
    node_qrow,
    node_rem,
    quotient,
    remainder,
    edge_src,
    edge_dst,
    block_count,
    w_self,
    w_neigh,
    bias,
    cotangent,
):
    nodes_dev = node_qrow.shape[0]
    feature_dim = quotient.shape[1]
    devices = lax.axis_size("dom") * lax.axis_size("blk")
    part_nodes = nodes_dev * lax.axis_size("blk")
    slot_cap = 2 * nodes_dev // devices
    slots = devices * slot_cap
    owner_dev = node_owner[:, 0]
    owner_hot = hot(owner_dev, devices)
    row_ids = jnp.arange(nodes_dev, dtype=jnp.int32)
    lower_mask = (row_ids[:, None] > row_ids[None, :]).astype(jnp.bfloat16)
    earlier = dot(lower_mask, owner_hot)
    slot_rank = jnp.sum(earlier * owner_hot.astype(jnp.float32), axis=1).astype(jnp.int32)
    slot_index = owner_dev * slot_cap + slot_rank
    rank_hot = hot(slot_rank, slot_cap)
    high = (node_qrow >> 5).astype(jnp.bfloat16)[:, None]
    low = (node_qrow & 31).astype(jnp.bfloat16)[:, None]
    asked = dot(owner_hot, jnp.concatenate([rank_hot * high, rank_hot * low], axis=1), ROWS)
    requests = (asked[:, :slot_cap] * 32.0 + asked[:, slot_cap:]).astype(jnp.int32)
    asked_rows = exchange(requests).reshape(slots)
    asked_hot = hot(asked_rows, quotient.shape[0])
    served = dot(asked_hot, quotient).astype(jnp.bfloat16)
    returned = exchange(served.reshape(devices, slot_cap, feature_dim)).reshape(slots, feature_dim)
    slot_hot = hot(slot_index, slots)
    quot_rows = dot(slot_hot, returned)
    rem_hot = hot(node_rem, remainder.shape[0])
    remain_rows = dot(rem_hot, remainder)
    features = (quot_rows * remain_rows).astype(jnp.bfloat16)
    part_gathered = lax.all_gather(features, "blk", axis=0, tiled=True)
    low_rows = shifted(features[nodes_dev - HALO :], "dom", 1)
    high_rows = shifted(features[:HALO], "dom", -1)
    halo_rows = jnp.concatenate([low_rows, high_rows], axis=0)

    counts, halo_counts, degree = build_counts(edge_src, edge_dst, block_count, part_nodes)
    divisor = jnp.maximum(degree, 1.0)
    agg_sum = dot(counts, part_gathered) + dot(halo_counts, halo_rows)
    neighbour = (agg_sum / divisor).astype(jnp.bfloat16)
    preact = dot(features, w_self) + dot(neighbour, w_neigh) + bias
    sigma = jax.nn.sigmoid(preact)
    out = (preact * sigma).astype(jnp.bfloat16)
    dpre = (cotangent.astype(jnp.float32) * sigma * (1.0 + preact * (1.0 - sigma))).astype(
        jnp.bfloat16
    )
    dagg_scaled = (dot(dpre, w_neigh, COLS) / divisor).astype(jnp.bfloat16)
    halo_grads = dot(halo_counts, dagg_scaled, ROWS).astype(jnp.bfloat16)
    source_grads = dot(counts, dagg_scaled, ROWS).astype(jnp.bfloat16)
    own_grads = lax.psum_scatter(source_grads, "blk", scatter_dimension=0, tiled=True)
    tail_grad = shifted(halo_grads[:HALO], "dom", -1)
    head_grad = shifted(halo_grads[HALO:], "dom", 1)
    local_self = dot(features, dpre, ROWS)
    local_neigh = dot(neighbour, dpre, ROWS)
    local_bias = jnp.sum(dpre.astype(jnp.float32), axis=0)
    dx_self = dot(dpre, w_self, COLS)
    edges = jnp.concatenate(
        [
            head_grad.astype(jnp.float32),
            jnp.zeros((nodes_dev - 2 * HALO, feature_dim), jnp.float32),
            tail_grad.astype(jnp.float32),
        ],
        axis=0,
    )
    grad_x = dx_self + own_grads.astype(jnp.float32) + edges
    outgoing = dot(slot_hot, (grad_x * remain_rows).astype(jnp.bfloat16), ROWS).astype(jnp.bfloat16)
    local_remain = dot(rem_hot, (grad_x * quot_rows).astype(jnp.bfloat16), ROWS)

    def per_owner(value):
        return value.astype(jnp.bfloat16).reshape(devices, -1, feature_dim)

    bias_high = local_bias.astype(jnp.bfloat16)
    bias_low = (local_bias - bias_high.astype(jnp.float32)).astype(jnp.bfloat16)
    bias_pair = jnp.concatenate([bias_high.reshape(devices, -1), bias_low.reshape(devices, -1)], axis=1)
    bias_each = feature_dim // devices
    bias_rows = jnp.pad(bias_pair, ((0, 0), (0, feature_dim - 2 * bias_each)))[:, None, :]
    incoming = exchange(
        jnp.concatenate(
            [
                per_owner(outgoing),
                per_owner(local_remain),
                per_owner(local_self),
                per_owner(local_neigh),
                bias_rows,
            ],
            axis=1,
        )
    )
    returned_grads = incoming[:, :slot_cap].reshape(slots, feature_dim)
    d_quotient = dot(asked_hot, returned_grads, ROWS)
    summed = jnp.sum(incoming[:, slot_cap:].astype(jnp.float32), axis=0)
    gathered = lax.all_gather(summed, AXES, axis=0, tiled=False)
    rem_each = remainder.shape[0] // devices
    w_each = feature_dim // devices
    nodes_total = nodes_dev * devices
    weight_scale = 1.0 / math.sqrt(nodes_total)
    remain_scale = math.sqrt(remainder.shape[0] / nodes_total)
    d_remainder = gathered[:, :rem_each].reshape(-1, feature_dim) * remain_scale
    d_self = gathered[:, rem_each : rem_each + w_each].reshape(-1, feature_dim) * weight_scale
    d_neigh = gathered[:, rem_each + w_each : rem_each + 2 * w_each].reshape(-1, feature_dim) * weight_scale
    last = gathered[:, rem_each + 2 * w_each]
    d_bias = (last[:, :bias_each] + last[:, bias_each : 2 * bias_each]).reshape(-1) * weight_scale
    return (out, d_quotient, d_remainder, d_self, d_neigh, d_bias)


def solution(mesh):
    both = P(AXES)
    rows = P(AXES, None)
    return jax.shard_map(
        per_device,
        mesh=mesh,
        in_specs=(rows, both, both, rows, P(), rows, rows, both, P(), P(), P(), rows),
        out_specs=(rows, rows, P(), P(), P(), P()),
        check_vma=False,
    )
```

time: 1560 us -> 517 us (0.33)
  other arithmetic: 855 us -> 6.88 us
  local copies, waits for them, and re-layouts: 186 us -> 12.3 us
  Pallas kernels: 0 us -> 173 us
  matrix products: 168 us -> 58.4 us
  waiting for transfers between devices: 220 us -> 168 us
  blocking collectives: 92.8 us -> 59.7 us
    scatter-add x18 -> x0, other arithmetic: 750 us -> none  [the longest x16 729 us: block_adjacency(): jnp.zeros((ROWS_BLK * width,), jnp.bfloat16).at[flat_index].add(live_slot)]
    pallas_call x0 -> x2, Pallas kernels: none -> 173 us  [the longest x1 171 us: build_counts(): pl.pallas_call(functools.partial(count_kernel, dump), grid=(blocks,), out...]
    reshape x18 -> x2, local copies, waits for them, and re-layouts: 140 us -> 0.11 us  [per_owner(): return value.astype(jnp.bfloat16).reshape(devices, -1, feature_dim)]
    dot_general x23 -> x18, matrix products: 168 us -> 58.4 us  [dot(): return lax.dot_general(a, b, dims, preferred_element_type=jnp.float32)]
    psum x1 -> x0, blocking collectives: 71.9 us -> none  [per_device(): lax.psum((local_self, local_neigh, local_bias, local_remain), ('dom', 'bl...]
    psum x1 -> x0, waiting for transfers between devices: 66.2 us -> none  [per_device(): lax.psum((local_self, local_neigh, local_bias, local_remain), ('dom', 'bl...]
    all_gather x1, waiting for transfers between devices: 59 us -> 0.02 us  [per_device(): part_gathered = lax.all_gather(features, 'blk', axis=0, tiled=True)]
    all_gather x0 -> x1, waiting for transfers between devices: none -> 58.2 us  [per_device(): gathered = lax.all_gather(summed, AXES, axis=0, tiled=False)]
  transfers between devices with their start and end apart: 9 -> 8, of which waited for: 5 -> 5; matrix products, arithmetic and copies ran while one was open for 2% -> 5% of each run, Pallas kernels for 0% -> 33%
where the time goes in v1:
time: 517 us; the launch traced here: 516 us
  Pallas kernels  173 us (33%)
  waiting for transfers between devices  168 us (32%)
  blocking collectives  59.7 us (12%)
  matrix products  58.4 us (11%)
  starting transfers between devices  23.9 us (5%)
  between operations  14.2 us (3%)
  local copies, waits for them, and re-layouts  12.3 us (2%)
  other arithmetic  6.88 us (1%)
    pallas_call x1, Pallas kernels, build_counts(): pl.pallas_call(functools.partial(count_kernel, dump), grid=(blocks,), out...  171 us
    reduce_scatter x1, waiting for transfers between devices, per_device(): lax.psum_scatter(source_grads, 'blk', scatter_dimension=0, tiled=True)  72.6 us
    all_to_all x2, blocking collectives, exchange(): return lax.all_to_all(buffer, AXES, split_axis=0, concat_axis=0, tiled=True)  59.7 us
    dot_general x18, matrix products, dot(): return lax.dot_general(a, b, dims, preferred_element_type=jnp.float32)  58.4 us
    all_gather x1, waiting for transfers between devices, per_device(): gathered = lax.all_gather(summed, AXES, axis=0, tiled=False)  58.2 us
    ppermute x4, waiting for transfers between devices, shifted(): return lax.ppermute(block, axis, route)  19.7 us
    ppermute x4, starting transfers between devices, shifted(): return lax.ppermute(block, axis, route)  18.9 us
    all_to_all x1, waiting for transfers between devices, exchange(): return lax.all_to_all(buffer, AXES, split_axis=0, concat_axis=0, tiled=True)  17.7 us
  transfers between devices with their start and end apart: 8, of which 5 were waited for; matrix products, arithmetic and copies ran while one was open for 5% of the time, Pallas kernels for 33%

profile of v1, /device:TPU:1, one launch (start us, length us, event | category | flops | bytes accessed | tf_op | source)
XLA Modules:
  0.0 516.3 jit_solution(16208752763880120652)
XLA Ops:
  7.2 1.4 fusion.22
  10.3 20.9 %all_to_all.19 = s32[128,1,16]{2,1,0:T(1,128)S(1)} all-to-all(s32[128,1,16]{2,1,0:T(1,128)S(1)} %copy.34), channel_id=1, replica_groups=mesh['dom'=8,'blk'=16] {'dom','blk'}, dimensions={0} | all-to-all | bytes 16384 | tf_op jit(solution)/shard_map/all_to_all | solution.py:150
  32.6 2.5 fusion.12
  35.1 4.5 all-to-all-start.1
  40.6 17.7 %all-to-all-done.1 = bf16[128,16,256]{2,1,0:T(8,128)(2,1)S(1)} async-done(((bf16[128,16,256]{2,1,0:T(8,128)(2,1)}), bf16[128,16,256]{2,1,0:T(8,128)(2,1)S(1)}, u32[]{:S(2)}, u32[]{:S(2)}) %all-to-all-start.1) | async-done | bytes 1048608 | tf_op jit(solution)/shard_map/all_to_all | solution.py:150
  58.3 2.7 multiply_convert_fusion.4
  61.3 1.9 edge_prep.1
  63.2 170.7 %edge_counts.1 = (bf16[1024,16384]{1,0:T(8,128)(2,1)}, bf16[1024,512]{1,0:T(8,128)(2,1)S(1)}, f32[1024,1]{1,0:T(8,128)S(1)}) custom-call(s32[8]{0:T(128)S(1)} %copy-done.4, s32[8,6144]{1,0:T(8,128)S(1)} %get-tuple-element.12.fast_ref, s32[8,6144]{1,0:T(8,128)S(1)} %get-tuple-element.13.slow_ref, s32[8,128]{1,0:T(8,128)S(1)} %get-tuple-element.14.flag_ref), custom_call_target="tpu_custom_call" | custom-call | flops 80000000000 | bytes 40000000 | tf_op jit(solution)/shard_map/edge_counts/pallas_call | solution.py:122
  235.0 17.4 %fusion.48 = f32[1024,256]{1,0:T(8,128)S(1)} fusion(bf16[1024,16384]{1,0:T(8,128)(2,1)} %get-tuple-element.15, bf16[16384,256]{1,0:T(8,128)(2,1)} %all-gather.5.cloned.1.call-done), kind=kOutput, calls=%fused_computation.84 | convolution fusion | flops 8589934592 | bytes 42991616 | tf_op jit(solution)/shard_map/dot_general | solution.py:158
  253.5 1.5 convert_reduce_fusion.1
  255.3 17.6 %convolution_convert_fusion = bf16[16384,256]{1,0:T(8,128)(2,1)} fusion(bf16[1024,16384]{1,0:T(8,128)(2,1)} %get-tuple-element.15, bf16[1024,256]{1,0:T(8,128)(2,1)S(1)} %fusion.19), kind=kOutput, calls=%fused_computation | convolution fusion | flops 8594128896 | bytes 42467328 | tf_op jit(solution)/shard_map/dot_general | solution.py:158
  274.4 1.5 convolution_convert_fusion.1
  275.9 18.4 %collective-permute-start.2 = (bf16[256,256]{1,0:T(8,128)(2,1)S(1)}, bf16[256,256]{1,0:T(8,128)(2,1)S(1)}, u32[]{:S(2)}, u32[]{:S(2)}) collective-permute-start(bf16[256,256]{1,0:T(8,128)(2,1)S(1)} %get-tuple-element.27), channel_id=1, source_target_pairs={{112,0},{0,16},{16,32},{32,48},{48,64},{64,80},{80,96},{96,112},{1... | collective-permute-start | bytes 393224 | tf_op jit(solution)/shard_map/ppermute | solution.py:146
  294.7 1.5 collective-permute-done.2
  296.3 18.1 %collective-permute-done.3 = bf16[256,256]{1,0:T(8,128)(2,1)S(1)} collective-permute-done((bf16[256,256]{1,0:T(8,128)(2,1)S(1)}, bf16[256,256]{1,0:T(8,128)(2,1)S(1)}, u32[]{:S(2)}, u32[]{:S(2)}) %collective-permute-start.3) | collective-permute-done | bytes 131104 | tf_op jit(solution)/shard_map/ppermute | solution.py:146
  314.5 72.6 %reduce-scatter.2.cloned.1.call-done = bf16[1024,256]{1,0:T(8,128)(2,1)} async-done(((bf16[16384,256]{1,0:T(8,128)(2,1)}), bf16[1024,256]{1,0:T(8,128)(2,1)}) %reduce-scatter.2.cloned.1.call-update) | async-done | bytes 524304 | tf_op jit(solution)/shard_map/reduce_scatter | solution.py:220
  388.5 3.9 fusion.11
  392.4 1.4 fusion.20
  393.8 6.1 %concatenate.19 = bf16[128,29,256]{2,1,0:T(8,128)(2,1)} concatenate(bf16[128,16,256]{2,1,0:T(8,128)(2,1)S(1)} %bitcast.46, bf16[128,8,256]{2,1,0:T(8,128)(2,1)S(1)} %fusion.20, bf16[128,2,256]{2,1,0:T(2,128)(2,1)S(1)} %reshape.70, bf16[128,2,256]{2,1,0:T(2,128)(2,1)S(1)} %reshape.71, bf16[128,1,256]{2,1,0:T(2,128)(2,1)S(1)} %copy.39), dimensions={1} | concatenate | bytes 3801088 | tf_op jit(solution)/shard_map/concatenate | solution.py:248
  399.9 38.9 %all_to_all.20 = bf16[128,29,256]{2,1,0:T(8,128)(2,1)S(1)} all-to-all(bf16[128,29,256]{2,1,0:T(8,128)(2,1)} %concatenate.19), channel_id=1, replica_groups=mesh['dom'=8,'blk'=16] {'dom','blk'}, dimensions={0} | all-to-all | bytes 3801088 | tf_op jit(solution)/shard_map/all_to_all | solution.py:150
  439.8 3.7 fusion
  443.5 58.2 %all-gather.7.cloned.1.call-done = f32[128,13,256]{2,1,0:T(8,128)} async-done(((f32[1,13,256]{2,1,0:T(8,128)}), f32[128,13,256]{2,1,0:T(8,128)}) %all-gather.7.cloned.1.call-update) | async-done | bytes 1703952 | tf_op jit(solution)/shard_map/all_gather | solution.py:262
  501.7 1.9 slice_multiply_fusion.1
  507.5 2.3 fusion.23
  (88 shorter events, 14.9 us)
Async XLA Ops:
  7.2 25.4 %copy-start = (bf16[1024,256]{1,0:T(8,128)(2,1)S(1)}, bf16[1024,256]{1,0:T(8,128)(2,1)}, u32[]{:S(2)}) copy-start(bf16[1024,256]{1,0:T(8,128)(2,1)} %param.15) | copy-start | bytes 1572868
  32.6 7.1 %copy-start.7 = (s32[1024,1]{0,1:T(1,128)S(1)}, s32[1024,1]{0,1:T(1,128)}, u32[]{:S(2)}) copy-start(s32[1024,1]{0,1:T(1,128)} %param.12) | copy-start | bytes 12292
  32.6 7.1 %copy-start.8 = (bf16[1024,256]{1,0:T(8,128)(2,1)S(1)}, bf16[1024,256]{1,0:T(8,128)(2,1)}, u32[]{:S(2)}) copy-start(bf16[1024,256]{1,0:T(8,128)(2,1)} %param.16) | copy-start | bytes 1572868
  32.6 7.1 %copy-start.11 = (s32[1024]{0:T(1024)S(1)}, s32[1024]{0:T(1024)}, u32[]{:S(2)}) copy-start(s32[1024]{0:T(1024)} %param.14) | copy-start | bytes 12292
  35.1 23.2 %all-to-all-start.1 = ((bf16[128,16,256]{2,1,0:T(8,128)(2,1)}), bf16[128,16,256]{2,1,0:T(8,128)(2,1)S(1)}, u32[]{:S(2)}, u32[]{:S(2)}) async-start(bf16[128,16,256]{2,1,0:T(8,128)(2,1)} %bitcast.4), calls=%async_computation.1 | async-start | bytes 2097152 | tf_op jit(solution)/shard_map/all_to_all | solution.py:150
  39.6 195.4 %all-gather.5.cloned.1.call-start = ((), (), s32[]{:S(2)}) async-start(), calls=%async_computation.4 | async-start | bytes 8912896 | tf_op jit(solution)/shard_map/all_gather | solution.py:202
  40.5 20.4 %copy-start.17 = (f32[1024,256]{1,0:T(8,128)}, f32[1024,256]{1,0:T(8,128)S(1)}, u32[]{:S(2)}) copy-start(f32[1024,256]{1,0:T(8,128)S(1)} %fusion.5) | copy-start | bytes 3145732
  58.3 2.9 copy-start.4
  58.3 3.0 copy-start.2
  58.3 3.0 copy-start.3
  61.0 326.1 %reduce-scatter.2.cloned.1.call-start = ((), (), s32[]{:S(2)}) async-start(), calls=%async_computation.5 | async-start | bytes 8912896 | tf_op jit(solution)/shard_map/reduce_scatter | solution.py:220
  63.2 170.9 %copy-start.5 = (bf16[1024,256]{1,0:T(8,128)(2,1)S(1)}, bf16[1024,256]{1,0:T(8,128)(2,1)}, u32[]{:S(2)}) copy-start(bf16[1024,256]{1,0:T(8,128)(2,1)} %get-tuple-element.33) | copy-start | bytes 1572868
  63.2 171.4 %copy-start.6 = (bf16[256,256]{1,0:T(8,128)(2,1)S(1)}, bf16[256,256]{1,0:T(8,128)(2,1)}, u32[]{:S(2)}) copy-start(bf16[256,256]{1,0:T(8,128)(2,1)} %param.20) | copy-start | bytes 393220
  234.1 18.3 %collective-permute-start = (bf16[256,256]{1,0:T(8,128)(2,1)S(1)}, bf16[256,256]{1,0:T(8,128)(2,1)S(1)}, u32[]{:S(2)}, u32[]{:S(2)}) collective-permute-start(bf16[256,256]{1,0:T(8,128)(2,1)S(1)} %get-tuple-element.25), channel_id=1, source_target_pairs={{112,0},{0,16},{16,32},{32,48},{48,64},{64,80},{80,96},{96,112},{1... | collective-permute-start | bytes 393224 | tf_op jit(solution)/shard_map/ppermute | solution.py:146
  234.2 18.3 %collective-permute-start.1 = (bf16[256,256]{1,0:T(8,128)(2,1)S(1)}, bf16[256,256]{1,0:T(8,128)(2,1)S(1)}, u32[]{:S(2)}, u32[]{:S(2)}) collective-permute-start(bf16[256,256]{1,0:T(8,128)(2,1)S(1)} %get-tuple-element.26), channel_id=1, source_target_pairs={{16,0},{32,16},{48,32},{64,48},{80,64},{96,80},{112,96},{0,112},{1... | collective-permute-start | bytes 393224 | tf_op jit(solution)/shard_map/ppermute | solution.py:146
  252.4 1.0 copy-start.9
  252.4 1.1 copy-start.10
  253.5 1.5 copy-start.13
  255.3 17.6 %copy-start.15 = (bf16[1024,256]{1,0:T(8,128)(2,1)}, bf16[1024,256]{1,0:T(8,128)(2,1)S(1)}, u32[]{:S(2)}) copy-start(bf16[1024,256]{1,0:T(8,128)(2,1)S(1)} %fusion.19) | copy-start | bytes 1572868
  272.9 228.7 %all-gather.7.cloned.1.call-start = ((), (), s32[]{:S(2)}) async-start(), calls=%async_computation.6 | async-start | bytes 2113536 | tf_op jit(solution)/shard_map/all_gather | solution.py:262
  275.9 20.3 %collective-permute-start.2 = (bf16[256,256]{1,0:T(8,128)(2,1)S(1)}, bf16[256,256]{1,0:T(8,128)(2,1)S(1)}, u32[]{:S(2)}, u32[]{:S(2)}) collective-permute-start(bf16[256,256]{1,0:T(8,128)(2,1)S(1)} %get-tuple-element.27), channel_id=1, source_target_pairs={{112,0},{0,16},{16,32},{32,48},{48,64},{64,80},{80,96},{96,112},{1... | collective-permute-start | bytes 393224 | tf_op jit(solution)/shard_map/ppermute | solution.py:146
  294.3 20.1 %collective-permute-start.3 = (bf16[256,256]{1,0:T(8,128)(2,1)S(1)}, bf16[256,256]{1,0:T(8,128)(2,1)S(1)}, u32[]{:S(2)}, u32[]{:S(2)}) collective-permute-start(bf16[256,256]{1,0:T(8,128)(2,1)S(1)} %get-tuple-element.28), channel_id=1, source_target_pairs={{16,0},{32,16},{48,32},{64,48},{80,64},{96,80},{112,96},{0,112},{1... | collective-permute-start | bytes 393224 | tf_op jit(solution)/shard_map/ppermute | solution.py:146
  388.5 3.9 copy-start.16
  439.8 70.0 %copy-start.1 = (bf16[1024,256]{1,0:T(8,128)(2,1)S(1)}, bf16[1024,256]{1,0:T(8,128)(2,1)}, u32[]{:S(2)}) copy-start(bf16[1024,256]{1,0:T(8,128)(2,1)} %param.15) | copy-start | bytes 1572868
  (2 other events, 2.1 us)
Sparse Core Ops, SparseCore 0:
  61.1 66.8 all-gather.4
  273.1 113.9 reduce-scatter.1
  439.8 61.8 all-gather.6

commit v2 on v1

--- a/solution.py
+++ b/solution.py
@@ -13,6 +13,7 @@
 LANES = 128
 BATCH = 16
 AXES = ("dom", "blk")
+MESH = pl.DeviceIdType.MESH
 ROWS = (((0,), (0,)), ((), ()))
 COLS = (((1,), (1,)), ((), ()))
 
@@ -33,14 +34,21 @@
     clash = clash & live
     fast_ref[...] = jnp.where(clash, spare, cell)
     slow_ref[...] = jnp.where(clash, cell, spare)
-    ones = jnp.where(clash, 1.0, 0.0)
+    ones = jnp.where(clash, 1.0, 0.0).astype(jnp.bfloat16)
     chunks = slots // LANES
     col = lax.broadcasted_iota(jnp.int32, (blocks, LANES), 1)
-    flags = jnp.zeros((blocks, LANES), jnp.float32)
+    into = lax.broadcasted_iota(jnp.int32, (LANES, LANES), 0) // BATCH
+    group = (into == lax.broadcasted_iota(jnp.int32, (LANES, LANES), 1)).astype(jnp.bfloat16)
+    found = jnp.zeros((blocks, LANES), jnp.int32)
+    number = jnp.zeros((blocks, 1), jnp.int32)
     for c in range(chunks):
-        total = jnp.sum(ones[:, c * LANES : (c + 1) * LANES], axis=1, keepdims=True)
-        flags = flags + jnp.where(col == c, total, 0.0)
-    flag_ref[...] = flags.astype(jnp.int32)
+        hits = jnp.dot(ones[:, c * LANES : (c + 1) * LANES], group, preferred_element_type=jnp.float32)
+        bits = jnp.sum(jnp.where(hits > 0.5, (1 << (col & 7)).astype(jnp.float32), 0.0), axis=1, keepdims=True)
+        bits = bits.astype(jnp.int32)
+        some = bits > 0
+        found = found + jnp.where((col == number) & some, c * 256 + bits, 0)
+        number = number + some.astype(jnp.int32)
+    flag_ref[...] = jnp.where(col == LANES - 1, number, found)
 
 
 def count_kernel(dump, count_ref, fast_ref, slow_ref, flag_ref, main_ref, halo_ref, deg_ref, cells):
@@ -62,7 +70,7 @@
     lanes = lax.broadcasted_iota(jnp.int32, (1, LANES), 1)
 
     def batch(t, carry):
-        keys = [fast_ref[j, t * BATCH + i] for i in range(BATCH)]
+        keys = [fast_ref[0, 0, t * BATCH + i] for i in range(BATCH)]
         rows = [k >> 7 for k in keys]
         olds = [cells[pl.ds(r, 1), :] for r in rows]
         news = [old + jnp.where(lanes == (k & 127), 1.0, 0.0) for old, k in zip(olds, keys)]
@@ -73,23 +81,23 @@
     lax.fori_loop(0, (count + BATCH - 1) // BATCH, batch, 0)
 
     def chunk(c, carry):
-        @pl.when(flag_ref[j, c] > 0)
-        def _():
-            def one(i, inner):
-                k = slow_ref[j, c * LANES + i]
-
-                @pl.when(k != dump * LANES)
-                def _():
+        entry = flag_ref[0, 0, c]
+        first = (entry >> 8) * LANES
+
+        def some(g, inner):
+            @pl.when(((entry >> g) & 1) != 0)
+            def _():
+                for i in range(BATCH):
+                    k = slow_ref[0, 0, first + g * BATCH + i]
                     r = k >> 7
                     cells[pl.ds(r, 1), :] = cells[pl.ds(r, 1), :] + jnp.where(lanes == (k & 127), 1.0, 0.0)
 
-                return inner
-
-            lax.fori_loop(0, LANES, one, 0)
-
-        return carry
-
-    lax.fori_loop(0, (count + LANES - 1) // LANES, chunk, 0)
+            return inner
+
+        lax.fori_loop(0, LANES // BATCH, some, 0)
+        return carry
+
+    lax.fori_loop(0, flag_ref[0, 0, LANES - 1], chunk, 0)
 
     def flush(ref, first):
         def step(h, total):
@@ -117,7 +125,6 @@
         compiler_params=pltpu.CompilerParams(vmem_limit_bytes=32 << 20),
         name="edge_prep",
     )(edge_src, edge_dst, block_count[:, None])
-    smem = pl.BlockSpec(memory_space=pltpu.SMEM)
     nodes = blocks * ROWS_BLK
     return pl.pallas_call(
         functools.partial(count_kernel, dump),
@@ -127,7 +134,12 @@
             jax.ShapeDtypeStruct((nodes, 2 * HALO), jnp.bfloat16),
             jax.ShapeDtypeStruct((nodes, 1), jnp.float32),
         ),
-        in_specs=[smem, smem, smem, smem],
+        in_specs=[
+            pl.BlockSpec(memory_space=pltpu.SMEM),
+            pl.BlockSpec((1, 1, slots), lambda j: (j, 0, 0), memory_space=pltpu.SMEM),
+            pl.BlockSpec((1, 1, slots), lambda j: (j, 0, 0), memory_space=pltpu.SMEM),
+            pl.BlockSpec((1, 1, LANES), lambda j: (j, 0, 0), memory_space=pltpu.SMEM),
+        ],
         out_specs=(
             pl.BlockSpec((ROWS_BLK, part_nodes), lambda j: (j, 0)),
             pl.BlockSpec((ROWS_BLK, 2 * HALO), lambda j: (j, 0)),
@@ -137,17 +149,234 @@
         compiler_params=pltpu.CompilerParams(vmem_limit_bytes=40 << 20),
         cost_estimate=pl.CostEstimate(flops=80_000_000_000, bytes_accessed=40_000_000, transcendentals=0),
         name="edge_counts",
-    )(block_count, fast, slow, flags)
+    )(block_count, fast[:, None], slow[:, None], flags[:, None])
+
+
+def ring_place():
+    blk = lax.axis_size("blk")
+    return lax.axis_index("dom") * blk + lax.axis_index("blk")
+
+
+def meet_all(devices):
+    barrier = pltpu.get_barrier_semaphore()
+    me = ring_place()
+
+    def greet(k, carry):
+        other = lax.rem(me + k, devices)
+        pl.semaphore_signal(barrier, inc=1, device_id=coords(other), device_id_type=MESH)
+        return carry
+
+    lax.fori_loop(1, devices, greet, 0)
+    pl.semaphore_wait(barrier, devices - 1)
+
+
+def coords(device):
+    blk = lax.axis_size("blk")
+    return (device // blk, lax.rem(device, blk))
+
+
+def send(src, dst, device, send_sem, recv_sem):
+    pltpu.make_async_remote_copy(
+        src_ref=src,
+        dst_ref=dst,
+        send_sem=send_sem,
+        recv_sem=recv_sem,
+        device_id=coords(device),
+        device_id_type=MESH,
+    ).start()
+
+
+def drain(ref, sem):
+    pltpu.make_async_copy(ref, ref, sem).wait()
+
+
+def fetch_kernel(devices, ids_ref, table_ref, rows_ref, asked_ref, ids_in, served, rows_in, sems):
+    slot_cap = served.shape[0] // devices
+    slots = served.shape[0]
+    me = ring_place()
+    meet_all(devices)
+
+    def ask(k, carry):
+        other = lax.rem(me + k, devices)
+        send(ids_ref.at[other], ids_in.at[me], other, sems.at[0], sems.at[1])
+        return carry
+
+    lax.fori_loop(1, devices, ask, 0)
+    own = pltpu.make_async_copy(ids_ref.at[me], ids_in.at[me], sems.at[2])
+    own.start()
+    own.wait()
+    drain(ids_in.at[pl.ds(0, devices - 1)], sems.at[1])
+    ids = ids_in[:, 0, :].astype(jnp.bfloat16)
+    step = 16
+    part = step * slot_cap
+    lanes = ids.shape[1]
+    lane = lax.broadcasted_iota(jnp.int32, (part, lanes), 1)
+    slot = lax.broadcasted_iota(jnp.int32, (part, lanes), 0)
+    rank = lax.rem(slot, slot_cap)
+    weight = jnp.where(lane == rank, 32.0, 0.0) + jnp.where(lane == rank + slot_cap, 1.0, 0.0)
+    column = lax.broadcasted_iota(jnp.int32, (part, table_ref.shape[0]), 1)
+
+    def serve(c, carry):
+        turn = lax.rem(c + me // step, devices // step)
+        pick = (lane - turn * step == slot // slot_cap).astype(jnp.bfloat16)
+        spread = jnp.dot(pick, ids, preferred_element_type=jnp.float32)
+        asked = jnp.sum(spread * weight, axis=1, keepdims=True).astype(jnp.int32)
+        at = pl.multiple_of(turn * part, part)
+        asked_ref[pl.ds(at, part), :] = asked
+        pick_row = (column == asked).astype(jnp.bfloat16)
+        served[pl.ds(at, part), :] = jnp.dot(
+            pick_row, table_ref[...], preferred_element_type=jnp.float32
+        ).astype(jnp.bfloat16)
+
+        def back(i, inner):
+            other = turn * step + lax.rem(me + i, step)
+
+            @pl.when(other != me)
+            def _():
+                send(
+                    served.at[pl.ds(pl.multiple_of(other * slot_cap, slot_cap), slot_cap)],
+                    rows_in.at[pl.ds(pl.multiple_of(me * slot_cap, slot_cap), slot_cap)],
+                    other,
+                    sems.at[3],
+                    sems.at[4],
+                )
+
+            return inner
+
+        lax.fori_loop(0, step, back, 0)
+        return carry
+
+    lax.fori_loop(0, devices // step, serve, 0)
+    mine = pl.ds(pl.multiple_of(me * slot_cap, slot_cap), slot_cap)
+    own_rows = pltpu.make_async_copy(served.at[mine], rows_in.at[mine], sems.at[2])
+    own_rows.start()
+    own_rows.wait()
+    drain(rows_in.at[pl.ds(0, slots - slot_cap)], sems.at[4])
+    rows_ref[...] = rows_in[...]
+    drain(ids_in.at[pl.ds(0, devices - 1)], sems.at[0])
+    drain(rows_in.at[pl.ds(0, slots - slot_cap)], sems.at[3])
+
+
+def fetch_rows(ids, quotient, slot_cap):
+    devices, _, lanes = ids.shape
+    slots = devices * slot_cap
+    width = quotient.shape[1]
+    vmem = pl.BlockSpec(memory_space=pltpu.VMEM)
+    return pl.pallas_call(
+        functools.partial(fetch_kernel, devices),
+        out_shape=(
+            jax.ShapeDtypeStruct((slots, width), jnp.bfloat16),
+            jax.ShapeDtypeStruct((slots, 1), jnp.int32),
+        ),
+        in_specs=[vmem, vmem],
+        out_specs=(vmem, vmem),
+        scratch_shapes=[
+            pltpu.VMEM((devices, 1, lanes), jnp.float32),
+            pltpu.VMEM((slots, width), jnp.bfloat16),
+            pltpu.VMEM((slots, width), jnp.bfloat16),
+            pltpu.SemaphoreType.DMA((5,)),
+        ],
+        compiler_params=pltpu.CompilerParams(
+            collective_id=1, has_side_effects=True, vmem_limit_bytes=32 << 20
+        ),
+        name="fetch_rows",
+    )(ids, quotient)
+
+
+def spread_kernel(devices, scale, grads_ref, rem_ref, back_ref, total_ref, grads_in, rem_in, piece, whole, sems):
+    slot_cap = grads_ref.shape[0] // devices
+    slots = grads_ref.shape[0]
+    tall = piece.shape[0]
+    wide = piece.shape[1]
+    across = rem_ref.shape[1] // wide
+    me = ring_place()
+    meet_all(devices)
+
+    def tile(device):
+        top = pl.multiple_of(device // across * tall, tall)
+        return (pl.ds(top, tall), pl.ds(pl.multiple_of(lax.rem(device, across) * wide, wide), wide))
+
+    def slot(device):
+        return pl.ds(pl.multiple_of(device * slot_cap, slot_cap), slot_cap)
+
+    def send_rem(k, carry):
+        other = lax.rem(me + k, devices)
+        send(rem_ref.at[tile(other)], rem_in.at[me], other, sems.at[0], sems.at[1])
+        return carry
+
+    def send_grads(k, carry):
+        other = lax.rem(me + k, devices)
+        send(grads_ref.at[slot(other)], grads_in.at[slot(me)], other, sems.at[2], sems.at[3])
+        return carry
+
+    def send_total(k, carry):
+        other = lax.rem(me + k, devices)
+        send(piece, whole.at[me], other, sems.at[4], sems.at[5])
+        return carry
+
+    lax.fori_loop(1, devices, send_rem, 0)
+    lax.fori_loop(1, devices, send_grads, 0)
+    own_rem = pltpu.make_async_copy(rem_ref.at[tile(me)], rem_in.at[me], sems.at[6])
+    own_rem.start()
+    own_rem.wait()
+    own_grads = pltpu.make_async_copy(grads_ref.at[slot(me)], grads_in.at[slot(me)], sems.at[6])
+    own_grads.start()
+    own_grads.wait()
+    drain(rem_in.at[pl.ds(0, devices - 1)], sems.at[1])
+    piece[...] = jnp.sum(rem_in[...].astype(jnp.float32), axis=0) * scale
+    lax.fori_loop(1, devices, send_total, 0)
+    own_total = pltpu.make_async_copy(piece, whole.at[me], sems.at[6])
+    own_total.start()
+    own_total.wait()
+    drain(grads_in.at[pl.ds(0, slots - slot_cap)], sems.at[3])
+    back_ref[...] = grads_in[...]
+
+    drain(whole.at[pl.ds(0, devices - 1)], sems.at[5])
+
+    def lay(k, carry):
+        for part in range(across):
+            total_ref[pl.ds(pl.multiple_of(k * tall, tall), tall), part * wide : (part + 1) * wide] = whole[
+                k * across + part
+            ]
+        return carry
+
+    lax.fori_loop(0, devices // across, lay, 0)
+    drain(rem_in.at[pl.ds(0, devices - 1)], sems.at[0])
+    drain(grads_in.at[pl.ds(0, slots - slot_cap)], sems.at[2])
+    drain(whole.at[pl.ds(0, devices - 1)], sems.at[4])
+
+
+def spread_grads(outgoing, local_remain, devices, scale):
+    rows, width = local_remain.shape
+    wide = LANES
+    tall = rows * width // devices // wide
+    vmem = pl.BlockSpec(memory_space=pltpu.VMEM)
+    return pl.pallas_call(
+        functools.partial(spread_kernel, devices, scale),
+        out_shape=(
+            jax.ShapeDtypeStruct(outgoing.shape, jnp.bfloat16),
+            jax.ShapeDtypeStruct((rows, width), jnp.float32),
+        ),
+        in_specs=[vmem, vmem],
+        out_specs=(vmem, vmem),
+        scratch_shapes=[
+            pltpu.VMEM(outgoing.shape, jnp.bfloat16),
+            pltpu.VMEM((devices, tall, wide), jnp.bfloat16),
+            pltpu.VMEM((tall, wide), jnp.float32),
+            pltpu.VMEM((devices, tall, wide), jnp.float32),
+            pltpu.SemaphoreType.DMA((7,)),
+        ],
+        compiler_params=pltpu.CompilerParams(
+            collective_id=2, has_side_effects=True, vmem_limit_bytes=32 << 20
+        ),
+        name="spread_grads",
+    )(outgoing, local_remain)
 
 
 def shifted(block, axis, distance):
     devices = range(lax.axis_size(axis))
     route = [((i - distance) % len(devices), i) for i in devices]
     return lax.ppermute(block, axis, route)
-
-
-def exchange(buffer):
-    return lax.all_to_all(buffer, AXES, split_axis=0, concat_axis=0, tiled=True)
 
 
 def hot(index, size):
@@ -189,11 +418,9 @@
     high = (node_qrow >> 5).astype(jnp.bfloat16)[:, None]
     low = (node_qrow & 31).astype(jnp.bfloat16)[:, None]
     asked = dot(owner_hot, jnp.concatenate([rank_hot * high, rank_hot * low], axis=1), ROWS)
-    requests = (asked[:, :slot_cap] * 32.0 + asked[:, slot_cap:]).astype(jnp.int32)
-    asked_rows = exchange(requests).reshape(slots)
-    asked_hot = hot(asked_rows, quotient.shape[0])
-    served = dot(asked_hot, quotient).astype(jnp.bfloat16)
-    returned = exchange(served.reshape(devices, slot_cap, feature_dim)).reshape(slots, feature_dim)
+    ids = jnp.pad(asked, ((0, 0), (0, LANES - 2 * slot_cap)))[:, None, :]
+    returned, asked_rows = fetch_rows(ids, quotient, slot_cap)
+    asked_hot = hot(asked_rows[:, 0], quotient.shape[0])
     slot_hot = hot(slot_index, slots)
     quot_rows = dot(slot_hot, returned)
     rem_hot = hot(node_rem, remainder.shape[0])
@@ -223,6 +450,8 @@
     local_self = dot(features, dpre, ROWS)
     local_neigh = dot(neighbour, dpre, ROWS)
     local_bias = jnp.sum(dpre.astype(jnp.float32), axis=0)
+    bias_rows = jnp.pad(local_bias[None, :], ((0, 7), (0, 0)))
+    summed = lax.psum(jnp.concatenate([local_self, local_neigh, bias_rows], axis=0), AXES)
     dx_self = dot(dpre, w_self, COLS)
     edges = jnp.concatenate(
         [
@@ -236,40 +465,16 @@
     outgoing = dot(slot_hot, (grad_x * remain_rows).astype(jnp.bfloat16), ROWS).astype(jnp.bfloat16)
     local_remain = dot(rem_hot, (grad_x * quot_rows).astype(jnp.bfloat16), ROWS)
 
-    def per_owner(value):
-        return value.astype(jnp.bfloat16).reshape(devices, -1, feature_dim)
-
-    bias_high = local_bias.astype(jnp.bfloat16)
-    bias_low = (local_bias - bias_high.astype(jnp.float32)).astype(jnp.bfloat16)
-    bias_pair = jnp.concatenate([bias_high.reshape(devices, -1), bias_low.reshape(devices, -1)], axis=1)
-    bias_each = feature_dim // devices
-    bias_rows = jnp.pad(bias_pair, ((0, 0), (0, feature_dim - 2 * bias_each)))[:, None, :]
-    incoming = exchange(
-        jnp.concatenate(
-            [
-                per_owner(outgoing),
-                per_owner(local_remain),
-                per_owner(local_self),
-                per_owner(local_neigh),
-                bias_rows,
-            ],
-            axis=1,
-        )
-    )
-    returned_grads = incoming[:, :slot_cap].reshape(slots, feature_dim)
-    d_quotient = dot(asked_hot, returned_grads, ROWS)
-    summed = jnp.sum(incoming[:, slot_cap:].astype(jnp.float32), axis=0)
-    gathered = lax.all_gather(summed, AXES, axis=0, tiled=False)
-    rem_each = remainder.shape[0] // devices
-    w_each = feature_dim // devices
     nodes_total = nodes_dev * devices
     weight_scale = 1.0 / math.sqrt(nodes_total)
     remain_scale = math.sqrt(remainder.shape[0] / nodes_total)
-    d_remainder = gathered[:, :rem_each].reshape(-1, feature_dim) * remain_scale
-    d_self = gathered[:, rem_each : rem_each + w_each].reshape(-1, feature_dim) * weight_scale
-    d_neigh = gathered[:, rem_each + w_each : rem_each + 2 * w_each].reshape(-1, feature_dim) * weight_scale
-    last = gathered[:, rem_each + 2 * w_each]
-    d_bias = (last[:, :bias_each] + last[:, bias_each : 2 * bias_each]).reshape(-1) * weight_scale
+    returned_grads, d_remainder = spread_grads(
+        outgoing, local_remain.astype(jnp.bfloat16), devices, remain_scale
+    )
+    d_quotient = dot(asked_hot, returned_grads, ROWS)
+    d_self = summed[:feature_dim] * weight_scale
+    d_neigh = summed[feature_dim : 2 * feature_dim] * weight_scale
+    d_bias = summed[2 * feature_dim] * weight_scale
     return (out, d_quotient, d_remainder, d_self, d_neigh, d_bias)
 
 

time: 517 us -> 463 us (0.90)
  blocking collectives: 59.7 us -> 0 us
  waiting for transfers between devices: 168 us -> 211 us
  Pallas kernels: 173 us -> 154 us
  starting transfers between devices: 23.9 us -> 13.6 us
  local copies, waits for them, and re-layouts: 12.3 us -> 3.47 us
    psum x0 -> x1, waiting for transfers between devices: none -> 126 us  [per_device(): lax.psum(jnp.concatenate([local_self, local_neigh, bias_rows], axis=0), A...]
    pallas_call x1, Pallas kernels: 171 us -> 74.2 us  [build_counts(): pl.pallas_call(functools.partial(count_kernel, dump), grid=(blocks,), out...]
    pallas_call x0 -> x2, Pallas kernels: none -> 78.9 us  [the longest x1 43.5 us: spread_grads(): pl.pallas_call(functools.partial(spread_kernel, devices, scale), out_shap...]
    all_to_all x2 -> x0, blocking collectives: 59.7 us -> none  [exchange(): return lax.all_to_all(buffer, AXES, split_axis=0, concat_axis=0, tiled=True)]
    all_gather x1 -> x0, waiting for transfers between devices: 58.2 us -> none  [per_device(): gathered = lax.all_gather(summed, AXES, axis=0, tiled=False)]
    ppermute x4, waiting for transfers between devices: 19.7 us -> 1.61 us  [shifted(): return lax.ppermute(block, axis, route)]
    all_to_all x1 -> x0, waiting for transfers between devices: 17.7 us -> none  [exchange(): return lax.all_to_all(buffer, AXES, split_axis=0, concat_axis=0, tiled=True)]
    reduce_scatter x1, waiting for transfers between devices: 72.6 us -> 83.2 us  [per_device(): lax.psum_scatter(source_grads, 'blk', scatter_dimension=0, tiled=True)]
  transfers between devices with their start and end apart: 8 -> 7, of which waited for: 5 -> 4; matrix products, arithmetic and copies ran while one was open for 5% -> 9% of each run, Pallas kernels for 33% -> 16%
where the time goes in v2:
time: 463 us
  waiting for transfers between devices  211 us (46%)
  Pallas kernels  154 us (33%)
  matrix products  60 us (13%)
  between operations  14.1 us (3%)
  starting transfers between devices  13.6 us (3%)
  other arithmetic  5.94 us (1%)
    psum x1, waiting for transfers between devices, per_device(): lax.psum(jnp.concatenate([local_self, local_neigh, bias_rows], axis=0), A...  126 us
    reduce_scatter x1, waiting for transfers between devices, per_device(): lax.psum_scatter(source_grads, 'blk', scatter_dimension=0, tiled=True)  83.2 us
    pallas_call x1, Pallas kernels, build_counts(): pl.pallas_call(functools.partial(count_kernel, dump), grid=(blocks,), out...  74.2 us
    dot_general x17, matrix products, dot(): return lax.dot_general(a, b, dims, preferred_element_type=jnp.float32)  60 us
    pallas_call x1, Pallas kernels, spread_grads(): pl.pallas_call(functools.partial(spread_kernel, devices, scale), out_shap...  43.5 us
    pallas_call x1, Pallas kernels, fetch_rows(): pl.pallas_call(functools.partial(fetch_kernel, devices), out_shape=(jax.S...  35.4 us
    ppermute x4, starting transfers between devices, shifted(): return lax.ppermute(block, axis, route)  13.3 us
  transfers between devices with their start and end apart: 7, of which 4 were waited for; matrix products, arithmetic and copies ran while one was open for 9% of the time, Pallas kernels for 16%

profile of v2, /device:TPU:1, one launch (start us, length us, event | category | flops | bytes accessed | tf_op | source)
XLA Modules:
  0.0 462.6 jit_solution(8091244223188373183)
XLA Ops:
  7.2 1.4 fusion.18
  11.1 1.0 copy-done.2
  12.1 35.4 %fetch_rows.1 = (bf16[2048,256]{1,0:T(8,128)(2,1)S(1)}, s32[2048,1]{1,0:T(8,128)S(1)}) custom-call(f32[128,1,128]{2,1,0:T(1,128)S(1)} %bitcast.30, bf16[1024,256]{1,0:T(8,128)(2,1)S(1)} %copy-done.2), custom_call_target="tpu_custom_call" | custom-call | tf_op jit(solution)/shard_map/fetch_rows/pallas_call | solution.py:265
  47.5 1.5 fusion.5
  49.0 2.7 multiply_convert_fusion.4
  51.8 1.0 fusion.33
  52.7 2.0 collective-permute-start
  54.8 1.4 edge_prep.1
  56.5 74.2 %edge_counts.1 = (bf16[1024,16384]{1,0:T(8,128)(2,1)}, bf16[1024,512]{1,0:T(8,128)(2,1)S(1)}, f32[1024,1]{1,0:T(8,128)S(1)}) custom-call(s32[8]{0:T(128)S(1)} %copy-done.5, s32[8,1,6144]{2,1,0:T(1,128)S(1)} %broadcast_in_dim.16.fast_ref, s32[8,1,6144]{2,1,0:T(1,128)S(1)} %broadcast_in_dim.17.slow_ref, s32[8,1,128]{2,1,0:T(1,128)S(1)} %bitcast.32), custom_call_target="tpu_custom_call" | custom-call | flops 80000000000 | bytes 40000000 | tf_op jit(solution)/shard_map/edge_counts/pallas_call | solution.py:129
  130.9 1.3 fusion.35
  132.2 18.4 %fusion.36 = f32[1024,256]{1,0:T(8,128)} fusion(bf16[1024,16384]{1,0:T(8,128)(2,1)} %get-tuple-element.20, bf16[16384,256]{1,0:T(8,128)(2,1)} %all-gather.2.cloned.1.call-done), kind=kOutput, calls=%fused_computation.65 | convolution fusion | flops 8589934592 | bytes 42991616 | tf_op jit(solution)/shard_map/dot_general | solution.py:387
  150.6 1.8 fusion.14
  152.4 1.5 convert_reduce_fusion
  156.0 17.4 %convolution_convert_fusion = bf16[16384,256]{1,0:T(8,128)(2,1)} fusion(bf16[1024,16384]{1,0:T(8,128)(2,1)} %get-tuple-element.20, bf16[1024,256]{1,0:T(8,128)(2,1)S(1)} %fusion.16), kind=kOutput, calls=%fused_computation | convolution fusion | flops 8594128896 | bytes 42467328 | tf_op jit(solution)/shard_map/dot_general | solution.py:387
  174.0 11.3 %collective-permute-start.3 = (bf16[256,256]{1,0:T(8,128)(2,1)S(1)}, bf16[256,256]{1,0:T(8,128)(2,1)S(1)}, u32[]{:S(2)}, u32[]{:S(2)}) collective-permute-start(bf16[256,256]{1,0:T(8,128)(2,1)S(1)} %get-tuple-element.34), channel_id=1, source_target_pairs={{16,0},{32,16},{48,32},{64,48},{80,64},{96,80},{112,96},{0,112},{1... | collective-permute-start | bytes 393224 | tf_op jit(solution)/shard_map/ppermute | solution.py:379
  187.3 126.3 %all-reduce.4.cloned.1.call-done = f32[520,256]{1,0:T(8,128)} async-done(((f32[520,256]{1,0:T(8,128)}), f32[520,256]{1,0:T(8,128)}) %all-reduce.4.cloned.1.call-update) | async-done | bytes 532496 | tf_op jit(solution)/shard_map/psum | solution.py:454
  313.6 1.3 slice_multiply_fusion.2
  314.8 1.9 slice_multiply_fusion
  316.7 83.2 %reduce-scatter.2.cloned.1.call-done = bf16[1024,256]{1,0:T(8,128)(2,1)} async-done(((bf16[16384,256]{1,0:T(8,128)(2,1)}), bf16[1024,256]{1,0:T(8,128)(2,1)}) %reduce-scatter.2.cloned.1.call-update) | async-done | bytes 524304 | tf_op jit(solution)/shard_map/reduce_scatter | solution.py:447
  399.9 1.4 maximum_add_fusion
  401.3 3.8 fusion.9.grads_ref
  405.1 2.7 fusion.15.rem_ref
  407.8 43.5 %spread_grads.1 = (bf16[2048,256]{1,0:T(8,128)(2,1)S(1)}, f32[1024,256]{1,0:T(8,128)S(1)}) custom-call(bf16[2048,256]{1,0:T(8,128)(2,1)S(1)} %fusion.9.grads_ref, bf16[1024,256]{1,0:T(8,128)(2,1)S(1)} %fusion.15.rem_ref), custom_call_target="tpu_custom_call" | custom-call | tf_op jit(solution)/shard_map/spread_grads/pallas_call | solution.py:354
  451.4 3.7 fusion.2
  (62 shorter events, 8.7 us)
Async XLA Ops:
  7.2 40.3 %copy-start = (bf16[1024,256]{1,0:T(8,128)(2,1)S(1)}, bf16[1024,256]{1,0:T(8,128)(2,1)}, u32[]{:S(2)}) copy-start(bf16[1024,256]{1,0:T(8,128)(2,1)} %param.16) | copy-start | bytes 1572868
  7.2 125.0 %all-gather.2.cloned.1.call-start = ((), (), s32[]{:S(2)}) async-start(), calls=%async_computation.1 | async-start | bytes 8912896 | tf_op jit(solution)/shard_map/all_gather | solution.py:429
  10.0 44.7 %copy-start.5 = (s32[8]{0:T(128)S(1)}, s32[8]{0:T(128)}, u32[]{:S(2)}) copy-start(s32[8]{0:T(128)} %count_ref.1) | copy-start | bytes 100
  10.0 44.8 %copy-start.3 = (s32[8,6144]{1,0:T(8,128)S(1)}, s32[8,6144]{1,0:T(8,128)}, u32[]{:S(2)}) copy-start(s32[8,6144]{1,0:T(8,128)} %src_ref.1) | copy-start | bytes 589828
  10.1 44.8 %copy-start.4 = (s32[8,6144]{1,0:T(8,128)S(1)}, s32[8,6144]{1,0:T(8,128)}, u32[]{:S(2)}) copy-start(s32[8,6144]{1,0:T(8,128)} %dst_ref.1) | copy-start | bytes 589828
  11.0 1.0 copy-start.2
  49.0 2.7 copy-start.13
  51.7 261.9 %all-reduce.4.cloned.1.call-start = ((), (), s32[]{:S(2)}) async-start(), calls=%async_computation.3 | async-start | bytes 1064960 | tf_op jit(solution)/shard_map/psum | solution.py:454
  52.7 97.8 %collective-permute-start = (bf16[256,256]{1,0:T(8,128)(2,1)S(1)}, bf16[256,256]{1,0:T(8,128)(2,1)}, u32[]{:S(2)}, u32[]{:S(2)}) collective-permute-start(bf16[256,256]{1,0:T(8,128)(2,1)S(1)} %get-tuple-element.31), channel_id=1, source_target_pairs={{112,0},{0,16},{16,32},{32,48},{48,64},{64,80},{80,96},{96,112},{1... | collective-permute-start | bytes 393224 | tf_op jit(solution)/shard_map/ppermute | solution.py:379
  54.7 95.8 %collective-permute-start.1 = (bf16[256,256]{1,0:T(8,128)(2,1)S(1)}, bf16[256,256]{1,0:T(8,128)(2,1)}, u32[]{:S(2)}, u32[]{:S(2)}) collective-permute-start(bf16[256,256]{1,0:T(8,128)(2,1)S(1)} %get-tuple-element.32), channel_id=1, source_target_pairs={{16,0},{32,16},{48,32},{64,48},{80,64},{96,80},{112,96},{0,112},{1... | collective-permute-start | bytes 393224 | tf_op jit(solution)/shard_map/ppermute | solution.py:379
  56.5 74.4 %copy-start.6 = (bf16[1024,256]{1,0:T(8,128)(2,1)S(1)}, bf16[1024,256]{1,0:T(8,128)(2,1)}, u32[]{:S(2)}) copy-start(bf16[1024,256]{1,0:T(8,128)(2,1)} %get-tuple-element.39) | copy-start | bytes 1572868
  56.5 74.4 %copy-start.8 = (bf16[256,256]{1,0:T(8,128)(2,1)S(1)}, bf16[256,256]{1,0:T(8,128)(2,1)}, u32[]{:S(2)}) copy-start(bf16[256,256]{1,0:T(8,128)(2,1)} %param.20) | copy-start | bytes 393220
  132.2 20.2 %copy-start.7 = (f32[1024,256]{1,0:T(8,128)S(1)}, f32[1024,256]{1,0:T(8,128)}, u32[]{:S(2)}) copy-start(f32[1024,256]{1,0:T(8,128)} %fusion.35) | copy-start | bytes 3145732
  132.2 20.2 %copy-start.9 = (bf16[1024,256]{1,0:T(8,128)(2,1)S(1)}, bf16[1024,256]{1,0:T(8,128)(2,1)}, u32[]{:S(2)}) copy-start(bf16[1024,256]{1,0:T(8,128)(2,1)} %param.23) | copy-start | bytes 1572868
  132.2 20.2 %copy-start.10 = (bf16[256,256]{1,0:T(8,128)(2,1)S(1)}, bf16[256,256]{1,0:T(8,128)(2,1)}, u32[]{:S(2)}) copy-start(bf16[256,256]{1,0:T(8,128)(2,1)} %param.21) | copy-start | bytes 393220
  132.2 20.2 %copy-start.12 = (f32[256]{0:T(256)S(1)}, f32[256]{0:T(256)}, u32[]{:S(2)}) copy-start(f32[256]{0:T(256)} %param.22) | copy-start | bytes 3076
  155.8 244.1 %reduce-scatter.2.cloned.1.call-start = ((), (), s32[]{:S(2)}) async-start(), calls=%async_computation.2 | async-start | bytes 8912896 | tf_op jit(solution)/shard_map/reduce_scatter | solution.py:447
  174.0 231.1 %copy-start.11 = (s32[1024]{0:T(1024)S(1)}, s32[1024]{0:T(1024)}, u32[]{:S(2)}) copy-start(s32[1024]{0:T(1024)} %param.14) | copy-start | bytes 12292
  174.0 12.3 %collective-permute-start.3 = (bf16[256,256]{1,0:T(8,128)(2,1)S(1)}, bf16[256,256]{1,0:T(8,128)(2,1)S(1)}, u32[]{:S(2)}, u32[]{:S(2)}) collective-permute-start(bf16[256,256]{1,0:T(8,128)(2,1)S(1)} %get-tuple-element.34), channel_id=1, source_target_pairs={{16,0},{32,16},{48,32},{64,48},{80,64},{96,80},{112,96},{0,112},{1... | collective-permute-start | bytes 393224 | tf_op jit(solution)/shard_map/ppermute | solution.py:379
  185.3 2.0 collective-permute-start.2
  401.3 54.7 %copy-start.1 = (bf16[1024,256]{1,0:T(8,128)(2,1)S(1)}, bf16[1024,256]{1,0:T(8,128)(2,1)}, u32[]{:S(2)}) copy-start(bf16[1024,256]{1,0:T(8,128)(2,1)} %param.16) | copy-start | bytes 1572868
Sparse Core Ops, SparseCore 0:
  51.8 69.3 all-gather.1
  155.9 157.5 all-reduce.3
  317.4 82.4 reduce-scatter.1

commit v3 on v2

--- a/solution.py
+++ b/solution.py
@@ -283,13 +283,19 @@
     )(ids, quotient)
 
 
-def spread_kernel(devices, scale, grads_ref, rem_ref, back_ref, total_ref, grads_in, rem_in, piece, whole, sems):
+def spread_kernel(
+    devices, rem_scale, scale, grads_ref, rem_ref, sums_ref, back_ref, total_ref, weight_ref, bias_ref,
+    grads_in, rem_in, sums_in, piece, whole, sems
+):
     slot_cap = grads_ref.shape[0] // devices
     slots = grads_ref.shape[0]
-    tall = piece.shape[0]
-    wide = piece.shape[1]
+    tall, wide = rem_in.shape[1:]
     across = rem_ref.shape[1] // wide
+    peers = sums_in.shape[0]
+    high = sums_ref.shape[0] - 8
     me = ring_place()
+    dom = lax.axis_index("dom")
+    blk = lax.axis_index("blk")
     meet_all(devices)
 
     def tile(device):
@@ -299,11 +305,22 @@
     def slot(device):
         return pl.ds(pl.multiple_of(device * slot_cap, slot_cap), slot_cap)
 
+    def share(peer):
+        top = pl.multiple_of(peer // across * 8, 8)
+        return (pl.ds(top, 8), pl.ds(pl.multiple_of(lax.rem(peer, across) * wide, wide), wide))
+
     def send_rem(k, carry):
         other = lax.rem(me + k, devices)
         send(rem_ref.at[tile(other)], rem_in.at[me], other, sems.at[0], sems.at[1])
         return carry
 
+    def send_sums(k, carry):
+        other = lax.rem(blk + k, peers)
+        to = dom * peers + other
+        send(sums_ref.at[share(other)], sums_in.at[blk, pl.ds(0, 8), :], to, sems.at[7], sems.at[8])
+        send(sums_ref.at[pl.ds(high, 8), pl.ds(0, wide)], sums_in.at[blk, pl.ds(8, 8), :], to, sems.at[7], sems.at[8])
+        return carry
+
     def send_grads(k, carry):
         other = lax.rem(me + k, devices)
         send(grads_ref.at[slot(other)], grads_in.at[slot(me)], other, sems.at[2], sems.at[3])
@@ -314,63 +331,292 @@
         send(piece, whole.at[me], other, sems.at[4], sems.at[5])
         return carry
 
+    def keep(src, dst):
+        copy = pltpu.make_async_copy(src, dst, sems.at[6])
+        copy.start()
+        copy.wait()
+
+    lax.fori_loop(1, peers, send_sums, 0)
     lax.fori_loop(1, devices, send_rem, 0)
     lax.fori_loop(1, devices, send_grads, 0)
-    own_rem = pltpu.make_async_copy(rem_ref.at[tile(me)], rem_in.at[me], sems.at[6])
-    own_rem.start()
-    own_rem.wait()
-    own_grads = pltpu.make_async_copy(grads_ref.at[slot(me)], grads_in.at[slot(me)], sems.at[6])
-    own_grads.start()
-    own_grads.wait()
+    keep(rem_ref.at[tile(me)], rem_in.at[me])
+    keep(grads_ref.at[slot(me)], grads_in.at[slot(me)])
+    keep(sums_ref.at[share(blk)], sums_in.at[blk, pl.ds(0, 8), :])
+    keep(sums_ref.at[pl.ds(high, 8), pl.ds(0, wide)], sums_in.at[blk, pl.ds(8, 8), :])
+    drain(sums_in.at[pl.ds(0, peers - 1)], sems.at[8])
     drain(rem_in.at[pl.ds(0, devices - 1)], sems.at[1])
-    piece[...] = jnp.sum(rem_in[...].astype(jnp.float32), axis=0) * scale
+    piece[:tall] = (jnp.sum(rem_in[...].astype(jnp.float32), axis=0) * rem_scale).astype(jnp.bfloat16)
+    piece[tall:] = (jnp.sum(sums_in[...], axis=0) * scale).astype(jnp.bfloat16)
     lax.fori_loop(1, devices, send_total, 0)
-    own_total = pltpu.make_async_copy(piece, whole.at[me], sems.at[6])
-    own_total.start()
-    own_total.wait()
+    keep(piece, whole.at[me])
     drain(grads_in.at[pl.ds(0, slots - slot_cap)], sems.at[3])
     back_ref[...] = grads_in[...]
-
     drain(whole.at[pl.ds(0, devices - 1)], sems.at[5])
 
     def lay(k, carry):
         for part in range(across):
-            total_ref[pl.ds(pl.multiple_of(k * tall, tall), tall), part * wide : (part + 1) * wide] = whole[
-                k * across + part
-            ]
+            got = whole[k * across + part].astype(jnp.float32)
+            lanes = slice(part * wide, (part + 1) * wide)
+            total_ref[pl.ds(pl.multiple_of(k * tall, tall), tall), lanes] = got[:tall]
+            weight_ref[pl.ds(pl.multiple_of(k * 8, 8), 8), lanes] = got[tall : tall + 8]
         return carry
 
     lax.fori_loop(0, devices // across, lay, 0)
+    for d in range(devices // peers):
+        bias_ref[d : d + 1, :] = whole[d * peers, tall + 8 : tall + 16, :].astype(jnp.float32)[0:1]
     drain(rem_in.at[pl.ds(0, devices - 1)], sems.at[0])
     drain(grads_in.at[pl.ds(0, slots - slot_cap)], sems.at[2])
     drain(whole.at[pl.ds(0, devices - 1)], sems.at[4])
-
-
-def spread_grads(outgoing, local_remain, devices, scale):
+    drain(sums_in.at[pl.ds(0, peers - 1)], sems.at[7])
+
+
+def spread_grads(outgoing, local_remain, sums, devices, peers, rem_scale, scale):
     rows, width = local_remain.shape
     wide = LANES
     tall = rows * width // devices // wide
+    doms = devices // peers
     vmem = pl.BlockSpec(memory_space=pltpu.VMEM)
     return pl.pallas_call(
-        functools.partial(spread_kernel, devices, scale),
+        functools.partial(spread_kernel, devices, rem_scale, scale),
         out_shape=(
             jax.ShapeDtypeStruct(outgoing.shape, jnp.bfloat16),
             jax.ShapeDtypeStruct((rows, width), jnp.float32),
+            jax.ShapeDtypeStruct((doms * (sums.shape[0] - 8), width), jnp.float32),
+            jax.ShapeDtypeStruct((doms, wide), jnp.float32),
         ),
-        in_specs=[vmem, vmem],
-        out_specs=(vmem, vmem),
+        in_specs=[vmem, vmem, vmem],
+        out_specs=(vmem, vmem, vmem, vmem),
         scratch_shapes=[
             pltpu.VMEM(outgoing.shape, jnp.bfloat16),
             pltpu.VMEM((devices, tall, wide), jnp.bfloat16),
-            pltpu.VMEM((tall, wide), jnp.float32),
-            pltpu.VMEM((devices, tall, wide), jnp.float32),
-            pltpu.SemaphoreType.DMA((7,)),
+            pltpu.VMEM((peers, 16, wide), jnp.float32),
+            pltpu.VMEM((tall + 16, wide), jnp.bfloat16),
+            pltpu.VMEM((devices, tall + 16, wide), jnp.bfloat16),
+            pltpu.SemaphoreType.DMA((9,)),
         ],
         compiler_params=pltpu.CompilerParams(
             collective_id=2, has_side_effects=True, vmem_limit_bytes=32 << 20
         ),
         name="spread_grads",
-    )(outgoing, local_remain)
+    )(outgoing, local_remain, sums)
+
+
+def reduce_kernel(
+    counts_ref, grad_ref, weights_ref, out_ref, sums_ref, load, part, mid, fin, half_sum, mid2, fin2, sems_load, s_out, s_mid, s_fin, t_out, t_mid, t_fin, weights_in, w_out, w_in
+):
+    side = 4
+    nodes = grad_ref.shape[1]
+    feats = grad_ref.shape[0] // 2
+    span = nodes // 2
+    dom = lax.axis_index("dom")
+    blk = lax.axis_index("blk")
+    x, y = blk // side, lax.rem(blk, side)
+
+    def at(dx, dy):
+        return lax.rem(x + dx, side) * side + lax.rem(y + dy, side)
+
+    def device(half, first, second):
+        dx, dy = (first, second) if half == 0 else (second, first)
+        return (dom, at(dx, dy))
+
+    barrier = pltpu.get_barrier_semaphore()
+    for dx, dy in ((1, 0), (3, 0), (0, 1), (0, 3)):
+        pl.semaphore_signal(barrier, inc=1, device_id=(dom, at(dx, dy)), device_id_type=MESH)
+    doms = weights_ref.shape[0]
+    for k in range(1, doms):
+        pl.semaphore_signal(barrier, inc=1, device_id=(lax.rem(dom + k, doms), blk), device_id_type=MESH)
+
+    order = [(2, 2), (2, 1), (1, 2), (2, 3), (3, 2), (2, 0), (0, 2), (1, 1), (3, 3), (1, 3), (3, 1)]
+    order += [(1, 0), (0, 1), (3, 0), (0, 3), (0, 0)]
+    depth = load.shape[0]
+
+    def fetch(i):
+        dx, dy = order[i]
+        columns = pl.ds(pl.multiple_of(at(dx, dy) * nodes, nodes), nodes)
+        return pltpu.make_async_copy(counts_ref.at[:, columns], load.at[i % depth], sems_load.at[i % depth])
+
+    for i in range(depth - 1):
+        fetch(i).start()
+    pl.semaphore_wait(barrier, 4 + doms - 1)
+
+    def to_dom(k):
+        other = lax.rem(dom + k, doms)
+        return pltpu.make_async_remote_copy(
+            src_ref=weights_ref.at[other],
+            dst_ref=weights_in.at[k],
+            send_sem=w_out.at[k],
+            recv_sem=w_in.at[k],
+            device_id=(other, blk),
+            device_id_type=MESH,
+        )
+
+    for k in range(1, doms):
+        to_dom(k).start()
+
+    def remote(src, dst, half, first, second, send_sem, recv_sem):
+        return pltpu.make_async_remote_copy(
+            src_ref=src,
+            dst_ref=dst,
+            send_sem=send_sem,
+            recv_sem=recv_sem,
+            device_id=device(half, first, second),
+            device_id_type=MESH,
+        )
+
+    def along(unit):
+        return unit % 2 == 0
+
+    def to_mid(half, unit):
+        return remote(
+            part.at[half, 2, unit], mid.at[half, unit], half, 1 if along(unit) else 3, 0,
+            s_out.at[half, 0, unit], s_mid.at[half, unit],
+        )
+
+    def to_fin(half, first, unit):
+        way = 0 if first == 1 else 1
+        return remote(
+            part.at[half, first, unit], fin.at[half, way, unit], half, first, 0,
+            s_out.at[half, 1 + way, unit], s_fin.at[half, way, unit],
+        )
+
+    def relays(first, unit):
+        return along(unit) == (first == 1)
+
+    tile = 256
+    waiting = []
+    for i, (dx, dy) in enumerate(order):
+        if i + depth - 1 < len(order):
+            fetch(i + depth - 1).start()
+        fetch(i).wait()
+
+        def columns(n, carry, slot=i % depth, dx=dx, dy=dy):
+            cut = pl.ds(pl.multiple_of(n * tile, tile), tile)
+            value = jnp.dot(grad_ref[...], load[slot, :, cut], preferred_element_type=jnp.float32)
+            part[0, dx, dy, :, cut] = value[:feats].astype(jnp.bfloat16)
+            part[1, dy, dx, :, cut] = value[feats:].astype(jnp.bfloat16)
+            return carry
+
+        lax.fori_loop(0, nodes // tile, columns, 0)
+        for half, first, unit in ((0, dx, dy), (1, dy, dx)):
+            if first == 2:
+                to_mid(half, unit).start()
+            elif first != 0:
+                if relays(first, unit):
+                    waiting.append((half, first, unit))
+                else:
+                    to_fin(half, first, unit).start()
+    waiting.sort(key=lambda item: (2, 1, 3, 0).index(item[2]))
+    for half, first, unit in waiting:
+        to_mid(half, unit).wait_recv()
+        mine = part[half, first, unit].astype(jnp.float32)
+        part[half, first, unit] = (mine + mid[half, unit].astype(jnp.float32)).astype(jnp.bfloat16)
+        to_fin(half, first, unit).start()
+
+    def cut(piece):
+        return pl.ds(piece * span, span)
+
+    def to_mid2(half, piece):
+        return remote(
+            half_sum.at[half, 1, :, cut(piece)], mid2.at[half, piece], half, 0, 1 if piece == 0 else 3,
+            t_out.at[half, 0, piece], t_mid.at[half, piece],
+        )
+
+    def to_fin2(half, second, piece):
+        way = 0 if second == 1 else 1
+        return remote(
+            half_sum.at[half, 0 if second == 1 else 2, :, cut(piece)], fin2.at[half, way, piece], half, 0, second,
+            t_out.at[half, 1 + way, piece], t_fin.at[half, way, piece],
+        )
+
+    def summed(half, unit):
+        to_fin(half, 1, unit).wait_recv()
+        to_fin(half, 3, unit).wait_recv()
+        total = part[half, 0, unit].astype(jnp.float32) + fin[half, 0, unit].astype(jnp.float32)
+        return total + fin[half, 1, unit].astype(jnp.float32)
+
+    for half in range(2):
+        half_sum[half, 1] = summed(half, 2).astype(jnp.bfloat16)
+        to_mid2(half, 0).start()
+        to_mid2(half, 1).start()
+    for second in (1, 3):
+        direct, relayed = (1, 0) if second == 1 else (0, 1)
+        for half in range(2):
+            half_sum[half, second - 1] = summed(half, second).astype(jnp.bfloat16)
+            to_fin2(half, second, direct).start()
+    for second in (1, 3):
+        direct, relayed = (1, 0) if second == 1 else (0, 1)
+        for half in range(2):
+            to_mid2(half, relayed).wait_recv()
+            mine = half_sum[half, second - 1, :, cut(relayed)].astype(jnp.float32)
+            both = mine + mid2[half, relayed].astype(jnp.float32)
+            half_sum[half, second - 1, :, cut(relayed)] = both.astype(jnp.bfloat16)
+            to_fin2(half, second, relayed).start()
+    for half in range(2):
+        rows = pl.ds(half * feats, feats)
+        out_ref[rows, :] = summed(half, 0)
+    for half in range(2):
+        rows = pl.ds(half * feats, feats)
+        for piece in range(2):
+            to_fin2(half, 1, piece).wait_recv()
+            to_fin2(half, 3, piece).wait_recv()
+            total = out_ref[rows, cut(piece)] + fin2[half, 0, piece].astype(jnp.float32)
+            out_ref[rows, cut(piece)] = total + fin2[half, 1, piece].astype(jnp.float32)
+    sums = weights_ref[dom]
+    for k in range(1, doms):
+        to_dom(k).wait_recv()
+        sums = sums + weights_in[k]
+    sums_ref[...] = sums
+    for k in range(1, doms):
+        to_dom(k).wait_send()
+    for half in range(2):
+        for unit in range(side):
+            to_mid(half, unit).wait_send()
+            to_fin(half, 1, unit).wait_send()
+            to_fin(half, 3, unit).wait_send()
+        for piece in range(2):
+            to_mid2(half, piece).wait_send()
+            to_fin2(half, 1, piece).wait_send()
+            to_fin2(half, 3, piece).wait_send()
+
+
+def reduce_sources(counts, grad, weights):
+    feats, nodes = grad.shape
+    half = feats // 2
+    kind = jnp.bfloat16
+    dma = pltpu.SemaphoreType.DMA
+    vmem = pl.BlockSpec(memory_space=pltpu.VMEM)
+    return pl.pallas_call(
+        reduce_kernel,
+        out_shape=(
+            jax.ShapeDtypeStruct((feats, nodes), jnp.float32),
+            jax.ShapeDtypeStruct(weights.shape[1:], jnp.float32),
+        ),
+        in_specs=[pl.BlockSpec(memory_space=pl.ANY), vmem, vmem],
+        out_specs=(vmem, vmem),
+        scratch_shapes=[
+            pltpu.VMEM((3, nodes, nodes), kind),
+            pltpu.VMEM((2, 4, 4, half, nodes), kind),
+            pltpu.VMEM((2, 4, half, nodes), kind),
+            pltpu.VMEM((2, 2, 4, half, nodes), kind),
+            pltpu.VMEM((2, 3, half, nodes), kind),
+            pltpu.VMEM((2, 2, half, nodes // 2), kind),
+            pltpu.VMEM((2, 2, 2, half, nodes // 2), kind),
+            dma((3,)),
+            dma((2, 3, 4)),
+            dma((2, 4)),
+            dma((2, 2, 4)),
+            dma((2, 3, 2)),
+            dma((2, 2)),
+            dma((2, 2, 2)),
+            pltpu.VMEM(weights.shape, jnp.float32),
+            dma((weights.shape[0],)),
+            dma((weights.shape[0],)),
+        ],
+        compiler_params=pltpu.CompilerParams(
+            collective_id=3, has_side_effects=True, vmem_limit_bytes=44 << 20
+        ),
+        name="reduce_sources",
+    )(counts, grad, weights)
 
 
 def shifted(block, axis, distance):
@@ -443,15 +689,17 @@
     )
     dagg_scaled = (dot(dpre, w_neigh, COLS) / divisor).astype(jnp.bfloat16)
     halo_grads = dot(halo_counts, dagg_scaled, ROWS).astype(jnp.bfloat16)
-    source_grads = dot(counts, dagg_scaled, ROWS).astype(jnp.bfloat16)
-    own_grads = lax.psum_scatter(source_grads, "blk", scatter_dimension=0, tiled=True)
     tail_grad = shifted(halo_grads[:HALO], "dom", -1)
     head_grad = shifted(halo_grads[HALO:], "dom", 1)
     local_self = dot(features, dpre, ROWS)
     local_neigh = dot(neighbour, dpre, ROWS)
     local_bias = jnp.sum(dpre.astype(jnp.float32), axis=0)
-    bias_rows = jnp.pad(local_bias[None, :], ((0, 7), (0, 0)))
-    summed = lax.psum(jnp.concatenate([local_self, local_neigh, bias_rows], axis=0), AXES)
+    doms = lax.axis_size("dom")
+    bias_rows = jnp.pad(local_bias.reshape(doms, 1, -1), ((0, 0), (0, 7), (0, feature_dim - feature_dim // doms)))
+    weights = jnp.concatenate([local_self, local_neigh], axis=0).reshape(doms, -1, feature_dim)
+    weights = jnp.concatenate([weights, bias_rows], axis=1)
+    own_grads, weight_sums = reduce_sources(counts, dagg_scaled.T, weights)
+    own_grads = own_grads.T
     dx_self = dot(dpre, w_self, COLS)
     edges = jnp.concatenate(
         [
@@ -461,20 +709,25 @@
         ],
         axis=0,
     )
-    grad_x = dx_self + own_grads.astype(jnp.float32) + edges
+    grad_x = dx_self + own_grads + edges
     outgoing = dot(slot_hot, (grad_x * remain_rows).astype(jnp.bfloat16), ROWS).astype(jnp.bfloat16)
     local_remain = dot(rem_hot, (grad_x * quot_rows).astype(jnp.bfloat16), ROWS)
 
     nodes_total = nodes_dev * devices
     weight_scale = 1.0 / math.sqrt(nodes_total)
     remain_scale = math.sqrt(remainder.shape[0] / nodes_total)
-    returned_grads, d_remainder = spread_grads(
-        outgoing, local_remain.astype(jnp.bfloat16), devices, remain_scale
+    returned_grads, d_remainder, d_weights, d_bias = spread_grads(
+        outgoing,
+        local_remain.astype(jnp.bfloat16),
+        weight_sums,
+        devices,
+        lax.axis_size("blk"),
+        remain_scale,
+        weight_scale,
     )
     d_quotient = dot(asked_hot, returned_grads, ROWS)
-    d_self = summed[:feature_dim] * weight_scale
-    d_neigh = summed[feature_dim : 2 * feature_dim] * weight_scale
-    d_bias = summed[2 * feature_dim] * weight_scale
+    d_self, d_neigh = d_weights[:feature_dim], d_weights[feature_dim:]
+    d_bias = d_bias[:, : feature_dim // doms].reshape(-1)
     return (out, d_quotient, d_remainder, d_self, d_neigh, d_bias)
 
 

time: 463 us -> 291 us (0.63)
  waiting for transfers between devices: 211 us -> 0.1 us
  Pallas kernels: 154 us -> 211 us
  matrix products: 60 us -> 35.3 us
  local copies, waits for them, and re-layouts: 3.47 us -> 8.86 us
    psum x1 -> x0, waiting for transfers between devices: 126 us -> none  [per_device(): lax.psum(jnp.concatenate([local_self, local_neigh, bias_rows], axis=0), A...]
    reduce_scatter x1 -> x0, waiting for transfers between devices: 83.2 us -> none  [per_device(): lax.psum_scatter(source_grads, 'blk', scatter_dimension=0, tiled=True)]
    pallas_call x1 -> x2, Pallas kernels: 43.5 us -> 115 us  [the longest x1 71.5 us: reduce_sources(): pl.pallas_call(reduce_kernel, out_shape=(jax.ShapeDtypeStruct((feats, nod...]
    dot_general x17 -> x16, matrix products: 60 us -> 35.3 us  [dot(): return lax.dot_general(a, b, dims, preferred_element_type=jnp.float32)]
    pallas_call x1, Pallas kernels: 74.2 us -> 60 us  [build_counts(): pl.pallas_call(functools.partial(count_kernel, dump), grid=(blocks,), out...]
    ppermute x4, starting transfers between devices: 13.3 us -> 17.9 us  [shifted(): return lax.ppermute(block, axis, route)]
  transfers between devices with their start and end apart: 7 -> 5, of which waited for: 4 -> 1; matrix products, arithmetic and copies ran while one was open for 9% -> 8% of each run, Pallas kernels for 16% -> 46%
where the time goes in v3:
time: 291 us; the launch traced here: 290 us
  Pallas kernels  211 us (73%)
  matrix products  35.3 us (12%)
  starting transfers between devices  18 us (6%)
  between operations  14.4 us (5%)
  local copies, waits for them, and re-layouts  8.86 us (3%)
    pallas_call x1, Pallas kernels, reduce_sources(): pl.pallas_call(reduce_kernel, out_shape=(jax.ShapeDtypeStruct((feats, nod...  71.5 us
    pallas_call x1, Pallas kernels, build_counts(): pl.pallas_call(functools.partial(count_kernel, dump), grid=(blocks,), out...  60 us
    pallas_call x1, Pallas kernels, spread_grads(): pl.pallas_call(functools.partial(spread_kernel, devices, rem_scale, scale...  43.2 us
    pallas_call x1, Pallas kernels, fetch_rows(): pl.pallas_call(functools.partial(fetch_kernel, devices), out_shape=(jax.S...  35.4 us
    dot_general x16, matrix products, dot(): return lax.dot_general(a, b, dims, preferred_element_type=jnp.float32)  35.3 us
    ppermute x4, starting transfers between devices, shifted(): return lax.ppermute(block, axis, route)  17.9 us
  transfers between devices with their start and end apart: 5, of which 1 were waited for; matrix products, arithmetic and copies ran while one was open for 8% of the time, Pallas kernels for 46%

profile of v3, /device:TPU:1, one launch (start us, length us, event | category | flops | bytes accessed | tf_op | source)
XLA Modules:
  0.0 290.2 jit_solution(16168078831641728216)
XLA Ops:
  7.2 1.4 fusion.26
  10.0 0.9 fusion.27
  11.0 1.0 copy-done.2
  12.0 35.4 %fetch_rows.1 = (bf16[2048,256]{1,0:T(8,128)(2,1)S(1)}, s32[2048,1]{1,0:T(8,128)S(1)}) custom-call(f32[128,1,128]{2,1,0:T(1,128)S(1)} %bitcast.34, bf16[1024,256]{1,0:T(8,128)(2,1)S(1)} %copy-done.2), custom_call_target="tpu_custom_call" | custom-call | tf_op jit(solution)/shard_map/fetch_rows/pallas_call | solution.py:265
  47.4 1.5 fusion.7
  48.9 2.3 multiply_convert_fusion.4
  51.3 1.0 fusion.42
  52.3 2.0 collective-permute-start
  54.3 2.5 copy.43
  56.9 1.4 edge_prep.1
  58.6 1.3 copy.44
  60.2 60.0 %edge_counts.1 = (bf16[1024,16384]{1,0:T(8,128)(2,1)}, bf16[1024,512]{1,0:T(8,128)(2,1)S(1)}, f32[1024,1]{1,0:T(8,128)S(1)}) custom-call(s32[8]{0:T(128)S(1)} %copy-done.5, s32[8,1,6144]{2,1,0:T(1,128)S(1)} %broadcast_in_dim.14.fast_ref, s32[8,1,6144]{2,1,0:T(1,128)S(1)} %broadcast_in_dim.15.slow_ref, s32[8,1,128]{2,1,0:T(1,128)S(1)} %bitcast.37), custom_call_target="tpu_custom_call" | custom-call | flops 80000000000 | bytes 40000000 | tf_op jit(solution)/shard_map/edge_counts/pallas_call | solution.py:129
  120.9 17.5 %fusion.45 = f32[1024,256]{0,1:T(8,128)} fusion(bf16[1024,16384]{1,0:T(8,128)(2,1)} %get-tuple-element.24.counts_ref, bf16[16384,256]{1,0:T(8,128)(2,1)} %all-gather.2.cloned.1.call-done), kind=kOutput, calls=%fused_computation.65 | convolution fusion | flops 8589934592 | bytes 42991616 | tf_op jit(solution)/shard_map/dot_general | solution.py:633
  138.3 1.9 fusion.20
  140.3 1.5 convert_reduce_fusion
  143.3 1.8 collective-permute-start.2
  145.1 14.1 %collective-permute-start.3 = (bf16[256,256]{0,1:T(8,128)(2,1)S(1)}, bf16[256,256]{0,1:T(8,128)(2,1)S(1)}, u32[]{:S(2)}, u32[]{:S(2)}) collective-permute-start(bf16[256,256]{0,1:T(8,128)(2,1)S(1)} %get-tuple-element.42), channel_id=1, source_target_pairs={{16,0},{32,16},{48,32},{64,48},{80,64},{96,80},{112,96},{0,112},{1... | collective-permute-start | bytes 393224 | tf_op jit(solution)/shard_map/ppermute | solution.py:625
  159.4 71.5 %reduce_sources.1 = (f32[256,1024]{1,0:T(8,128)S(1)}, f32[72,256]{1,0:T(8,128)S(1)}) custom-call(bf16[1024,16384]{1,0:T(8,128)(2,1)} %get-tuple-element.24.counts_ref, bf16[256,1024]{1,0:T(8,128)(2,1)S(1)} %bitcast.33, f32[8,72,256]{2,1,0:T(8,128)S(1)} %select_maximum_fusion.weights_ref), custom_call_target="tpu_custom_call" | custom-call | tf_op jit(solution)/shard_map/reduce_sources/pallas_call | solution.py:588
  231.4 1.0 fusion.21.rem_ref
  232.4 1.6 fusion.11.grads_ref
  234.0 43.2 %spread_grads.1 = (bf16[2048,256]{1,0:T(8,128)(2,1)S(1)}, f32[1024,256]{1,0:T(8,128)S(1)}, f32[512,256]{1,0:T(8,128)S(1)}, f32[8,128]{1,0:T(8,128)S(1)}) custom-call(bf16[2048,256]{1,0:T(8,128)(2,1)S(1)} %fusion.11.grads_ref, bf16[1024,256]{1,0:T(8,128)(2,1)S(1)} %fusion.21.rem_ref, f32[72,256]{1,0:T(8,128)S(1)} %get-tuple-element.29.sums_ref), custom_call_target="tpu_custom_call" | custom-call | tf_op jit(solution)/shard_map/spread_grads/pallas_call | solution.py:379
  277.3 0.8 fusion.41
  278.7 3.7 %fusion.2 = f32[1024,256]{1,0:T(8,128)} fusion(bf16[2048,256]{1,0:T(8,128)(2,1)S(1)} %get-tuple-element.30, s32[2048]{0:T(1024)S(1)} %reduce.1), kind=kOutput, calls=%fused_computation.4 | convolution fusion | flops 1075838976 | bytes 2105344 | tf_op jit(solution)/shard_map/dot_general | solution.py:633
  282.4 1.0 copy.52
  (66 shorter events, 5.5 us)
Async XLA Ops:
  7.2 40.2 %copy-start = (bf16[1024,256]{1,0:T(8,128)(2,1)S(1)}, bf16[1024,256]{1,0:T(8,128)(2,1)}, u32[]{:S(2)}) copy-start(bf16[1024,256]{1,0:T(8,128)(2,1)} %param.16) | copy-start | bytes 1572868
  7.2 113.7 %all-gather.2.cloned.1.call-start = ((), (), s32[]{:S(2)}) async-start(), calls=%async_computation | async-start | bytes 8912896 | tf_op jit(solution)/shard_map/all_gather | solution.py:675
  10.0 41.3 %copy-start.11 = (s32[1024,1]{0,1:T(1,128)}, s32[1024,1]{0,1:T(1,128)S(1)}, u32[]{:S(2)}) copy-start(s32[1024,1]{0,1:T(1,128)S(1)} %multiply_add_fusion) | copy-start | bytes 12292
  11.0 1.0 copy-start.2
  48.9 2.4 copy-start.9
  48.9 7.9 %copy-start.5 = (s32[8]{0:T(128)S(1)}, s32[8]{0:T(128)}, u32[]{:S(2)}) copy-start(s32[8]{0:T(128)} %count_ref.1) | copy-start | bytes 100
  48.9 8.0 %copy-start.3 = (s32[8,6144]{1,0:T(8,128)S(1)}, s32[8,6144]{1,0:T(8,128)}, u32[]{:S(2)}) copy-start(s32[8,6144]{1,0:T(8,128)} %src_ref.1) | copy-start | bytes 589828
  48.9 8.0 %copy-start.4 = (s32[8,6144]{1,0:T(8,128)S(1)}, s32[8,6144]{1,0:T(8,128)}, u32[]{:S(2)}) copy-start(s32[8,6144]{1,0:T(8,128)} %dst_ref.1) | copy-start | bytes 589828
  52.3 86.0 %collective-permute-start = (bf16[256,256]{1,0:T(8,128)(2,1)S(1)}, bf16[256,256]{1,0:T(8,128)(2,1)}, u32[]{:S(2)}, u32[]{:S(2)}) collective-permute-start(bf16[256,256]{1,0:T(8,128)(2,1)S(1)} %get-tuple-element.39), channel_id=1, source_target_pairs={{112,0},{0,16},{16,32},{32,48},{48,64},{64,80},{80,96},{96,112},{1... | collective-permute-start | bytes 393224 | tf_op jit(solution)/shard_map/ppermute | solution.py:625
  54.3 84.0 %collective-permute-start.1 = (bf16[256,256]{1,0:T(8,128)(2,1)S(1)}, bf16[256,256]{1,0:T(8,128)(2,1)}, u32[]{:S(2)}, u32[]{:S(2)}) collective-permute-start(bf16[256,256]{1,0:T(8,128)(2,1)S(1)} %get-tuple-element.40), channel_id=1, source_target_pairs={{16,0},{32,16},{48,32},{64,48},{80,64},{96,80},{112,96},{0,112},{1... | collective-permute-start | bytes 393224 | tf_op jit(solution)/shard_map/ppermute | solution.py:625
  60.2 60.3 %copy-start.6 = (bf16[1024,256]{1,0:T(8,128)(2,1)S(1)}, bf16[1024,256]{1,0:T(8,128)(2,1)}, u32[]{:S(2)}) copy-start(bf16[1024,256]{1,0:T(8,128)(2,1)} %get-tuple-element.47) | copy-start | bytes 1572868
  60.2 60.2 %copy-start.10 = (bf16[256,256]{1,0:T(8,128)(2,1)S(1)}, bf16[256,256]{1,0:T(8,128)(2,1)}, u32[]{:S(2)}) copy-start(bf16[256,256]{1,0:T(8,128)(2,1)} %param.20) | copy-start | bytes 393220
  138.3 1.9 copy-start.13
  138.3 1.9 copy-start.14
  138.3 2.0 copy-start.16
  143.3 87.7 %collective-permute-start.2 = (bf16[256,256]{0,1:T(8,128)(2,1)S(1)}, bf16[256,256]{0,1:T(8,128)(2,1)S(1)}, u32[]{:S(2)}, u32[]{:S(2)}) collective-permute-start(bf16[256,256]{0,1:T(8,128)(2,1)S(1)} %get-tuple-element.41), channel_id=1, source_target_pairs={{112,0},{0,16},{16,32},{32,48},{48,64},{64,80},{80,96},{96,112},{1... | collective-permute-start | bytes 393224 | tf_op jit(solution)/shard_map/ppermute | solution.py:625
  145.1 85.9 %collective-permute-start.3 = (bf16[256,256]{0,1:T(8,128)(2,1)S(1)}, bf16[256,256]{0,1:T(8,128)(2,1)S(1)}, u32[]{:S(2)}, u32[]{:S(2)}) collective-permute-start(bf16[256,256]{0,1:T(8,128)(2,1)S(1)} %get-tuple-element.42), channel_id=1, source_target_pairs={{16,0},{32,16},{48,32},{64,48},{80,64},{96,80},{112,96},{0,112},{1... | collective-permute-start | bytes 393224 | tf_op jit(solution)/shard_map/ppermute | solution.py:625
  159.4 72.0 %copy-start.8 = (f32[1024,256]{0,1:T(8,128)S(1)}, f32[1024,256]{0,1:T(8,128)}, u32[]{:S(2)}) copy-start(f32[1024,256]{0,1:T(8,128)} %copy.44) | copy-start | bytes 3145732
  159.4 72.0 %copy-start.15 = (s32[1024]{0:T(1024)S(1)}, s32[1024]{0:T(1024)}, u32[]{:S(2)}) copy-start(s32[1024]{0:T(1024)} %param.14) | copy-start | bytes 12292
  231.1 1.4 copy-start.7
  231.1 1.4 copy-start.12
  278.7 4.6 %copy-start.1 = (bf16[1024,256]{1,0:T(8,128)(2,1)S(1)}, bf16[1024,256]{1,0:T(8,128)(2,1)}, u32[]{:S(2)}) copy-start(bf16[1024,256]{1,0:T(8,128)(2,1)} %param.16) | copy-start | bytes 1572868
Sparse Core Ops, SparseCore 0:
  51.4 69.3 all-gather.1

commit v4 on v3

--- a/solution.py
+++ b/solution.py
@@ -11,7 +11,7 @@
 ROWS_BLK = 128
 HALO = 256
 LANES = 128
-BATCH = 16
+BATCH = 8
 AXES = ("dom", "blk")
 MESH = pl.DeviceIdType.MESH
 ROWS = (((0,), (0,)), ((), ()))
@@ -43,75 +43,102 @@
     number = jnp.zeros((blocks, 1), jnp.int32)
     for c in range(chunks):
         hits = jnp.dot(ones[:, c * LANES : (c + 1) * LANES], group, preferred_element_type=jnp.float32)
-        bits = jnp.sum(jnp.where(hits > 0.5, (1 << (col & 7)).astype(jnp.float32), 0.0), axis=1, keepdims=True)
+        bits = jnp.sum(jnp.where(hits > 0.5, (1 << (col & (LANES // BATCH - 1))).astype(jnp.float32), 0.0), axis=1, keepdims=True)
         bits = bits.astype(jnp.int32)
         some = bits > 0
-        found = found + jnp.where((col == number) & some, c * 256 + bits, 0)
+        found = found + jnp.where((col == number) & some, c * 65536 + bits, 0)
         number = number + some.astype(jnp.int32)
     flag_ref[...] = jnp.where(col == LANES - 1, number, found)
 
 
-def count_kernel(dump, count_ref, fast_ref, slow_ref, flag_ref, main_ref, halo_ref, deg_ref, cells):
+def count_kernel(dump, count_ref, fast_ref, slow_ref, flag_ref, main_ref, halo_ref, deg_ref, *cells):
     j = pl.program_id(0)
+    blocks = pl.num_programs(0) - 1
     his = dump // ROWS_BLK
     his_main = main_ref.shape[1] // LANES
     zero = jnp.zeros((ROWS_BLK, LANES), jnp.float32)
+    lanes = lax.broadcasted_iota(jnp.int32, (1, LANES), 1)
 
     @pl.when(j == 0)
     def _():
         def clear(i, carry):
-            cells[pl.ds(pl.multiple_of(i * ROWS_BLK, ROWS_BLK), ROWS_BLK), :] = zero
+            for ref in cells[:2]:
+                ref[pl.ds(pl.multiple_of(i * ROWS_BLK, ROWS_BLK), ROWS_BLK), :] = zero
             return carry
 
         lax.fori_loop(0, his, clear, 0)
-        cells[pl.ds(dump, 8), :] = jnp.zeros((8, LANES), jnp.float32)
-
-    count = count_ref[j]
-    lanes = lax.broadcasted_iota(jnp.int32, (1, LANES), 1)
-
-    def batch(t, carry):
-        keys = [fast_ref[0, 0, t * BATCH + i] for i in range(BATCH)]
+        for ref in cells:
+            ref[pl.ds(dump, 8), :] = jnp.zeros((8, LANES), jnp.float32)
+
+    count = jnp.where(j < blocks, count_ref[jnp.minimum(j, blocks - 1)], 0)
+    pairs = (count + 2 * BATCH - 1) // (2 * BATCH)
+
+    def add_batch(ref, first):
+        keys = [fast_ref[0, 0, first + i] for i in range(BATCH)]
         rows = [k >> 7 for k in keys]
-        olds = [cells[pl.ds(r, 1), :] for r in rows]
+        olds = [ref[pl.ds(r, 1), :] for r in rows]
         news = [old + jnp.where(lanes == (k & 127), 1.0, 0.0) for old, k in zip(olds, keys)]
         for r, new in zip(rows, news):
-            cells[pl.ds(r, 1), :] = new
-        return carry
-
-    lax.fori_loop(0, (count + BATCH - 1) // BATCH, batch, 0)
-
-    def chunk(c, carry):
-        entry = flag_ref[0, 0, c]
-        first = (entry >> 8) * LANES
-
-        def some(g, inner):
-            @pl.when(((entry >> g) & 1) != 0)
-            def _():
-                for i in range(BATCH):
-                    k = slow_ref[0, 0, first + g * BATCH + i]
-                    r = k >> 7
-                    cells[pl.ds(r, 1), :] = cells[pl.ds(r, 1), :] + jnp.where(lanes == (k & 127), 1.0, 0.0)
-
-            return inner
-
-        lax.fori_loop(0, LANES // BATCH, some, 0)
-        return carry
-
-    lax.fori_loop(0, flag_ref[0, 0, LANES - 1], chunk, 0)
-
-    def flush(ref, first):
-        def step(h, total):
-            at = pl.multiple_of((first + h) * ROWS_BLK, ROWS_BLK)
-            value = cells[pl.ds(at, ROWS_BLK), :]
-            ref[:, pl.ds(pl.multiple_of(h * LANES, LANES), LANES)] = value.astype(jnp.bfloat16)
-            cells[pl.ds(at, ROWS_BLK), :] = zero
-            return total + value
-
-        return step
-
-    total = lax.fori_loop(0, his_main, flush(main_ref, 0), zero, unroll=2)
-    total = lax.fori_loop(0, his - his_main, flush(halo_ref, his_main), total, unroll=2)
-    deg_ref[...] = jnp.sum(total, axis=1, keepdims=True)
+            ref[pl.ds(r, 1), :] = new
+
+    def turn(fill, leave):
+        def add_pair(t, carry):
+            add_batch(fill[0], t * 2 * BATCH)
+            add_batch(fill[1], t * 2 * BATCH + BATCH)
+            return carry
+
+        def flush(ref, first):
+            def step(h, total):
+                at = pl.multiple_of((first + h) * ROWS_BLK, ROWS_BLK)
+                rows = pl.ds(at, ROWS_BLK)
+                value = leave[0][rows, :] + leave[1][rows, :]
+                ref[:, pl.ds(pl.multiple_of(h * LANES, LANES), LANES)] = value.astype(jnp.bfloat16)
+                leave[0][rows, :] = zero
+                leave[1][rows, :] = zero
+                return total + value
+
+            return step
+
+        def both(t, total):
+            add_pair(t, 0)
+            return flush(main_ref, 0)(t, total)
+
+        steps = his_main
+        joint = jnp.minimum(pairs, steps)
+        total = lax.fori_loop(0, joint, both, zero)
+        lax.fori_loop(joint, pairs, add_pair, 0)
+        total = lax.fori_loop(joint, steps, flush(main_ref, 0), total)
+
+        total = lax.fori_loop(0, his - his_main, flush(halo_ref, his_main), total)
+        deg_ref[...] = jnp.sum(total, axis=1, keepdims=True)
+
+        def chunk(c, carry):
+            entry = flag_ref[0, 0, c]
+            first = (entry >> 16) * LANES
+
+            def some(g, inner):
+                @pl.when(((entry >> g) & 1) != 0)
+                def _():
+                    for i in range(BATCH):
+                        k = slow_ref[0, 0, first + g * BATCH + i]
+                        r = k >> 7
+                        old = fill[0][pl.ds(r, 1), :]
+                        fill[0][pl.ds(r, 1), :] = old + jnp.where(lanes == (k & 127), 1.0, 0.0)
+
+                return inner
+
+            lax.fori_loop(0, LANES // BATCH, some, 0)
+            return carry
+
+        lax.fori_loop(0, jnp.where(j < blocks, flag_ref[0, 0, LANES - 1], 0), chunk, 0)
+
+    @pl.when(lax.rem(j, 2) == 0)
+    def _():
+        turn(cells[:2], cells[2:])
+
+    @pl.when(lax.rem(j, 2) == 1)
+    def _():
+        turn(cells[2:], cells[:2])
 
 
 def build_counts(edge_src, edge_dst, block_count, part_nodes):
@@ -126,9 +153,16 @@
         name="edge_prep",
     )(edge_src, edge_dst, block_count[:, None])
     nodes = blocks * ROWS_BLK
+
+    def filled(j):
+        return (jnp.minimum(j, blocks - 1), 0, 0)
+
+    def left(j):
+        return (jnp.maximum(j - 1, 0), 0)
+
     return pl.pallas_call(
         functools.partial(count_kernel, dump),
-        grid=(blocks,),
+        grid=(blocks + 1,),
         out_shape=(
             jax.ShapeDtypeStruct((nodes, part_nodes), jnp.bfloat16),
             jax.ShapeDtypeStruct((nodes, 2 * HALO), jnp.bfloat16),
@@ -136,17 +170,17 @@
         ),
         in_specs=[
             pl.BlockSpec(memory_space=pltpu.SMEM),
-            pl.BlockSpec((1, 1, slots), lambda j: (j, 0, 0), memory_space=pltpu.SMEM),
-            pl.BlockSpec((1, 1, slots), lambda j: (j, 0, 0), memory_space=pltpu.SMEM),
-            pl.BlockSpec((1, 1, LANES), lambda j: (j, 0, 0), memory_space=pltpu.SMEM),
+            pl.BlockSpec((1, 1, slots), filled, memory_space=pltpu.SMEM),
+            pl.BlockSpec((1, 1, slots), filled, memory_space=pltpu.SMEM),
+            pl.BlockSpec((1, 1, LANES), filled, memory_space=pltpu.SMEM),
         ],
         out_specs=(
-            pl.BlockSpec((ROWS_BLK, part_nodes), lambda j: (j, 0)),
-            pl.BlockSpec((ROWS_BLK, 2 * HALO), lambda j: (j, 0)),
-            pl.BlockSpec((ROWS_BLK, 1), lambda j: (j, 0)),
+            pl.BlockSpec((ROWS_BLK, part_nodes), left),
+            pl.BlockSpec((ROWS_BLK, 2 * HALO), left),
+            pl.BlockSpec((ROWS_BLK, 1), left),
         ),
-        scratch_shapes=[pltpu.VMEM((dump + 8, LANES), jnp.float32)],
-        compiler_params=pltpu.CompilerParams(vmem_limit_bytes=40 << 20),
+        scratch_shapes=[pltpu.VMEM((dump + 8, LANES), jnp.float32)] * 4,
+        compiler_params=pltpu.CompilerParams(vmem_limit_bytes=52 << 20),
         cost_estimate=pl.CostEstimate(flops=80_000_000_000, bytes_accessed=40_000_000, transcendentals=0),
         name="edge_counts",
     )(block_count, fast[:, None], slow[:, None], flags[:, None])
@@ -401,8 +435,103 @@
     )(outgoing, local_remain, sums)
 
 
+def forward_kernel(
+    counts_ref, rows_ref, halo_counts_ref, halo_rows_ref, deg_ref, x_ref, w_self_ref, w_neigh_ref, bias_ref, cot_ref,
+    out_ref, grad_ref, halo_ref, dx_ref, weights_ref, total, acc_self, acc_neigh
+):
+    k = pl.program_id(0)
+    nodes, feats = total.shape
+    tile = 256
+
+    def cut(r):
+        return pl.ds(pl.multiple_of(r * tile, tile), tile)
+
+    @pl.when(k == 0)
+    def _():
+        def start(r, carry):
+            total[cut(r), :] = dot(halo_counts_ref[cut(r), :], halo_rows_ref[...])
+            return carry
+
+        lax.fori_loop(0, nodes // tile, start, 0)
+
+    def step(r, carry):
+        total[cut(r), :] += dot(counts_ref[cut(r), :], rows_ref[...])
+        return carry
+
+    lax.fori_loop(0, nodes // tile, step, 0)
+
+    @pl.when(k == pl.num_programs(0) - 1)
+    def _():
+        acc_self[...] = jnp.zeros_like(acc_self)
+        acc_neigh[...] = jnp.zeros_like(acc_neigh)
+
+        def layer(r, bias_sum):
+            rows = cut(r)
+            divisor = jnp.maximum(deg_ref[rows, :], 1.0)
+            x = x_ref[rows, :]
+            neighbour = (total[rows, :] / divisor).astype(jnp.bfloat16)
+            preact = dot(x, w_self_ref[...]) + dot(neighbour, w_neigh_ref[...]) + bias_ref[...]
+            sigma = jax.nn.sigmoid(preact)
+            out_ref[rows, :] = (preact * sigma).astype(jnp.bfloat16)
+            slope = sigma * (1.0 + preact * (1.0 - sigma))
+            dpre = (cot_ref[rows, :].astype(jnp.float32) * slope).astype(jnp.bfloat16)
+            scaled = dot(dpre, w_neigh_ref[...], COLS) / divisor
+            grad_ref[:, rows] = scaled.T.astype(jnp.bfloat16)
+            dx_ref[rows, :] = dot(dpre, w_self_ref[...], COLS)
+            acc_self[...] += dot(x, dpre, ROWS)
+            acc_neigh[...] += dot(neighbour, dpre, ROWS)
+            return bias_sum + jnp.sum(dpre.astype(jnp.float32), axis=0, keepdims=True)
+
+        bias_sum = lax.fori_loop(0, nodes // tile, layer, jnp.zeros((1, feats), jnp.float32))
+        halo_ref[...] = dot(grad_ref[...], halo_counts_ref[...]).T.astype(jnp.bfloat16)
+        doms = weights_ref.shape[0]
+        each = 2 * feats // doms
+        wide = feats // doms
+        spread = jnp.broadcast_to(bias_sum, (8, feats))
+        for c in range(doms):
+            source, at = (acc_self, c * each) if c * each < feats else (acc_neigh, c * each - feats)
+            weights_ref[c, :each, :] = source[at : at + each, :]
+            shift = (feats - c * wide) % feats
+            weights_ref[c, each:, :] = pltpu.roll(spread, shift, 1) if shift else spread
+
+
+def forward(counts, gathered, halo_counts, halo_rows, degree, features, w_self, w_neigh, bias, cotangent, doms):
+    nodes, feats = features.shape
+    steps = counts.shape[1] // nodes
+
+    def whole(array):
+        return pl.BlockSpec(array.shape, lambda k: (0,) * len(array.shape))
+
+    out_shape = (
+        jax.ShapeDtypeStruct((nodes, feats), jnp.bfloat16),
+        jax.ShapeDtypeStruct((feats, nodes), jnp.bfloat16),
+        jax.ShapeDtypeStruct(halo_rows.shape, jnp.bfloat16),
+        jax.ShapeDtypeStruct((nodes, feats), jnp.float32),
+        jax.ShapeDtypeStruct((doms, 2 * feats // doms + 8, feats), jnp.float32),
+    )
+    kept = (halo_counts, halo_rows, degree, features, w_self, w_neigh, bias, cotangent)
+    return pl.pallas_call(
+        forward_kernel,
+        grid=(steps,),
+        out_shape=out_shape,
+        in_specs=[
+            pl.BlockSpec((nodes, nodes), lambda k: (0, k)),
+            pl.BlockSpec((nodes, feats), lambda k: (k, 0)),
+        ]
+        + [whole(array) for array in kept],
+        out_specs=tuple(whole(array) for array in out_shape),
+        scratch_shapes=[
+            pltpu.VMEM((nodes, feats), jnp.float32),
+            pltpu.VMEM((feats, feats), jnp.float32),
+            pltpu.VMEM((feats, feats), jnp.float32),
+        ],
+        compiler_params=pltpu.CompilerParams(vmem_limit_bytes=40 << 20),
+        name="forward_layer",
+    )(counts, gathered, *kept)
+
+
 def reduce_kernel(
-    counts_ref, grad_ref, weights_ref, out_ref, sums_ref, load, part, mid, fin, half_sum, mid2, fin2, sems_load, s_out, s_mid, s_fin, t_out, t_mid, t_fin, weights_in, w_out, w_in
+    counts_ref, grad_ref, weights_ref, halo_ref, dx_ref, out_ref, sums_ref, load, part, mid, fin, half_sum, mid2, fin2, sems_load, s_out, s_mid, s_fin, t_out, t_mid, t_fin, weights_in, w_out, w_in, halo_in, own, h_out, h_in
 ):
     side = 4
     nodes = grad_ref.shape[1]
@@ -450,8 +579,22 @@
             device_id_type=MESH,
         )
 
+    halo = halo_in.shape[1]
+
+    def to_side(side_index):
+        return pltpu.make_async_remote_copy(
+            src_ref=halo_ref.at[pl.ds(side_index * halo, halo)],
+            dst_ref=halo_in.at[side_index],
+            send_sem=h_out.at[side_index],
+            recv_sem=h_in.at[side_index],
+            device_id=(lax.rem(dom + (doms - 1 if side_index == 0 else 1), doms), blk),
+            device_id_type=MESH,
+        )
+
     for k in range(1, doms):
         to_dom(k).start()
+    to_side(0).start()
+    to_side(1).start()
 
     def remote(src, dst, half, first, second, send_sem, recv_sem):
         return pltpu.make_async_remote_copy(
@@ -552,15 +695,22 @@
             half_sum[half, second - 1, :, cut(relayed)] = both.astype(jnp.bfloat16)
             to_fin2(half, second, relayed).start()
     for half in range(2):
-        rows = pl.ds(half * feats, feats)
-        out_ref[rows, :] = summed(half, 0)
+        own[half * feats : (half + 1) * feats, :] = summed(half, 0)
+    to_side(0).wait_recv()
+    to_side(1).wait_recv()
     for half in range(2):
-        rows = pl.ds(half * feats, feats)
+        rows = slice(half * feats, (half + 1) * feats)
         for piece in range(2):
             to_fin2(half, 1, piece).wait_recv()
             to_fin2(half, 3, piece).wait_recv()
-            total = out_ref[rows, cut(piece)] + fin2[half, 0, piece].astype(jnp.float32)
-            out_ref[rows, cut(piece)] = total + fin2[half, 1, piece].astype(jnp.float32)
+            total = own[rows, piece * span : (piece + 1) * span] + fin2[half, 0, piece].astype(jnp.float32)
+            total = (total + fin2[half, 1, piece].astype(jnp.float32)).T
+            near = slice(piece * span, (piece + 1) * span)
+            out_ref[near, rows] = dx_ref[near, rows] + total
+            edge = slice(0, halo) if piece == 0 else slice(nodes - halo, nodes)
+            out_ref[edge, rows] += halo_in[1 - piece, :, rows].astype(jnp.float32)
+    to_side(0).wait_send()
+    to_side(1).wait_send()
     sums = weights_ref[dom]
     for k in range(1, doms):
         to_dom(k).wait_recv()
@@ -579,7 +729,7 @@
             to_fin2(half, 3, piece).wait_send()
 
 
-def reduce_sources(counts, grad, weights):
+def reduce_sources(counts, grad, weights, halo, dx):
     feats, nodes = grad.shape
     half = feats // 2
     kind = jnp.bfloat16
@@ -588,10 +738,10 @@
     return pl.pallas_call(
         reduce_kernel,
         out_shape=(
-            jax.ShapeDtypeStruct((feats, nodes), jnp.float32),
+            jax.ShapeDtypeStruct((nodes, feats), jnp.float32),
             jax.ShapeDtypeStruct(weights.shape[1:], jnp.float32),
         ),
-        in_specs=[pl.BlockSpec(memory_space=pl.ANY), vmem, vmem],
+        in_specs=[pl.BlockSpec(memory_space=pl.ANY), vmem, vmem, vmem, vmem],
         out_specs=(vmem, vmem),
         scratch_shapes=[
             pltpu.VMEM((3, nodes, nodes), kind),
@@ -611,12 +761,16 @@
             pltpu.VMEM(weights.shape, jnp.float32),
             dma((weights.shape[0],)),
             dma((weights.shape[0],)),
+            pltpu.VMEM((2, halo.shape[0] // 2, feats), kind),
+            pltpu.VMEM((feats, nodes), jnp.float32),
+            dma((2,)),
+            dma((2,)),
         ],
         compiler_params=pltpu.CompilerParams(
-            collective_id=3, has_side_effects=True, vmem_limit_bytes=44 << 20
+            collective_id=3, has_side_effects=True, vmem_limit_bytes=48 << 20
         ),
         name="reduce_sources",
-    )(counts, grad, weights)
+    )(counts, grad, weights, halo, dx)
 
 
 def shifted(block, axis, distance):
@@ -678,38 +832,11 @@
     halo_rows = jnp.concatenate([low_rows, high_rows], axis=0)
 
     counts, halo_counts, degree = build_counts(edge_src, edge_dst, block_count, part_nodes)
-    divisor = jnp.maximum(degree, 1.0)
-    agg_sum = dot(counts, part_gathered) + dot(halo_counts, halo_rows)
-    neighbour = (agg_sum / divisor).astype(jnp.bfloat16)
-    preact = dot(features, w_self) + dot(neighbour, w_neigh) + bias
-    sigma = jax.nn.sigmoid(preact)
-    out = (preact * sigma).astype(jnp.bfloat16)
-    dpre = (cotangent.astype(jnp.float32) * sigma * (1.0 + preact * (1.0 - sigma))).astype(
-        jnp.bfloat16
+    doms = lax.axis_size("dom")
+    out, grad_t, halo_grads, dx_self, weights = forward(
+        counts, part_gathered, halo_counts, halo_rows, degree, features, w_self, w_neigh, bias[None], cotangent, doms
     )
-    dagg_scaled = (dot(dpre, w_neigh, COLS) / divisor).astype(jnp.bfloat16)
-    halo_grads = dot(halo_counts, dagg_scaled, ROWS).astype(jnp.bfloat16)
-    tail_grad = shifted(halo_grads[:HALO], "dom", -1)
-    head_grad = shifted(halo_grads[HALO:], "dom", 1)
-    local_self = dot(features, dpre, ROWS)
-    local_neigh = dot(neighbour, dpre, ROWS)
-    local_bias = jnp.sum(dpre.astype(jnp.float32), axis=0)
-    doms = lax.axis_size("dom")
-    bias_rows = jnp.pad(local_bias.reshape(doms, 1, -1), ((0, 0), (0, 7), (0, feature_dim - feature_dim // doms)))
-    weights = jnp.concatenate([local_self, local_neigh], axis=0).reshape(doms, -1, feature_dim)
-    weights = jnp.concatenate([weights, bias_rows], axis=1)
-    own_grads, weight_sums = reduce_sources(counts, dagg_scaled.T, weights)
-    own_grads = own_grads.T
-    dx_self = dot(dpre, w_self, COLS)
-    edges = jnp.concatenate(
-        [
-            head_grad.astype(jnp.float32),
-            jnp.zeros((nodes_dev - 2 * HALO, feature_dim), jnp.float32),
-            tail_grad.astype(jnp.float32),
-        ],
-        axis=0,
-    )
-    grad_x = dx_self + own_grads + edges
+    grad_x, weight_sums = reduce_sources(counts, grad_t, weights, halo_grads, dx_self)
     outgoing = dot(slot_hot, (grad_x * remain_rows).astype(jnp.bfloat16), ROWS).astype(jnp.bfloat16)
     local_remain = dot(rem_hot, (grad_x * quot_rows).astype(jnp.bfloat16), ROWS)
 

time: 291 us -> 277 us (0.952)
  matrix products: 35.3 us -> 14.2 us
  starting transfers between devices: 18 us -> 2.02 us
  Pallas kernels: 211 us -> 226 us
  waiting for transfers between devices: 0.1 us -> 3.68 us
    dot_general x16 -> x7, matrix products: 35.3 us -> 14.2 us  [dot(): return lax.dot_general(a, b, dims, preferred_element_type=jnp.float32)]
    pallas_call x2 -> x3, Pallas kernels: 132 us -> 149 us  [the longest x1 61.4 us: reduce_sources(): pl.pallas_call(reduce_kernel, out_shape=(jax.ShapeDtypeStruct((nodes, fea...]
    ppermute x4 -> x2, starting transfers between devices: 17.9 us -> 1.98 us  [shifted(): return lax.ppermute(block, axis, route)]
    unnamed x35 -> x39, local copies, waits for them, and re-layouts: 2.1 us -> 8.21 us
    dot_general x2 -> x0, local copies, waits for them, and re-layouts: 3.84 us -> none  [dot(): return lax.dot_general(a, b, dims, preferred_element_type=jnp.float32)]
    all_gather x1, waiting for transfers between devices: 0.07 us -> 3.66 us  [per_device(): part_gathered = lax.all_gather(features, 'blk', axis=0, tiled=True)]
    pallas_call x1, Pallas kernels: 43.2 us -> 39.9 us  [spread_grads(): pl.pallas_call(functools.partial(spread_kernel, devices, rem_scale, scale...]
  transfers between devices with their start and end apart: 5 -> 3, of which waited for: 1 -> 1; matrix products, arithmetic and copies ran while one was open for 8% -> 1% of each run, Pallas kernels for 46% -> 22%
where the time goes in v4:
time: 277 us; the launch traced here: 274 us
  Pallas kernels  226 us (82%)
  between operations  14.3 us (5%)
  matrix products  14.2 us (5%)
  local copies, waits for them, and re-layouts  11.7 us (4%)
  waiting for transfers between devices  3.68 us (1%)
    pallas_call x1, Pallas kernels, reduce_sources(): pl.pallas_call(reduce_kernel, out_shape=(jax.ShapeDtypeStruct((nodes, fea...  61.4 us
    pallas_call x1, Pallas kernels, build_counts(): pl.pallas_call(functools.partial(count_kernel, dump), grid=(blocks + 1,),...  59 us
    pallas_call x1, Pallas kernels, spread_grads(): pl.pallas_call(functools.partial(spread_kernel, devices, rem_scale, scale...  39.9 us
    pallas_call x1, Pallas kernels, fetch_rows(): pl.pallas_call(functools.partial(fetch_kernel, devices), out_shape=(jax.S...  35.7 us
    pallas_call x1, Pallas kernels, forward(): pl.pallas_call(forward_kernel, grid=(steps,), out_shape=out_shape, in_spe...  29.1 us
    dot_general x7, matrix products, dot(): return lax.dot_general(a, b, dims, preferred_element_type=jnp.float32)  14.2 us
    unnamed x39, local copies, waits for them, and re-layouts  8.21 us
  transfers between devices with their start and end apart: 3, of which 1 were waited for; matrix products, arithmetic and copies ran while one was open for 1% of the time, Pallas kernels for 22%

profile of v4, /device:TPU:1, one launch (start us, length us, event | category | flops | bytes accessed | tf_op | source)
XLA Modules:
  0.0 274.4 jit_solution(13184641040330135089)
XLA Ops:
  7.2 1.4 fusion.14
  10.1 0.9 fusion.15
  11.0 1.5 fusion.5
  12.5 35.7 %fetch_rows.1 = (bf16[2048,256]{1,0:T(8,128)(2,1)S(1)}, s32[2048,1]{1,0:T(8,128)S(1)}) custom-call(f32[128,1,128]{2,1,0:T(1,128)S(1)} %bitcast.11, bf16[1024,256]{1,0:T(8,128)(2,1)S(1)} %copy-done.6), custom_call_target="tpu_custom_call" | custom-call | tf_op jit(solution)/shard_map/fetch_rows/pallas_call | solution.py:299
  48.3 2.7 multiply_convert_fusion.2
  51.1 1.6 fusion.26
  52.7 2.0 collective-permute-start
  54.8 0.8 edge_prep.1
  55.9 59.0 %edge_counts.1 = (bf16[1024,16384]{1,0:T(8,128)(2,1)}, bf16[1024,512]{1,0:T(8,128)(2,1)S(1)}, f32[1024,1]{1,0:T(8,128)S(1)}) custom-call(s32[8]{0:T(128)S(1)} %copy-done.12, s32[8,1,6144]{2,1,0:T(1,128)S(1)} %broadcast_in_dim.13.fast_ref, s32[8,1,6144]{2,1,0:T(1,128)S(1)} %broadcast_in_dim.14.slow_ref, s32[8,1,128]{2,1,0:T(1,128)S(1)} %bitcast.15), custom_call_target="tpu_custom_call" | custom-call | flops 80000000000 | bytes 40000000 | tf_op jit(solution)/shard_map/edge_counts/pallas_call | solution.py:163
  114.8 0.8 copy-done.4
  116.0 0.9 pad_maximum_fusion.halo_rows_ref
  116.9 3.7 %all-gather.2.cloned.1.call-done.rows_ref = bf16[16384,256]{1,0:T(8,128)(2,1)} async-done(((bf16[1024,256]{1,0:T(8,128)(2,1)}), bf16[16384,256]{1,0:T(8,128)(2,1)}) %all-gather.2.cloned.1.call-update) | async-done | bytes 8388624 | tf_op jit(solution)/shard_map/all_gather | solution.py:829
  120.6 3.4 %copy-done.1 = bf16[16384,256]{1,0:T(8,128)(2,1)S(1)} copy-done((bf16[16384,256]{1,0:T(8,128)(2,1)S(1)}, bf16[16384,256]{1,0:T(8,128)(2,1)}, u32[]{:S(2)}) %copy-start.1) | copy-done | bytes 8388632
  124.0 1.0 copy-done.3
  125.0 1.0 copy-done.5
  126.1 0.9 copy-done.10
  127.0 29.1 %forward_layer.1 = (bf16[1024,256]{1,0:T(8,128)(2,1)}, bf16[256,1024]{1,0:T(8,128)(2,1)S(1)}, bf16[512,256]{1,0:T(8,128)(2,1)S(1)}, f32[1024,256]{1,0:T(8,128)S(1)}, f32[8,72,256]{2,1,0:T(8,128)S(1)}) custom-call(bf16[1024,16384]{1,0:T(8,128)(2,1)} %get-tuple-element.28.counts_ref, bf16[16384,256]{1,0:T(8,128)(2,1)S(1)} %copy-done.1, ...), custom_call_target="tpu_custom_call" | custom-call | tf_op jit(solution)/shard_map/forward_layer/pallas_call | solution.py:513
  156.1 61.4 %reduce_sources.1 = (f32[1024,256]{1,0:T(8,128)S(1)}, f32[72,256]{1,0:T(8,128)S(1)}) custom-call(bf16[1024,16384]{1,0:T(8,128)(2,1)} %get-tuple-element.28.counts_ref, bf16[256,1024]{1,0:T(8,128)(2,1)S(1)} %get-tuple-element.34.grad_ref, f32[8,72,256]{2,1,0:T(8,128)S(1)} %get-tuple-element.35.weights_ref, bf16[512,256]{1,0:T(8,128)(2,1)S(1)} %get-tuple-element.36.halo_ref, ...), custom_call_target="tpu_custom_call" | custom-call | tf_op jit(solution)/shard_map/reduce_sources/pallas_call | solution.py:738
  217.5 2.6 fusion.9.grads_ref
  220.1 1.5 fusion.12.rem_ref
  221.5 39.9 %spread_grads.1 = (bf16[2048,256]{1,0:T(8,128)(2,1)S(1)}, f32[1024,256]{1,0:T(8,128)S(1)}, f32[512,256]{1,0:T(8,128)S(1)}, f32[8,128]{1,0:T(8,128)S(1)}) custom-call(bf16[2048,256]{1,0:T(8,128)(2,1)S(1)} %fusion.9.grads_ref, bf16[1024,256]{1,0:T(8,128)(2,1)S(1)} %fusion.12.rem_ref, f32[72,256]{1,0:T(8,128)S(1)} %get-tuple-element.39.sums_ref), custom_call_target="tpu_custom_call" | custom-call | tf_op jit(solution)/shard_map/spread_grads/pallas_call | solution.py:413
  262.1 0.8 fusion.25
  262.9 3.7 %fusion.2 = f32[1024,256]{1,0:T(8,128)} fusion(bf16[2048,256]{1,0:T(8,128)(2,1)S(1)} %get-tuple-element.40, s32[2048]{0:T(1024)S(1)} %reduce), kind=kOutput, calls=%fused_computation.4 | convolution fusion | flops 1075838976 | bytes 2105344 | tf_op jit(solution)/shard_map/dot_general | solution.py:787
  266.6 1.0 copy.26
  (48 shorter events, 2.9 us)
Async XLA Ops:
  7.2 3.8 %copy-start = (bf16[1024,256]{1,0:T(8,128)(2,1)S(1)}, bf16[1024,256]{1,0:T(8,128)(2,1)}, u32[]{:S(2)}) copy-start(bf16[1024,256]{1,0:T(8,128)(2,1)} %param.16) | copy-start | bytes 1572868
  7.2 5.4 %copy-start.6 = (bf16[1024,256]{1,0:T(8,128)(2,1)S(1)}, bf16[1024,256]{1,0:T(8,128)(2,1)}, u32[]{:S(2)}) copy-start(bf16[1024,256]{1,0:T(8,128)(2,1)} %table_ref.1) | copy-start | bytes 1572868
  7.2 113.4 %all-gather.2.cloned.1.call-start = ((), (), s32[]{:S(2)}) async-start(), calls=%async_computation | async-start | bytes 8912896 | tf_op jit(solution)/shard_map/all_gather | solution.py:829
  9.4 41.7 %copy-start.13 = (s32[1024,1]{0,1:T(1,128)}, s32[1024,1]{0,1:T(1,128)S(1)}, u32[]{:S(2)}) copy-start(s32[1024,1]{0,1:T(1,128)S(1)} %multiply_add_fusion) | copy-start | bytes 12292
  12.5 38.5 %copy-start.17 = (f32[1024,256]{1,0:T(8,128)}, f32[1024,256]{1,0:T(8,128)S(1)}, u32[]{:S(2)}) copy-start(f32[1024,256]{1,0:T(8,128)S(1)} %fusion.5) | copy-start | bytes 3145732
  48.3 6.4 %copy-start.12 = (s32[8]{0:T(128)S(1)}, s32[8]{0:T(128)}, u32[]{:S(2)}) copy-start(s32[8]{0:T(128)} %count_ref.1) | copy-start | bytes 100
  48.3 6.5 %copy-start.7 = (s32[8,6144]{1,0:T(8,128)S(1)}, s32[8,6144]{1,0:T(8,128)}, u32[]{:S(2)}) copy-start(s32[8,6144]{1,0:T(8,128)} %src_ref.1) | copy-start | bytes 589828
  48.3 6.4 %copy-start.8 = (s32[8,6144]{1,0:T(8,128)S(1)}, s32[8,6144]{1,0:T(8,128)}, u32[]{:S(2)}) copy-start(s32[8,6144]{1,0:T(8,128)} %dst_ref.1) | copy-start | bytes 589828
  52.7 63.3 %collective-permute-start = (bf16[256,256]{1,0:T(8,128)(2,1)}, bf16[256,256]{1,0:T(8,128)(2,1)S(1)}, u32[]{:S(2)}, u32[]{:S(2)}) collective-permute-start(bf16[256,256]{1,0:T(8,128)(2,1)} %get-tuple-element.46), channel_id=1, source_target_pairs={{112,0},{0,16},{16,32},{32,48},{48,64},{64,80},{80,96},{96,112},{1... | collective-permute-start | bytes 393224 | tf_op jit(solution)/shard_map/ppermute | solution.py:779
  54.7 61.3 %collective-permute-start.1 = (bf16[256,256]{1,0:T(8,128)(2,1)S(1)}, bf16[256,256]{1,0:T(8,128)(2,1)}, u32[]{:S(2)}, u32[]{:S(2)}) collective-permute-start(bf16[256,256]{1,0:T(8,128)(2,1)S(1)} %get-tuple-element.47), channel_id=1, source_target_pairs={{16,0},{32,16},{48,32},{64,48},{80,64},{96,80},{112,96},{0,112},{1... | collective-permute-start | bytes 393224 | tf_op jit(solution)/shard_map/ppermute | solution.py:779
  55.8 64.8 %copy-start.2 = (bf16[1024,256]{1,0:T(8,128)(2,1)S(1)}, bf16[1024,256]{1,0:T(8,128)(2,1)}, u32[]{:S(2)}) copy-start(bf16[1024,256]{1,0:T(8,128)(2,1)} %get-tuple-element.52.x_ref) | copy-start | bytes 1572868
  55.8 64.7 %copy-start.9 = (bf16[256,256]{1,0:T(8,128)(2,1)S(1)}, bf16[256,256]{1,0:T(8,128)(2,1)}, u32[]{:S(2)}) copy-start(bf16[256,256]{1,0:T(8,128)(2,1)} %w_self_ref.1) | copy-start | bytes 393220
  55.9 64.7 %copy-start.11 = (f32[256]{0:T(256)S(1)}, f32[256]{0:T(256)}, u32[]{:S(2)}) copy-start(f32[256]{0:T(256)} %param.22) | copy-start | bytes 3076
  114.8 0.8 copy-start.4
  120.6 3.4 %copy-start.1 = (bf16[16384,256]{1,0:T(8,128)(2,1)S(1)}, bf16[16384,256]{1,0:T(8,128)(2,1)}, u32[]{:S(2)}) copy-start(bf16[16384,256]{1,0:T(8,128)(2,1)} %all-gather.2.cloned.1.call-done.rows_ref) | copy-start | bytes 25165828
  124.0 1.0 copy-start.3
  125.0 1.0 copy-start.5
  126.1 0.9 copy-start.10
  156.1 61.4 %copy-start.14 = (s32[1024,1]{0,1:T(1,128)S(1)}, s32[1024,1]{0,1:T(1,128)}, u32[]{:S(2)}) copy-start(s32[1024,1]{0,1:T(1,128)} %copy-done.13) | copy-start | bytes 12292
  156.1 61.4 %copy-start.18 = (f32[1024,256]{1,0:T(8,128)S(1)}, f32[1024,256]{1,0:T(8,128)}, u32[]{:S(2)}) copy-start(f32[1024,256]{1,0:T(8,128)} %copy-done.17) | copy-start | bytes 3145732
  217.5 2.6 copy-start.15
  217.5 2.6 copy-start.16
Sparse Core Ops, SparseCore 0:
  51.2 69.3 all-gather.1

commit v5 on v4

--- a/solution.py
+++ b/solution.py
@@ -191,17 +191,35 @@
     return lax.axis_index("dom") * blk + lax.axis_index("blk")
 
 
-def meet_all(devices):
-    barrier = pltpu.get_barrier_semaphore()
+def greet_all(devices):
     me = ring_place()
 
     def greet(k, carry):
         other = lax.rem(me + k, devices)
+        barrier = pltpu.get_barrier_semaphore()
         pl.semaphore_signal(barrier, inc=1, device_id=coords(other), device_id_type=MESH)
         return carry
 
     lax.fori_loop(1, devices, greet, 0)
-    pl.semaphore_wait(barrier, devices - 1)
+
+
+def meet_all(devices):
+    pl.semaphore_wait(pltpu.get_barrier_semaphore(), devices - 1)
+
+
+def as_row(column):
+    wide = jnp.broadcast_to(column.astype(jnp.float32), (column.shape[0], LANES))
+    return wide.T[0:1].astype(jnp.int32)
+
+
+def pick(column, first, size):
+    lane = lax.broadcasted_iota(jnp.int32, (column.shape[0], size), 1) + first
+    return (lane == column).astype(jnp.bfloat16)
+
+
+def pick_rows(row, first, size):
+    line = lax.broadcasted_iota(jnp.int32, (size, row.shape[1]), 0) + first
+    return (line == row).astype(jnp.bfloat16)
 
 
 def coords(device):
@@ -224,43 +242,69 @@
     pltpu.make_async_copy(ref, ref, sem).wait()
 
 
-def fetch_kernel(devices, ids_ref, table_ref, rows_ref, asked_ref, ids_in, served, rows_in, sems):
-    slot_cap = served.shape[0] // devices
-    slots = served.shape[0]
+def fetch_kernel(
+    devices, owner_ref, qrow_ref, rem_ref, table_ref, remainder_ref, x_ref, qv_ref, rv_ref, asked_ref, slot_ref,
+    ids_out, ids_in, served, rows_in, slot_col, slot_hot, sems
+):
+    slots, width = served.shape
+    slot_cap = slots // devices
+    nodes = owner_ref.shape[0]
     me = ring_place()
+    tile = 256
+    greet_all(devices)
+
+    def cut(r):
+        return pl.ds(pl.multiple_of(r * tile, tile), tile)
+
+    owner_hot = pick(owner_ref[...], 0, devices)
+    lane = lax.broadcasted_iota(jnp.int32, (tile, devices), 1)
+    wish = jnp.zeros((devices, devices), jnp.float32)
+    for r in range(nodes // tile):
+        rows = slice(r * tile, (r + 1) * tile)
+        line = lax.broadcasted_iota(jnp.int32, (tile, nodes), 0) + r * tile
+        before = (line > lax.broadcasted_iota(jnp.int32, (tile, nodes), 1)).astype(jnp.bfloat16)
+        mine = owner_hot[rows]
+        rank = jnp.sum(dot(before, owner_hot) * mine.astype(jnp.float32), axis=1, keepdims=True).astype(jnp.int32)
+        slot_col[rows, :] = owner_ref[rows, :] * slot_cap + rank
+        qrow = qrow_ref[rows, :]
+        parts = jnp.where(lane == rank, qrow >> 5, 0) + jnp.where(lane == rank + slot_cap, qrow & 31, 0)
+        wish = wish + dot(mine, parts.astype(jnp.float32).astype(jnp.bfloat16), ROWS)
+    ids_out[:, 0, :] = wish
     meet_all(devices)
 
     def ask(k, carry):
         other = lax.rem(me + k, devices)
-        send(ids_ref.at[other], ids_in.at[me], other, sems.at[0], sems.at[1])
+        send(ids_out.at[other], ids_in.at[me], other, sems.at[0], sems.at[1])
         return carry
 
     lax.fori_loop(1, devices, ask, 0)
-    own = pltpu.make_async_copy(ids_ref.at[me], ids_in.at[me], sems.at[2])
+
+    def remain(r, carry):
+        rows = cut(r)
+        rv_ref[rows, :] = dot(pick(rem_ref[rows, :], 0, remainder_ref.shape[0]), remainder_ref[...]).astype(jnp.bfloat16)
+        return carry
+
+    lax.fori_loop(0, nodes // tile, remain, 0)
+    slot_ref[...] = as_row(slot_col[...])
+    own = pltpu.make_async_copy(ids_out.at[me], ids_in.at[me], sems.at[2])
     own.start()
     own.wait()
     drain(ids_in.at[pl.ds(0, devices - 1)], sems.at[1])
     ids = ids_in[:, 0, :].astype(jnp.bfloat16)
     step = 16
     part = step * slot_cap
-    lanes = ids.shape[1]
-    lane = lax.broadcasted_iota(jnp.int32, (part, lanes), 1)
-    slot = lax.broadcasted_iota(jnp.int32, (part, lanes), 0)
-    rank = lax.rem(slot, slot_cap)
-    weight = jnp.where(lane == rank, 32.0, 0.0) + jnp.where(lane == rank + slot_cap, 1.0, 0.0)
-    column = lax.broadcasted_iota(jnp.int32, (part, table_ref.shape[0]), 1)
+    slot = lax.broadcasted_iota(jnp.int32, (part, devices), 0)
+    place = lax.broadcasted_iota(jnp.int32, (part, devices), 1)
+    rank_of = lax.rem(slot, slot_cap)
+    weight = jnp.where(place == rank_of, 32.0, 0.0) + jnp.where(place == rank_of + slot_cap, 1.0, 0.0)
 
     def serve(c, carry):
         turn = lax.rem(c + me // step, devices // step)
-        pick = (lane - turn * step == slot // slot_cap).astype(jnp.bfloat16)
-        spread = jnp.dot(pick, ids, preferred_element_type=jnp.float32)
-        asked = jnp.sum(spread * weight, axis=1, keepdims=True).astype(jnp.int32)
+        whose = (place - turn * step == slot // slot_cap).astype(jnp.bfloat16)
+        asked = jnp.sum(dot(whose, ids) * weight, axis=1, keepdims=True).astype(jnp.int32)
         at = pl.multiple_of(turn * part, part)
-        asked_ref[pl.ds(at, part), :] = asked
-        pick_row = (column == asked).astype(jnp.bfloat16)
-        served[pl.ds(at, part), :] = jnp.dot(
-            pick_row, table_ref[...], preferred_element_type=jnp.float32
-        ).astype(jnp.bfloat16)
+        asked_ref[:, pl.ds(at, part)] = as_row(asked)
+        served[pl.ds(at, part), :] = dot(pick(asked, 0, table_ref.shape[0]), table_ref[...]).astype(jnp.bfloat16)
 
         def back(i, inner):
             other = turn * step + lax.rem(me + i, step)
@@ -284,42 +328,63 @@
     mine = pl.ds(pl.multiple_of(me * slot_cap, slot_cap), slot_cap)
     own_rows = pltpu.make_async_copy(served.at[mine], rows_in.at[mine], sems.at[2])
     own_rows.start()
+
+    def prepare(r, carry):
+        slot_hot[cut(r), :] = pick(slot_col[cut(r), :], 0, slots)
+        return carry
+
+    lax.fori_loop(0, nodes // tile, prepare, 0)
     own_rows.wait()
     drain(rows_in.at[pl.ds(0, slots - slot_cap)], sems.at[4])
-    rows_ref[...] = rows_in[...]
+
+    def finish(r, carry):
+        rows = cut(r)
+        qv = dot(slot_hot[rows, :], rows_in[...])
+        qv_ref[rows, :] = qv.astype(jnp.bfloat16)
+        x_ref[rows, :] = (qv * rv_ref[rows, :].astype(jnp.float32)).astype(jnp.bfloat16)
+        return carry
+
+    lax.fori_loop(0, nodes // tile, finish, 0)
     drain(ids_in.at[pl.ds(0, devices - 1)], sems.at[0])
     drain(rows_in.at[pl.ds(0, slots - slot_cap)], sems.at[3])
 
 
-def fetch_rows(ids, quotient, slot_cap):
-    devices, _, lanes = ids.shape
-    slots = devices * slot_cap
+def fetch_rows(owner, qrow, rem, quotient, remainder, devices):
+    nodes = owner.shape[0]
+    slots = 2 * nodes
     width = quotient.shape[1]
     vmem = pl.BlockSpec(memory_space=pltpu.VMEM)
+    rows = jax.ShapeDtypeStruct((nodes, width), jnp.bfloat16)
     return pl.pallas_call(
         functools.partial(fetch_kernel, devices),
         out_shape=(
-            jax.ShapeDtypeStruct((slots, width), jnp.bfloat16),
-            jax.ShapeDtypeStruct((slots, 1), jnp.int32),
+            rows,
+            rows,
+            rows,
+            jax.ShapeDtypeStruct((1, slots), jnp.int32),
+            jax.ShapeDtypeStruct((1, nodes), jnp.int32),
         ),
-        in_specs=[vmem, vmem],
-        out_specs=(vmem, vmem),
+        in_specs=[vmem] * 5,
+        out_specs=(vmem,) * 5,
         scratch_shapes=[
-            pltpu.VMEM((devices, 1, lanes), jnp.float32),
+            pltpu.VMEM((devices, 1, devices), jnp.float32),
+            pltpu.VMEM((devices, 1, devices), jnp.float32),
             pltpu.VMEM((slots, width), jnp.bfloat16),
             pltpu.VMEM((slots, width), jnp.bfloat16),
+            pltpu.VMEM((nodes, 1), jnp.int32),
+            pltpu.VMEM((nodes, slots), jnp.bfloat16),
             pltpu.SemaphoreType.DMA((5,)),
         ],
         compiler_params=pltpu.CompilerParams(
-            collective_id=1, has_side_effects=True, vmem_limit_bytes=32 << 20
+            collective_id=1, has_side_effects=True, vmem_limit_bytes=40 << 20
         ),
         name="fetch_rows",
-    )(ids, quotient)
+    )(owner, qrow, rem, quotient, remainder)
 
 
 def spread_kernel(
-    devices, rem_scale, scale, grads_ref, rem_ref, sums_ref, back_ref, total_ref, weight_ref, bias_ref,
-    grads_in, rem_in, sums_in, piece, whole, sems
+    devices, rem_scale, scale, grad_ref, qv_ref, rv_ref, slot_ref, node_rem_ref, asked_ref, sums_ref,
+    quot_ref, total_ref, weight_ref, bias_ref, grads_ref, rem_ref, by_rv, grads_in, rem_in, sums_in, piece, whole, sems
 ):
     slot_cap = grads_ref.shape[0] // devices
     slots = grads_ref.shape[0]
@@ -327,9 +392,23 @@
     across = rem_ref.shape[1] // wide
     peers = sums_in.shape[0]
     high = sums_ref.shape[0] - 8
+    size = 256
     me = ring_place()
     dom = lax.axis_index("dom")
     blk = lax.axis_index("blk")
+    greet_all(devices)
+
+    def cut(r):
+        return pl.ds(pl.multiple_of(r * size, size), size)
+
+    by_rv[...] = (grad_ref[...] * qv_ref[...].astype(jnp.float32)).astype(jnp.bfloat16)
+
+    def remain(r, carry):
+        rem_ref[cut(r), :] = dot(pick_rows(node_rem_ref[...], r * size, size), by_rv[...]).astype(jnp.bfloat16)
+        return carry
+
+    lax.fori_loop(0, rem_ref.shape[0] // size, remain, 0)
+    by_rv[...] = (grad_ref[...] * rv_ref[...].astype(jnp.float32)).astype(jnp.bfloat16)
     meet_all(devices)
 
     def tile(device):
@@ -355,9 +434,22 @@
         send(sums_ref.at[pl.ds(high, 8), pl.ds(0, wide)], sums_in.at[blk, pl.ds(8, 8), :], to, sems.at[7], sems.at[8])
         return carry
 
-    def send_grads(k, carry):
-        other = lax.rem(me + k, devices)
-        send(grads_ref.at[slot(other)], grads_in.at[slot(me)], other, sems.at[2], sems.at[3])
+    step = size // slot_cap
+
+    def send_grads(c, carry):
+        turn = lax.rem(c + me // step, devices // step)
+        grads_ref[cut(turn), :] = dot(pick_rows(slot_ref[...], turn * size, size), by_rv[...]).astype(jnp.bfloat16)
+
+        def one(i, inner):
+            other = turn * step + lax.rem(me + i, step)
+
+            @pl.when(other != me)
+            def _():
+                send(grads_ref.at[slot(other)], grads_in.at[slot(me)], other, sems.at[2], sems.at[3])
+
+            return inner
+
+        lax.fori_loop(0, step, one, 0)
         return carry
 
     def send_total(k, carry):
@@ -372,7 +464,7 @@
 
     lax.fori_loop(1, peers, send_sums, 0)
     lax.fori_loop(1, devices, send_rem, 0)
-    lax.fori_loop(1, devices, send_grads, 0)
+    lax.fori_loop(0, devices // step, send_grads, 0)
     keep(rem_ref.at[tile(me)], rem_in.at[me])
     keep(grads_ref.at[slot(me)], grads_in.at[slot(me)])
     keep(sums_ref.at[share(blk)], sums_in.at[blk, pl.ds(0, 8), :])
@@ -384,7 +476,12 @@
     lax.fori_loop(1, devices, send_total, 0)
     keep(piece, whole.at[me])
     drain(grads_in.at[pl.ds(0, slots - slot_cap)], sems.at[3])
-    back_ref[...] = grads_in[...]
+
+    def collect(r, carry):
+        quot_ref[cut(r), :] = dot(pick_rows(asked_ref[...], r * size, size), grads_in[...])
+        return carry
+
+    lax.fori_loop(0, quot_ref.shape[0] // size, collect, 0)
     drain(whole.at[pl.ds(0, devices - 1)], sems.at[5])
 
     def lay(k, carry):
@@ -404,35 +501,41 @@
     drain(sums_in.at[pl.ds(0, peers - 1)], sems.at[7])
 
 
-def spread_grads(outgoing, local_remain, sums, devices, peers, rem_scale, scale):
-    rows, width = local_remain.shape
+def spread_grads(grad, qv, rv, slot_row, rem_row, asked_row, sums, table_rows, rem_rows, peers, rem_scale, scale):
+    nodes, width = grad.shape
+    slots = asked_row.shape[1]
+    doms = lax.axis_size("dom")
+    devices = doms * peers
     wide = LANES
-    tall = rows * width // devices // wide
-    doms = devices // peers
+    tall = rem_rows * width // devices // wide
+    kind = jnp.bfloat16
     vmem = pl.BlockSpec(memory_space=pltpu.VMEM)
     return pl.pallas_call(
         functools.partial(spread_kernel, devices, rem_scale, scale),
         out_shape=(
-            jax.ShapeDtypeStruct(outgoing.shape, jnp.bfloat16),
-            jax.ShapeDtypeStruct((rows, width), jnp.float32),
+            jax.ShapeDtypeStruct((table_rows, width), jnp.float32),
+            jax.ShapeDtypeStruct((rem_rows, width), jnp.float32),
             jax.ShapeDtypeStruct((doms * (sums.shape[0] - 8), width), jnp.float32),
             jax.ShapeDtypeStruct((doms, wide), jnp.float32),
         ),
-        in_specs=[vmem, vmem, vmem],
+        in_specs=[vmem] * 7,
         out_specs=(vmem, vmem, vmem, vmem),
         scratch_shapes=[
-            pltpu.VMEM(outgoing.shape, jnp.bfloat16),
-            pltpu.VMEM((devices, tall, wide), jnp.bfloat16),
+            pltpu.VMEM((slots, width), kind),
+            pltpu.VMEM((rem_rows, width), kind),
+            pltpu.VMEM((nodes, width), kind),
+            pltpu.VMEM((slots, width), kind),
+            pltpu.VMEM((devices, tall, wide), kind),
             pltpu.VMEM((peers, 16, wide), jnp.float32),
-            pltpu.VMEM((tall + 16, wide), jnp.bfloat16),
-            pltpu.VMEM((devices, tall + 16, wide), jnp.bfloat16),
+            pltpu.VMEM((tall + 16, wide), kind),
+            pltpu.VMEM((devices, tall + 16, wide), kind),
             pltpu.SemaphoreType.DMA((9,)),
         ],
         compiler_params=pltpu.CompilerParams(
-            collective_id=2, has_side_effects=True, vmem_limit_bytes=32 << 20
+            collective_id=2, has_side_effects=True, vmem_limit_bytes=40 << 20
         ),
         name="spread_grads",
-    )(outgoing, local_remain, sums)
+    )(grad, qv, rv, slot_row, rem_row, asked_row, sums)
 
 
 def forward_kernel(
@@ -454,11 +557,7 @@
 
         lax.fori_loop(0, nodes // tile, start, 0)
 
-    def step(r, carry):
-        total[cut(r), :] += dot(counts_ref[cut(r), :], rows_ref[...])
-        return carry
-
-    lax.fori_loop(0, nodes // tile, step, 0)
+    total[...] += dot(counts_ref[...], rows_ref[...])
 
     @pl.when(k == pl.num_programs(0) - 1)
     def _():
@@ -497,7 +596,8 @@
 
 def forward(counts, gathered, halo_counts, halo_rows, degree, features, w_self, w_neigh, bias, cotangent, doms):
     nodes, feats = features.shape
-    steps = counts.shape[1] // nodes
+    wide = 4 * nodes
+    steps = counts.shape[1] // wide
 
     def whole(array):
         return pl.BlockSpec(array.shape, lambda k: (0,) * len(array.shape))
@@ -515,8 +615,8 @@
         grid=(steps,),
         out_shape=out_shape,
         in_specs=[
-            pl.BlockSpec((nodes, nodes), lambda k: (0, k)),
-            pl.BlockSpec((nodes, feats), lambda k: (k, 0)),
+            pl.BlockSpec((nodes, wide), lambda k: (0, k)),
+            pl.BlockSpec((wide, feats), lambda k: (k, 0)),
         ]
         + [whole(array) for array in kept],
         out_specs=tuple(whole(array) for array in out_shape),
@@ -525,7 +625,7 @@
             pltpu.VMEM((feats, feats), jnp.float32),
             pltpu.VMEM((feats, feats), jnp.float32),
         ],
-        compiler_params=pltpu.CompilerParams(vmem_limit_bytes=40 << 20),
+        compiler_params=pltpu.CompilerParams(vmem_limit_bytes=58 << 20),
         name="forward_layer",
     )(counts, gathered, *kept)
 
@@ -779,10 +879,6 @@
     return lax.ppermute(block, axis, route)
 
 
-def hot(index, size):
-    return (index[:, None] == jnp.arange(size, dtype=jnp.int32)[None, :]).astype(jnp.bfloat16)
-
-
 def dot(a, b, dims=(((1,), (0,)), ((), ()))):
     return lax.dot_general(a, b, dims, preferred_element_type=jnp.float32)
 
@@ -805,54 +901,37 @@
     feature_dim = quotient.shape[1]
     devices = lax.axis_size("dom") * lax.axis_size("blk")
     part_nodes = nodes_dev * lax.axis_size("blk")
-    slot_cap = 2 * nodes_dev // devices
-    slots = devices * slot_cap
-    owner_dev = node_owner[:, 0]
-    owner_hot = hot(owner_dev, devices)
-    row_ids = jnp.arange(nodes_dev, dtype=jnp.int32)
-    lower_mask = (row_ids[:, None] > row_ids[None, :]).astype(jnp.bfloat16)
-    earlier = dot(lower_mask, owner_hot)
-    slot_rank = jnp.sum(earlier * owner_hot.astype(jnp.float32), axis=1).astype(jnp.int32)
-    slot_index = owner_dev * slot_cap + slot_rank
-    rank_hot = hot(slot_rank, slot_cap)
-    high = (node_qrow >> 5).astype(jnp.bfloat16)[:, None]
-    low = (node_qrow & 31).astype(jnp.bfloat16)[:, None]
-    asked = dot(owner_hot, jnp.concatenate([rank_hot * high, rank_hot * low], axis=1), ROWS)
-    ids = jnp.pad(asked, ((0, 0), (0, LANES - 2 * slot_cap)))[:, None, :]
-    returned, asked_rows = fetch_rows(ids, quotient, slot_cap)
-    asked_hot = hot(asked_rows[:, 0], quotient.shape[0])
-    slot_hot = hot(slot_index, slots)
-    quot_rows = dot(slot_hot, returned)
-    rem_hot = hot(node_rem, remainder.shape[0])
-    remain_rows = dot(rem_hot, remainder)
-    features = (quot_rows * remain_rows).astype(jnp.bfloat16)
+    doms = lax.axis_size("dom")
+    features, quot_rows, remain_rows, asked_row, slot_row = fetch_rows(
+        node_owner, node_qrow[:, None], node_rem[:, None], quotient, remainder, devices
+    )
     part_gathered = lax.all_gather(features, "blk", axis=0, tiled=True)
     low_rows = shifted(features[nodes_dev - HALO :], "dom", 1)
     high_rows = shifted(features[:HALO], "dom", -1)
     halo_rows = jnp.concatenate([low_rows, high_rows], axis=0)
 
     counts, halo_counts, degree = build_counts(edge_src, edge_dst, block_count, part_nodes)
-    doms = lax.axis_size("dom")
     out, grad_t, halo_grads, dx_self, weights = forward(
         counts, part_gathered, halo_counts, halo_rows, degree, features, w_self, w_neigh, bias[None], cotangent, doms
     )
     grad_x, weight_sums = reduce_sources(counts, grad_t, weights, halo_grads, dx_self)
-    outgoing = dot(slot_hot, (grad_x * remain_rows).astype(jnp.bfloat16), ROWS).astype(jnp.bfloat16)
-    local_remain = dot(rem_hot, (grad_x * quot_rows).astype(jnp.bfloat16), ROWS)
-
     nodes_total = nodes_dev * devices
     weight_scale = 1.0 / math.sqrt(nodes_total)
     remain_scale = math.sqrt(remainder.shape[0] / nodes_total)
-    returned_grads, d_remainder, d_weights, d_bias = spread_grads(
-        outgoing,
-        local_remain.astype(jnp.bfloat16),
+    d_quotient, d_remainder, d_weights, d_bias = spread_grads(
+        grad_x,
+        quot_rows,
+        remain_rows,
+        slot_row,
+        node_rem[None],
+        asked_row,
         weight_sums,
-        devices,
+        quotient.shape[0],
+        remainder.shape[0],
         lax.axis_size("blk"),
         remain_scale,
         weight_scale,
     )
-    d_quotient = dot(asked_hot, returned_grads, ROWS)
     d_self, d_neigh = d_weights[:feature_dim], d_weights[feature_dim:]
     d_bias = d_bias[:, : feature_dim // doms].reshape(-1)
     return (out, d_quotient, d_remainder, d_self, d_neigh, d_bias)

time: 277 us -> 263 us (0.949)
  matrix products: 14.2 us -> 0 us
  Pallas kernels: 226 us -> 216 us
  local copies, waits for them, and re-layouts: 11.7 us -> 19.5 us
  waiting for transfers between devices: 3.68 us -> 9.8 us
    dot_general x7 -> x0, matrix products: 14.2 us -> none  [dot(): return lax.dot_general(a, b, dims, preferred_element_type=jnp.float32)]
    pallas_call x1, Pallas kernels: 59 us -> 49.9 us  [build_counts(): pl.pallas_call(functools.partial(count_kernel, dump), grid=(blocks + 1,),...]
    pallas_call x1, Pallas kernels: 29.1 us -> 22.3 us  [forward(): pl.pallas_call(forward_kernel, grid=(steps,), out_shape=out_shape, in_spe...]
    all_gather x1, waiting for transfers between devices: 3.66 us -> 9.78 us  [per_device(): part_gathered = lax.all_gather(features, 'blk', axis=0, tiled=True)]
    unnamed x39 -> x31, local copies, waits for them, and re-layouts: 8.21 us -> 14.3 us
    pallas_call x1, Pallas kernels: 39.9 us -> 45.6 us  [spread_grads(): pl.pallas_call(functools.partial(spread_kernel, devices, rem_scale, scale...]
  transfers between devices with their start and end apart: 3 -> 3, of which waited for: 1 -> 1; matrix products, arithmetic and copies ran while one was open for 1% -> 1% of each run, Pallas kernels for 22% -> 19%
where the time goes in v5:
time: 263 us
  Pallas kernels  216 us (82%)
  local copies, waits for them, and re-layouts  19.5 us (7%)
  between operations  14.2 us (5%)
  waiting for transfers between devices  9.8 us (4%)
    pallas_call x1, Pallas kernels, reduce_sources(): pl.pallas_call(reduce_kernel, out_shape=(jax.ShapeDtypeStruct((nodes, fea...  59.9 us
    pallas_call x1, Pallas kernels, build_counts(): pl.pallas_call(functools.partial(count_kernel, dump), grid=(blocks + 1,),...  49.9 us
    pallas_call x1, Pallas kernels, spread_grads(): pl.pallas_call(functools.partial(spread_kernel, devices, rem_scale, scale...  45.6 us
    pallas_call x1, Pallas kernels, fetch_rows(): pl.pallas_call(functools.partial(fetch_kernel, devices), out_shape=(rows,...  37.9 us
    pallas_call x1, Pallas kernels, forward(): pl.pallas_call(forward_kernel, grid=(steps,), out_shape=out_shape, in_spe...  22.3 us
    unnamed x31, local copies, waits for them, and re-layouts  14.3 us
    all_gather x1, waiting for transfers between devices, per_device(): part_gathered = lax.all_gather(features, 'blk', axis=0, tiled=True)  9.78 us
  transfers between devices with their start and end apart: 3, of which 1 were waited for; matrix products, arithmetic and copies ran while one was open for 1% of the time, Pallas kernels for 19%

profile of v5, /device:TPU:1, one launch (start us, length us, event | category | flops | bytes accessed | tf_op | source)
XLA Modules:
  0.0 262.6 jit_solution(10567120589884240312)
XLA Ops:
  7.2 0.9 copy.21.owner_ref
  8.1 0.9 copy.22.qrow_ref
  9.0 0.9 copy.23.rem_ref
  10.0 1.0 copy-done.5
  11.0 1.0 copy-done.6
  12.0 37.9 %fetch_rows.1 = (bf16[1024,256]{1,0:T(8,128)(2,1)}, bf16[1024,256]{1,0:T(8,128)(2,1)S(1)}, bf16[1024,256]{1,0:T(8,128)(2,1)S(1)}, s32[1,2048]{1,0:T(1,128)S(1)}, s32[1,1024]{1,0:T(1,128)S(1)}) custom-call(s32[1024,1]{1,0:T(8,128)S(1)} %copy.21.owner_ref, s32[1024,1]{1,0:T(8,128)S(1)} %copy.22.qrow_ref, s32[1024,1]{1,0:T(8,128)S(1)} %copy.23.rem_ref, ...), custom_call_target="tpu_custom_call" | custom-call | tf_op jit(solution)/shard_map/fetch_rows/pallas_call | solution.py:358
  50.8 1.0 fusion.1
  51.8 2.0 collective-permute-start
  54.5 0.9 copy-done.10
  55.4 0.9 copy-done.11
  58.0 49.9 %edge_counts.1 = (bf16[1024,16384]{1,0:T(8,128)(2,1)}, bf16[1024,512]{1,0:T(8,128)(2,1)S(1)}, f32[1024,1]{1,0:T(8,128)S(1)}) custom-call(s32[8]{0:T(128)S(1)} %copy-done.13, s32[8,1,6144]{2,1,0:T(1,128)S(1)} %broadcast_in_dim.25.fast_ref, s32[8,1,6144]{2,1,0:T(1,128)S(1)} %broadcast_in_dim.26.slow_ref, s32[8,1,128]{2,1,0:T(1,128)S(1)} %bitcast.11), custom_call_target="tpu_custom_call" | custom-call | flops 80000000000 | bytes 40000000 | tf_op jit(solution)/shard_map/edge_counts/pallas_call | solution.py:163
  108.0 1.0 copy-done
  109.0 0.8 copy-done.3
  110.5 9.8 %all-gather.2.cloned.1.call-done.rows_ref = bf16[16384,256]{1,0:T(8,128)(2,1)} async-done(((bf16[1024,256]{1,0:T(8,128)(2,1)}), bf16[16384,256]{1,0:T(8,128)(2,1)}) %all-gather.2.cloned.1.call-update) | async-done | bytes 8388624 | tf_op jit(solution)/shard_map/all_gather | solution.py:908
  120.3 22.3 %forward_layer.1 = (bf16[1024,256]{1,0:T(8,128)(2,1)}, bf16[256,1024]{1,0:T(8,128)(2,1)}, bf16[512,256]{1,0:T(8,128)(2,1)}, f32[1024,256]{1,0:T(8,128)}, f32[8,72,256]{2,1,0:T(8,128)}) custom-call(bf16[1024,16384]{1,0:T(8,128)(2,1)} %get-tuple-element.31.counts_ref, bf16[16384,256]{1,0:T(8,128)(2,1)} %all-gather.2.cloned.1.call-done.rows_ref, ...), custom_call_target="tpu_custom_call" | custom-call | tf_op jit(solution)/shard_map/forward_layer/pallas_call | solution.py:613
  142.6 1.2 copy-done.1
  143.8 1.1 copy-done.2
  144.9 1.0 copy-done.4
  145.9 0.9 copy-done.9
  146.9 59.9 %reduce_sources.1 = (f32[1024,256]{1,0:T(8,128)S(1)}, f32[72,256]{1,0:T(8,128)S(1)}) custom-call(bf16[1024,16384]{1,0:T(8,128)(2,1)} %get-tuple-element.31.counts_ref, bf16[256,1024]{1,0:T(8,128)(2,1)S(1)} %copy-done.4, f32[8,72,256]{2,1,0:T(8,128)S(1)} %copy-done.2, bf16[512,256]{1,0:T(8,128)(2,1)S(1)} %copy-done.9, f32[1024,256]{1,0:T(8,128)S(1)} %copy-done.1), custom_call_target="tpu_custom_call" | custom-call | tf_op jit(solution)/shard_map/reduce_sources/pallas_call | solution.py:838
  206.8 45.6 %spread_grads.1 = (f32[1024,256]{1,0:T(8,128)S(1)}, f32[1024,256]{1,0:T(8,128)S(1)}, f32[512,256]{1,0:T(8,128)S(1)}, f32[8,128]{1,0:T(8,128)S(1)}) custom-call(f32[1024,256]{1,0:T(8,128)S(1)} %get-tuple-element.40.grad_ref, bf16[1024,256]{1,0:T(8,128)(2,1)S(1)} %get-tuple-element.41.qv_ref, bf16[1024,256]{1,0:T(8,128)(2,1)S(1)} %copy-done.8, ...), custom_call_target="tpu_custom_call" | custom-call | tf_op jit(solution)/shard_map/spread_grads/pallas_call | solution.py:513
  253.0 0.8 fusion
  253.8 1.0 copy.26
  254.8 1.0 copy.27
  (29 shorter events, 4.7 us)
Async XLA Ops:
  7.2 113.1 %all-gather.2.cloned.1.call-start = ((), (), s32[]{:S(2)}) async-start(), calls=%async_computation | async-start | bytes 8912896 | tf_op jit(solution)/shard_map/all_gather | solution.py:908
  9.9 1.0 copy-start.5
  11.0 1.0 copy-start.6
  50.0 0.8 copy-start.7
  51.8 58.0 %collective-permute-start = (bf16[256,256]{1,0:T(8,128)(2,1)S(1)}, bf16[256,256]{1,0:T(8,128)(2,1)S(1)}, u32[]{:S(2)}, u32[]{:S(2)}) collective-permute-start(bf16[256,256]{1,0:T(8,128)(2,1)S(1)} %get-tuple-element.52), channel_id=1, source_target_pairs={{112,0},{0,16},{16,32},{32,48},{48,64},{64,80},{80,96},{96,112},{1... | collective-permute-start | bytes 393224 | tf_op jit(solution)/shard_map/ppermute | solution.py:879
  53.7 56.0 %collective-permute-start.1 = (bf16[256,256]{1,0:T(8,128)(2,1)S(1)}, bf16[256,256]{1,0:T(8,128)(2,1)S(1)}, u32[]{:S(2)}, u32[]{:S(2)}) collective-permute-start(bf16[256,256]{1,0:T(8,128)(2,1)S(1)} %get-tuple-element.53), channel_id=1, source_target_pairs={{16,0},{32,16},{48,32},{64,48},{80,64},{96,80},{112,96},{0,112},{1... | collective-permute-start | bytes 393224 | tf_op jit(solution)/shard_map/ppermute | solution.py:879
  54.5 0.9 copy-start.10
  55.4 0.9 copy-start.11
  57.4 0.7 copy-start.13
  108.0 1.0 copy-start
  108.9 0.8 copy-start.3
  120.3 86.5 %copy-start.8 = (bf16[1024,256]{1,0:T(8,128)(2,1)S(1)}, bf16[1024,256]{1,0:T(8,128)(2,1)}, u32[]{:S(2)}) copy-start(bf16[1024,256]{1,0:T(8,128)(2,1)} %copy-done.7) | copy-start | bytes 1572868
  120.3 86.5 %copy-start.12 = (s32[1024]{0:T(1024)S(1)}, s32[1024]{0:T(1024)}, u32[]{:S(2)}) copy-start(s32[1024]{0:T(1024)} %param.14) | copy-start | bytes 12292
  142.6 1.2 copy-start.1
  143.8 1.1 copy-start.2
  144.9 1.0 copy-start.4
  145.9 0.9 copy-start.9
Sparse Core Ops, SparseCore 0:
  50.9 69.3 all-gather.1

commit v6 on v5

--- a/solution.py
+++ b/solution.py
@@ -18,12 +18,12 @@
 COLS = (((1,), (1,)), ((), ()))
 
 
-def prep_kernel(dump, src_ref, dst_ref, count_ref, fast_ref, slow_ref, flag_ref):
+def place_edges(dump, src_ref, dst_ref, counts, fast_ref, slow_ref, flag_ref):
     blocks, slots = src_ref.shape
     src = src_ref[...]
     lane = lax.broadcasted_iota(jnp.int32, (blocks, slots), 1)
     cell = ((src >> 7) * ROWS_BLK + dst_ref[...]) * LANES + (src & 127)
-    live = lane < count_ref[...]
+    live = lane < counts
     spare = dump * LANES
     cell = jnp.where(live, cell, spare)
     row = cell >> 7
@@ -141,17 +141,10 @@
         turn(cells[2:], cells[:2])
 
 
-def build_counts(edge_src, edge_dst, block_count, part_nodes):
-    blocks, slots = edge_src.shape
+def build_counts(fast, slow, flags, block_count, part_nodes):
+    blocks, slots = fast.shape
     width = part_nodes + 2 * HALO
     dump = width // LANES * ROWS_BLK
-    edge = jax.ShapeDtypeStruct((blocks, slots), jnp.int32)
-    fast, slow, flags = pl.pallas_call(
-        functools.partial(prep_kernel, dump),
-        out_shape=(edge, edge, jax.ShapeDtypeStruct((blocks, LANES), jnp.int32)),
-        compiler_params=pltpu.CompilerParams(vmem_limit_bytes=32 << 20),
-        name="edge_prep",
-    )(edge_src, edge_dst, block_count[:, None])
     nodes = blocks * ROWS_BLK
 
     def filled(j):
@@ -180,7 +173,7 @@
             pl.BlockSpec((ROWS_BLK, 1), left),
         ),
         scratch_shapes=[pltpu.VMEM((dump + 8, LANES), jnp.float32)] * 4,
-        compiler_params=pltpu.CompilerParams(vmem_limit_bytes=52 << 20),
+        compiler_params=pltpu.CompilerParams(vmem_limit_bytes=60 << 20),
         cost_estimate=pl.CostEstimate(flops=80_000_000_000, bytes_accessed=40_000_000, transcendentals=0),
         name="edge_counts",
     )(block_count, fast[:, None], slow[:, None], flags[:, None])
@@ -210,6 +203,11 @@
 def as_row(column):
     wide = jnp.broadcast_to(column.astype(jnp.float32), (column.shape[0], LANES))
     return wide.T[0:1].astype(jnp.int32)
+
+
+def as_column(row):
+    tall = jnp.broadcast_to(row.astype(jnp.float32), (LANES, row.shape[1]))
+    return tall.T[:, 0:1].astype(jnp.int32)
 
 
 def pick(column, first, size):
@@ -243,8 +241,10 @@
 
 
 def fetch_kernel(
-    devices, owner_ref, qrow_ref, rem_ref, table_ref, remainder_ref, x_ref, qv_ref, rv_ref, asked_ref, slot_ref,
-    ids_out, ids_in, served, rows_in, slot_col, slot_hot, sems
+    devices, dump, owner_row, qrow_row, rem_row, table_hbm, remainder_hbm, src_hbm, dst_hbm, count_ref,
+    x_ref, qv_ref, rv_ref, asked_ref, slot_ref, fast_ref, slow_ref, flag_ref,
+    ids_out, ids_in, served, rows_in, slot_col, slot_hot, owner_ref, qrow_ref, rem_ref, table_ref, remainder_ref,
+    src_ref, dst_ref, sems
 ):
     slots, width = served.shape
     slot_cap = slots // devices
@@ -252,9 +252,21 @@
     me = ring_place()
     tile = 256
     greet_all(devices)
+    loads = [
+        pltpu.make_async_copy(table_hbm, table_ref, sems.at[5]),
+        pltpu.make_async_copy(remainder_hbm, remainder_ref, sems.at[6]),
+        pltpu.make_async_copy(src_hbm, src_ref, sems.at[7]),
+        pltpu.make_async_copy(dst_hbm, dst_ref, sems.at[8]),
+    ]
+    for load in loads:
+        load.start()
 
     def cut(r):
         return pl.ds(pl.multiple_of(r * tile, tile), tile)
+
+    owner_ref[...] = as_column(owner_row[...])
+    qrow_ref[...] = as_column(qrow_row[...])
+    rem_ref[...] = as_column(rem_row[...])
 
     owner_hot = pick(owner_ref[...], 0, devices)
     lane = lax.broadcasted_iota(jnp.int32, (tile, devices), 1)
@@ -278,6 +290,7 @@
         return carry
 
     lax.fori_loop(1, devices, ask, 0)
+    loads[1].wait()
 
     def remain(r, carry):
         rows = cut(r)
@@ -289,6 +302,7 @@
     own = pltpu.make_async_copy(ids_out.at[me], ids_in.at[me], sems.at[2])
     own.start()
     own.wait()
+    loads[0].wait()
     drain(ids_in.at[pl.ds(0, devices - 1)], sems.at[1])
     ids = ids_in[:, 0, :].astype(jnp.bfloat16)
     step = 16
@@ -334,6 +348,14 @@
         return carry
 
     lax.fori_loop(0, nodes // tile, prepare, 0)
+    loads[2].wait()
+    loads[3].wait()
+    blocks = src_ref.shape[0]
+    which = lax.broadcasted_iota(jnp.int32, (blocks, 1), 0)
+    counts = jnp.zeros((blocks, 1), jnp.int32)
+    for j in range(blocks):
+        counts = counts + jnp.where(which == j, count_ref[j], 0)
+    place_edges(dump, src_ref, dst_ref, counts, fast_ref, slow_ref, flag_ref)
     own_rows.wait()
     drain(rows_in.at[pl.ds(0, slots - slot_cap)], sems.at[4])
 
@@ -349,37 +371,51 @@
     drain(rows_in.at[pl.ds(0, slots - slot_cap)], sems.at[3])
 
 
-def fetch_rows(owner, qrow, rem, quotient, remainder, devices):
-    nodes = owner.shape[0]
+def fetch_rows(owner, qrow, rem, quotient, remainder, edge_src, edge_dst, block_count, devices, part_nodes):
+    nodes = owner.shape[1]
     slots = 2 * nodes
     width = quotient.shape[1]
     vmem = pl.BlockSpec(memory_space=pltpu.VMEM)
+    anywhere = pl.BlockSpec(memory_space=pl.ANY)
     rows = jax.ShapeDtypeStruct((nodes, width), jnp.bfloat16)
+    edge = jax.ShapeDtypeStruct(edge_src.shape, jnp.int32)
+    dump = (part_nodes + 2 * HALO) // LANES * ROWS_BLK
+    column = pltpu.VMEM((nodes, 1), jnp.int32)
     return pl.pallas_call(
-        functools.partial(fetch_kernel, devices),
+        functools.partial(fetch_kernel, devices, dump),
         out_shape=(
             rows,
             rows,
             rows,
             jax.ShapeDtypeStruct((1, slots), jnp.int32),
             jax.ShapeDtypeStruct((1, nodes), jnp.int32),
+            edge,
+            edge,
+            jax.ShapeDtypeStruct((edge_src.shape[0], LANES), jnp.int32),
         ),
-        in_specs=[vmem] * 5,
-        out_specs=(vmem,) * 5,
+        in_specs=[vmem] * 3 + [anywhere] * 4 + [pl.BlockSpec(memory_space=pltpu.SMEM)],
+        out_specs=(vmem,) * 8,
         scratch_shapes=[
             pltpu.VMEM((devices, 1, devices), jnp.float32),
             pltpu.VMEM((devices, 1, devices), jnp.float32),
             pltpu.VMEM((slots, width), jnp.bfloat16),
             pltpu.VMEM((slots, width), jnp.bfloat16),
-            pltpu.VMEM((nodes, 1), jnp.int32),
+            column,
             pltpu.VMEM((nodes, slots), jnp.bfloat16),
-            pltpu.SemaphoreType.DMA((5,)),
+            column,
+            column,
+            column,
+            pltpu.VMEM(quotient.shape, jnp.bfloat16),
+            pltpu.VMEM(remainder.shape, jnp.bfloat16),
+            pltpu.VMEM(edge_src.shape, jnp.int32),
+            pltpu.VMEM(edge_src.shape, jnp.int32),
+            pltpu.SemaphoreType.DMA((9,)),
         ],
         compiler_params=pltpu.CompilerParams(
-            collective_id=1, has_side_effects=True, vmem_limit_bytes=40 << 20
+            collective_id=1, has_side_effects=True, vmem_limit_bytes=60 << 20
         ),
         name="fetch_rows",
-    )(owner, qrow, rem, quotient, remainder)
+    )(owner, qrow, rem, quotient, remainder, edge_src, edge_dst, block_count)
 
 
 def spread_kernel(
@@ -532,7 +568,7 @@
             pltpu.SemaphoreType.DMA((9,)),
         ],
         compiler_params=pltpu.CompilerParams(
-            collective_id=2, has_side_effects=True, vmem_limit_bytes=40 << 20
+            collective_id=2, has_side_effects=True, vmem_limit_bytes=60 << 20
         ),
         name="spread_grads",
     )(grad, qv, rv, slot_row, rem_row, asked_row, sums)
@@ -625,13 +661,13 @@
             pltpu.VMEM((feats, feats), jnp.float32),
             pltpu.VMEM((feats, feats), jnp.float32),
         ],
-        compiler_params=pltpu.CompilerParams(vmem_limit_bytes=58 << 20),
+        compiler_params=pltpu.CompilerParams(vmem_limit_bytes=60 << 20),
         name="forward_layer",
     )(counts, gathered, *kept)
 
 
 def reduce_kernel(
-    counts_ref, grad_ref, weights_ref, halo_ref, dx_ref, out_ref, sums_ref, load, part, mid, fin, half_sum, mid2, fin2, sems_load, s_out, s_mid, s_fin, t_out, t_mid, t_fin, weights_in, w_out, w_in, halo_in, own, h_out, h_in
+    counts_ref, grad_ref, weights_ref, halo_ref, dx_ref, out_ref, sums_ref, load, part, mid, fin, half_sum, mid2, fin2, sems_load, s_out, s_mid, s_fin, t_out, t_mid, t_fin, weights_in, w_out, w_in, halo_in, own, h_out, h_in, dx_in, mine_in, s_own
 ):
     side = 4
     nodes = grad_ref.shape[1]
@@ -666,6 +702,10 @@
 
     for i in range(depth - 1):
         fetch(i).start()
+    own_dx = pltpu.make_async_copy(dx_ref, dx_in, s_own.at[0])
+    own_dx.start()
+    own_weights = pltpu.make_async_copy(weights_ref.at[dom], mine_in, s_own.at[1])
+    own_weights.start()
     pl.semaphore_wait(barrier, 4 + doms - 1)
 
     def to_dom(k):
@@ -798,6 +838,7 @@
         own[half * feats : (half + 1) * feats, :] = summed(half, 0)
     to_side(0).wait_recv()
     to_side(1).wait_recv()
+    own_dx.wait()
     for half in range(2):
         rows = slice(half * feats, (half + 1) * feats)
         for piece in range(2):
@@ -806,12 +847,13 @@
             total = own[rows, piece * span : (piece + 1) * span] + fin2[half, 0, piece].astype(jnp.float32)
             total = (total + fin2[half, 1, piece].astype(jnp.float32)).T
             near = slice(piece * span, (piece + 1) * span)
-            out_ref[near, rows] = dx_ref[near, rows] + total
+            out_ref[near, rows] = dx_in[near, rows] + total
             edge = slice(0, halo) if piece == 0 else slice(nodes - halo, nodes)
             out_ref[edge, rows] += halo_in[1 - piece, :, rows].astype(jnp.float32)
     to_side(0).wait_send()
     to_side(1).wait_send()
-    sums = weights_ref[dom]
+    own_weights.wait()
+    sums = mine_in[...]
     for k in range(1, doms):
         to_dom(k).wait_recv()
         sums = sums + weights_in[k]
@@ -835,13 +877,14 @@
     kind = jnp.bfloat16
     dma = pltpu.SemaphoreType.DMA
     vmem = pl.BlockSpec(memory_space=pltpu.VMEM)
+    anywhere = pl.BlockSpec(memory_space=pl.ANY)
     return pl.pallas_call(
         reduce_kernel,
         out_shape=(
             jax.ShapeDtypeStruct((nodes, feats), jnp.float32),
             jax.ShapeDtypeStruct(weights.shape[1:], jnp.float32),
         ),
-        in_specs=[pl.BlockSpec(memory_space=pl.ANY), vmem, vmem, vmem, vmem],
+        in_specs=[anywhere, vmem, anywhere, anywhere, anywhere],
         out_specs=(vmem, vmem),
         scratch_shapes=[
             pltpu.VMEM((3, nodes, nodes), kind),
@@ -865,9 +908,12 @@
             pltpu.VMEM((feats, nodes), jnp.float32),
             dma((2,)),
             dma((2,)),
+            pltpu.VMEM((nodes, feats), jnp.float32),
+            pltpu.VMEM(weights.shape[1:], jnp.float32),
+            dma((2,)),
         ],
         compiler_params=pltpu.CompilerParams(
-            collective_id=3, has_side_effects=True, vmem_limit_bytes=48 << 20
+            collective_id=3, has_side_effects=True, vmem_limit_bytes=60 << 20
         ),
         name="reduce_sources",
     )(counts, grad, weights, halo, dx)
@@ -902,15 +948,24 @@
     devices = lax.axis_size("dom") * lax.axis_size("blk")
     part_nodes = nodes_dev * lax.axis_size("blk")
     doms = lax.axis_size("dom")
-    features, quot_rows, remain_rows, asked_row, slot_row = fetch_rows(
-        node_owner, node_qrow[:, None], node_rem[:, None], quotient, remainder, devices
+    features, quot_rows, remain_rows, asked_row, slot_row, fast, slow, flags = fetch_rows(
+        node_owner.reshape(1, -1),
+        node_qrow[None],
+        node_rem[None],
+        quotient,
+        remainder,
+        edge_src,
+        edge_dst,
+        block_count,
+        devices,
+        part_nodes,
     )
     part_gathered = lax.all_gather(features, "blk", axis=0, tiled=True)
     low_rows = shifted(features[nodes_dev - HALO :], "dom", 1)
     high_rows = shifted(features[:HALO], "dom", -1)
     halo_rows = jnp.concatenate([low_rows, high_rows], axis=0)
 
-    counts, halo_counts, degree = build_counts(edge_src, edge_dst, block_count, part_nodes)
+    counts, halo_counts, degree = build_counts(fast, slow, flags, block_count, part_nodes)
     out, grad_t, halo_grads, dx_self, weights = forward(
         counts, part_gathered, halo_counts, halo_rows, degree, features, w_self, w_neigh, bias[None], cotangent, doms
     )

time: 263 us -> 262 us (level)
  Pallas kernels: 216 us -> 231 us
  waiting for transfers between devices: 9.8 us -> 2.1 us
  local copies, waits for them, and re-layouts: 19.5 us -> 12.2 us
    pallas_call x1, Pallas kernels: 49.9 us -> 60.1 us  [build_counts(): pl.pallas_call(functools.partial(count_kernel, dump), grid=(blocks + 1,),...]
    unnamed x31 -> x2, local copies, waits for them, and re-layouts: 14.3 us -> 4.52 us
    all_gather x1, waiting for transfers between devices: 9.78 us -> 2.08 us  [per_device(): part_gathered = lax.all_gather(features, 'blk', axis=0, tiled=True)]
    pallas_call x1, Pallas kernels: 59.9 us -> 63.9 us  [reduce_sources(): pl.pallas_call(reduce_kernel, out_shape=(jax.ShapeDtypeStruct((nodes, fea...]
    pallas_call x2 -> x1, Pallas kernels: 38.7 us -> 40.1 us  [fetch_rows(): pl.pallas_call(functools.partial(fetch_kernel, devices, dump), out_shape=...]
  transfers between devices with their start and end apart: 3 -> 3, of which waited for: 1 -> 1; matrix products, arithmetic and copies ran while one was open for 1% -> 2% of each run, Pallas kernels for 19% -> 23%
where the time goes in v6:
time: 262 us; the launch traced here: 261 us
  Pallas kernels  231 us (88%)
  between operations  14.1 us (5%)
  local copies, waits for them, and re-layouts  12.2 us (5%)
    pallas_call x1, Pallas kernels, reduce_sources(): pl.pallas_call(reduce_kernel, out_shape=(jax.ShapeDtypeStruct((nodes, fea...  63.9 us
    pallas_call x1, Pallas kernels, build_counts(): pl.pallas_call(functools.partial(count_kernel, dump), grid=(blocks + 1,),...  60.1 us
    pallas_call x1, Pallas kernels, spread_grads(): pl.pallas_call(functools.partial(spread_kernel, devices, rem_scale, scale...  44.4 us
    pallas_call x1, Pallas kernels, fetch_rows(): pl.pallas_call(functools.partial(fetch_kernel, devices, dump), out_shape=...  40.1 us
    pallas_call x1, Pallas kernels, forward(): pl.pallas_call(forward_kernel, grid=(steps,), out_shape=out_shape, in_spe...  22.2 us
  transfers between devices with their start and end apart: 3, of which 1 were waited for; matrix products, arithmetic and copies ran while one was open for 2% of the time, Pallas kernels for 23%

profile of v6, /device:TPU:1, one launch (start us, length us, event | category | flops | bytes accessed | tf_op | source)
XLA Modules:
  0.0 261.4 jit_solution(15582015051210472609)
XLA Ops:
  7.2 0.0 all-gather.2.cloned.1.call-start
  7.2 40.1 %fetch_rows.1 = (bf16[1024,256]{1,0:T(8,128)(2,1)}, bf16[1024,256]{1,0:T(8,128)(2,1)}, bf16[1024,256]{1,0:T(8,128)(2,1)}, s32[1,2048]{1,0:T(1,128)}, s32[1,1024]...) custom-call(s32[1,1024]{1,0:T(1,128)} %bitcast.8, s32[1,1024]{1,0:T(1,128)} %bitcast.9, ...), custom_call_target="tpu_custom_call" | custom-call | tf_op jit(solution)/shard_map/fetch_rows/pallas_call | solution.py:384
  47.3 0.0 all-gather.2.cloned.1.call-update
  47.4 1.0 fusion.1
  48.3 1.6 collective-permute-start
  49.9 0.0 collective-permute-start.1
  49.9 1.7 broadcast_in_dim.21.fast_ref
  51.6 1.7 broadcast_in_dim.22.slow_ref
  53.4 60.1 %edge_counts.1 = (bf16[1024,16384]{1,0:T(8,128)(2,1)}, bf16[1024,512]{1,0:T(8,128)(2,1)}, f32[1024,1]{1,0:T(8,128)}) custom-call(s32[8]{0:T(128)} %count_ref.3, s32[8,1,6144]{2,1,0:T(1,128)} %broadcast_in_dim.21.fast_ref, s32[8,1,6144]{2,1,0:T(1,128)} %broadcast_in_dim.22.slow_ref, s32[8,1,128]{2,1,0:T(1,128)} %bitcast.12), custom_call_target="tpu_custom_call" | custom-call | flops 80000000000 | bytes 40000000 | tf_op jit(solution)/shard_map/edge_counts/pallas_call | solution.py:156
  113.5 0.0 collective-permute-done
  113.5 0.0 collective-permute-done.1
  113.5 0.7 pad_maximum_fusion.halo_rows_ref
  114.2 2.1 all-gather.2.cloned.1.call-done.rows_ref
  116.3 22.2 %forward_layer.1 = (bf16[1024,256]{1,0:T(8,128)(2,1)}, bf16[256,1024]{1,0:T(8,128)(2,1)}, bf16[512,256]{1,0:T(8,128)(2,1)}, f32[1024,256]{1,0:T(8,128)}, f32[8,72,256]{2,1,0:T(8,128)}) custom-call(bf16[1024,16384]{1,0:T(8,128)(2,1)} %get-tuple-element.31.counts_ref, bf16[16384,256]{1,0:T(8,128)(2,1)} %all-gather.2.cloned.1.call-done.rows_ref, ...), custom_call_target="tpu_custom_call" | custom-call | tf_op jit(solution)/shard_map/forward_layer/pallas_call | solution.py:649
  138.6 63.9 %reduce_sources.1 = (f32[1024,256]{1,0:T(8,128)}, f32[72,256]{1,0:T(8,128)}) custom-call(bf16[1024,16384]{1,0:T(8,128)(2,1)} %get-tuple-element.31.counts_ref, bf16[256,1024]{1,0:T(8,128)(2,1)} %get-tuple-element.36.grad_ref, f32[8,72,256]{2,1,0:T(8,128)} %get-tuple-element.37.weights_ref, bf16[512,256]{1,0:T(8,128)(2,1)} %get-tuple-element.38.halo_ref, ...), custom_call_target="tpu_custom_call" | custom-call | tf_op jit(solution)/shard_map/reduce_sources/pallas_call | solution.py:881
  202.4 44.4 %spread_grads.1 = (f32[1024,256]{1,0:T(8,128)}, f32[1024,256]{1,0:T(8,128)}, f32[512,256]{1,0:T(8,128)}, f32[8,128]{1,0:T(8,128)}) custom-call(f32[1024,256]{1,0:T(8,128)} %get-tuple-element.40.grad_ref, bf16[1024,256]{1,0:T(8,128)(2,1)} %get-tuple-element.41.qv_ref, bf16[1024,256]{1,0:T(8,128)(2,1)} %get-tuple-element.42.rv_ref, ...), custom_call_target="tpu_custom_call" | custom-call | tf_op jit(solution)/shard_map/spread_grads/pallas_call | solution.py:549
  246.9 1.3 reshape.19
  248.2 1.9 fusion
  250.0 2.3 copy.20
  252.3 2.3 copy.21
Async XLA Ops:
  7.2 109.1 %all-gather.2.cloned.1.call-start = ((), (), s32[]{:S(2)}) async-start(), calls=%async_computation | async-start | bytes 8912896 | tf_op jit(solution)/shard_map/all_gather | solution.py:963
  48.3 65.2 %collective-permute-start = (bf16[256,256]{1,0:T(8,128)(2,1)S(1)}, bf16[256,256]{1,0:T(8,128)(2,1)S(1)}, u32[]{:S(2)}, u32[]{:S(2)}) collective-permute-start(bf16[256,256]{1,0:T(8,128)(2,1)S(1)} %get-tuple-element.52), channel_id=1, source_target_pairs={{112,0},{0,16},{16,32},{32,48},{48,64},{64,80},{80,96},{96,112},{1... | collective-permute-start | bytes 393224 | tf_op jit(solution)/shard_map/ppermute | solution.py:925
  49.9 63.6 %collective-permute-start.1 = (bf16[256,256]{1,0:T(8,128)(2,1)S(1)}, bf16[256,256]{1,0:T(8,128)(2,1)S(1)}, u32[]{:S(2)}, u32[]{:S(2)}) collective-permute-start(bf16[256,256]{1,0:T(8,128)(2,1)S(1)} %get-tuple-element.53), channel_id=1, source_target_pairs={{16,0},{32,16},{48,32},{64,48},{80,64},{96,80},{112,96},{0,112},{1... | collective-permute-start | bytes 393224 | tf_op jit(solution)/shard_map/ppermute | solution.py:925
Sparse Core Ops, SparseCore 0:
  47.5 68.7 all-gather.1

commit v7 on v6

--- a/solution.py
+++ b/solution.py
@@ -32,8 +32,8 @@
     for s in range(1, BATCH):
         clash = clash | ((pltpu.roll(row, s, 1) == row) & (place >= s))
     clash = clash & live
-    fast_ref[...] = jnp.where(clash, spare, cell)
-    slow_ref[...] = jnp.where(clash, cell, spare)
+    fast_ref[:, 0, :] = jnp.where(clash, spare, cell)
+    slow_ref[:, 0, :] = jnp.where(clash, cell, spare)
     ones = jnp.where(clash, 1.0, 0.0).astype(jnp.bfloat16)
     chunks = slots // LANES
     col = lax.broadcasted_iota(jnp.int32, (blocks, LANES), 1)
@@ -48,7 +48,7 @@
         some = bits > 0
         found = found + jnp.where((col == number) & some, c * 65536 + bits, 0)
         number = number + some.astype(jnp.int32)
-    flag_ref[...] = jnp.where(col == LANES - 1, number, found)
+    flag_ref[:, 0, :] = jnp.where(col == LANES - 1, number, found)
 
 
 def count_kernel(dump, count_ref, fast_ref, slow_ref, flag_ref, main_ref, halo_ref, deg_ref, *cells):
@@ -71,7 +71,7 @@
             ref[pl.ds(dump, 8), :] = jnp.zeros((8, LANES), jnp.float32)
 
     count = jnp.where(j < blocks, count_ref[jnp.minimum(j, blocks - 1)], 0)
-    pairs = (count + 2 * BATCH - 1) // (2 * BATCH)
+    pairs = (count + 4 * BATCH - 1) // (4 * BATCH)
 
     def add_batch(ref, first):
         keys = [fast_ref[0, 0, first + i] for i in range(BATCH)]
@@ -83,8 +83,8 @@
 
     def turn(fill, leave):
         def add_pair(t, carry):
-            add_batch(fill[0], t * 2 * BATCH)
-            add_batch(fill[1], t * 2 * BATCH + BATCH)
+            for i in range(4):
+                add_batch(fill[i % 2], (t * 4 + i) * BATCH)
             return carry
 
         def flush(ref, first):
@@ -101,13 +101,15 @@
 
         def both(t, total):
             add_pair(t, 0)
-            return flush(main_ref, 0)(t, total)
+            for i in range(2):
+                total = flush(main_ref, 0)(t * 2 + i, total)
+            return total
 
         steps = his_main
-        joint = jnp.minimum(pairs, steps)
+        joint = jnp.minimum(pairs, steps // 2)
         total = lax.fori_loop(0, joint, both, zero)
         lax.fori_loop(joint, pairs, add_pair, 0)
-        total = lax.fori_loop(joint, steps, flush(main_ref, 0), total)
+        total = lax.fori_loop(joint * 2, steps, flush(main_ref, 0), total)
 
         total = lax.fori_loop(0, his - his_main, flush(halo_ref, his_main), total)
         deg_ref[...] = jnp.sum(total, axis=1, keepdims=True)
@@ -142,7 +144,7 @@
 
 
 def build_counts(fast, slow, flags, block_count, part_nodes):
-    blocks, slots = fast.shape
+    blocks, _, slots = fast.shape
     width = part_nodes + 2 * HALO
     dump = width // LANES * ROWS_BLK
     nodes = blocks * ROWS_BLK
@@ -176,7 +178,7 @@
         compiler_params=pltpu.CompilerParams(vmem_limit_bytes=60 << 20),
         cost_estimate=pl.CostEstimate(flops=80_000_000_000, bytes_accessed=40_000_000, transcendentals=0),
         name="edge_counts",
-    )(block_count, fast[:, None], slow[:, None], flags[:, None])
+    )(block_count, fast, slow, flags)
 
 
 def ring_place():
@@ -242,7 +244,7 @@
 
 def fetch_kernel(
     devices, dump, owner_row, qrow_row, rem_row, table_hbm, remainder_hbm, src_hbm, dst_hbm, count_ref,
-    x_ref, qv_ref, rv_ref, asked_ref, slot_ref, fast_ref, slow_ref, flag_ref,
+    x_ref, qv_ref, rv_ref, asked_ref, slot_ref, fast_ref, slow_ref, flag_ref, first_ref, last_ref,
     ids_out, ids_in, served, rows_in, slot_col, slot_hot, owner_ref, qrow_ref, rem_ref, table_ref, remainder_ref,
     src_ref, dst_ref, sems
 ):
@@ -367,6 +369,8 @@
         return carry
 
     lax.fori_loop(0, nodes // tile, finish, 0)
+    first_ref[...] = x_ref[:HALO, :]
+    last_ref[...] = x_ref[nodes - HALO :, :]
     drain(ids_in.at[pl.ds(0, devices - 1)], sems.at[0])
     drain(rows_in.at[pl.ds(0, slots - slot_cap)], sems.at[3])
 
@@ -378,7 +382,9 @@
     vmem = pl.BlockSpec(memory_space=pltpu.VMEM)
     anywhere = pl.BlockSpec(memory_space=pl.ANY)
     rows = jax.ShapeDtypeStruct((nodes, width), jnp.bfloat16)
-    edge = jax.ShapeDtypeStruct(edge_src.shape, jnp.int32)
+    blocks, edges = edge_src.shape
+    edge = jax.ShapeDtypeStruct((blocks, 1, edges), jnp.int32)
+    half = jax.ShapeDtypeStruct((HALO, width), jnp.bfloat16)
     dump = (part_nodes + 2 * HALO) // LANES * ROWS_BLK
     column = pltpu.VMEM((nodes, 1), jnp.int32)
     return pl.pallas_call(
@@ -391,10 +397,12 @@
             jax.ShapeDtypeStruct((1, nodes), jnp.int32),
             edge,
             edge,
-            jax.ShapeDtypeStruct((edge_src.shape[0], LANES), jnp.int32),
+            jax.ShapeDtypeStruct((blocks, 1, LANES), jnp.int32),
+            half,
+            half,
         ),
         in_specs=[vmem] * 3 + [anywhere] * 4 + [pl.BlockSpec(memory_space=pltpu.SMEM)],
-        out_specs=(vmem,) * 8,
+        out_specs=(vmem,) * 10,
         scratch_shapes=[
             pltpu.VMEM((devices, 1, devices), jnp.float32),
             pltpu.VMEM((devices, 1, devices), jnp.float32),
@@ -568,14 +576,14 @@
             pltpu.SemaphoreType.DMA((9,)),
         ],
         compiler_params=pltpu.CompilerParams(
-            collective_id=2, has_side_effects=True, vmem_limit_bytes=60 << 20
+            collective_id=2, has_side_effects=True, vmem_limit_bytes=40 << 20
         ),
         name="spread_grads",
     )(grad, qv, rv, slot_row, rem_row, asked_row, sums)
 
 
 def forward_kernel(
-    counts_ref, rows_ref, halo_counts_ref, halo_rows_ref, deg_ref, x_ref, w_self_ref, w_neigh_ref, bias_ref, cot_ref,
+    counts_ref, rows_ref, halo_counts_ref, low_ref, high_ref, deg_ref, x_ref, w_self_ref, w_neigh_ref, bias_ref, cot_ref,
     out_ref, grad_ref, halo_ref, dx_ref, weights_ref, total, acc_self, acc_neigh
 ):
     k = pl.program_id(0)
@@ -588,7 +596,8 @@
     @pl.when(k == 0)
     def _():
         def start(r, carry):
-            total[cut(r), :] = dot(halo_counts_ref[cut(r), :], halo_rows_ref[...])
+            low = dot(halo_counts_ref[cut(r), :HALO], low_ref[...])
+            total[cut(r), :] = low + dot(halo_counts_ref[cut(r), HALO:], high_ref[...])
             return carry
 
         lax.fori_loop(0, nodes // tile, start, 0)
@@ -630,7 +639,7 @@
             weights_ref[c, each:, :] = pltpu.roll(spread, shift, 1) if shift else spread
 
 
-def forward(counts, gathered, halo_counts, halo_rows, degree, features, w_self, w_neigh, bias, cotangent, doms):
+def forward(counts, gathered, halo_counts, low_rows, high_rows, degree, features, w_self, w_neigh, bias, cotangent, doms):
     nodes, feats = features.shape
     wide = 4 * nodes
     steps = counts.shape[1] // wide
@@ -641,11 +650,11 @@
     out_shape = (
         jax.ShapeDtypeStruct((nodes, feats), jnp.bfloat16),
         jax.ShapeDtypeStruct((feats, nodes), jnp.bfloat16),
-        jax.ShapeDtypeStruct(halo_rows.shape, jnp.bfloat16),
+        jax.ShapeDtypeStruct((2 * HALO, feats), jnp.bfloat16),
         jax.ShapeDtypeStruct((nodes, feats), jnp.float32),
         jax.ShapeDtypeStruct((doms, 2 * feats // doms + 8, feats), jnp.float32),
     )
-    kept = (halo_counts, halo_rows, degree, features, w_self, w_neigh, bias, cotangent)
+    kept = (halo_counts, low_rows, high_rows, degree, features, w_self, w_neigh, bias, cotangent)
     return pl.pallas_call(
         forward_kernel,
         grid=(steps,),
@@ -948,7 +957,7 @@
     devices = lax.axis_size("dom") * lax.axis_size("blk")
     part_nodes = nodes_dev * lax.axis_size("blk")
     doms = lax.axis_size("dom")
-    features, quot_rows, remain_rows, asked_row, slot_row, fast, slow, flags = fetch_rows(
+    features, quot_rows, remain_rows, asked_row, slot_row, fast, slow, flags, first, last = fetch_rows(
         node_owner.reshape(1, -1),
         node_qrow[None],
         node_rem[None],
@@ -961,13 +970,12 @@
         part_nodes,
     )
     part_gathered = lax.all_gather(features, "blk", axis=0, tiled=True)
-    low_rows = shifted(features[nodes_dev - HALO :], "dom", 1)
-    high_rows = shifted(features[:HALO], "dom", -1)
-    halo_rows = jnp.concatenate([low_rows, high_rows], axis=0)
+    low_rows = shifted(last, "dom", 1)
+    high_rows = shifted(first, "dom", -1)
 
     counts, halo_counts, degree = build_counts(fast, slow, flags, block_count, part_nodes)
     out, grad_t, halo_grads, dx_self, weights = forward(
-        counts, part_gathered, halo_counts, halo_rows, degree, features, w_self, w_neigh, bias[None], cotangent, doms
+        counts, part_gathered, halo_counts, low_rows, high_rows, degree, features, w_self, w_neigh, bias[None], cotangent, doms
     )
     grad_x, weight_sums = reduce_sources(counts, grad_t, weights, halo_grads, dx_self)
     nodes_total = nodes_dev * devices

time: 262 us -> 251 us (0.958)
  Pallas kernels: 231 us -> 215 us
  waiting for transfers between devices: 2.1 us -> 15 us
  local copies, waits for them, and re-layouts: 12.2 us -> 5.53 us
    all_gather x1, waiting for transfers between devices: 2.08 us -> 15 us  [per_device(): part_gathered = lax.all_gather(features, 'blk', axis=0, tiled=True)]
    pallas_call x1, Pallas kernels: 60.1 us -> 52.4 us  [build_counts(): pl.pallas_call(functools.partial(count_kernel, dump), grid=(blocks + 1,),...]
    pallas_call x1, Pallas kernels: 63.9 us -> 56.1 us  [reduce_sources(): pl.pallas_call(reduce_kernel, out_shape=(jax.ShapeDtypeStruct((nodes, fea...]
    broadcast_in_dim x2 -> x0, local copies, waits for them, and re-layouts: 3.48 us -> none  [the longest x1 1.74 us: build_counts(): fast[:, None]]
  transfers between devices with their start and end apart: 3 -> 3, of which waited for: 1 -> 1; matrix products, arithmetic and copies ran while one was open for 2% -> 0% of each run, Pallas kernels for 23% -> 21%
where the time goes in v7:
time: 251 us
  Pallas kernels  215 us (86%)
  waiting for transfers between devices  15 us (6%)
  between operations  14.2 us (6%)
  local copies, waits for them, and re-layouts  5.53 us (2%)
    pallas_call x1, Pallas kernels, reduce_sources(): pl.pallas_call(reduce_kernel, out_shape=(jax.ShapeDtypeStruct((nodes, fea...  56.1 us
    pallas_call x1, Pallas kernels, build_counts(): pl.pallas_call(functools.partial(count_kernel, dump), grid=(blocks + 1,),...  52.4 us
    pallas_call x1, Pallas kernels, spread_grads(): pl.pallas_call(functools.partial(spread_kernel, devices, rem_scale, scale...  43.7 us
    pallas_call x1, Pallas kernels, fetch_rows(): pl.pallas_call(functools.partial(fetch_kernel, devices, dump), out_shape=...  40.1 us
    pallas_call x1, Pallas kernels, forward(): pl.pallas_call(forward_kernel, grid=(steps,), out_shape=out_shape, in_spe...  22.4 us
    all_gather x1, waiting for transfers between devices, per_device(): part_gathered = lax.all_gather(features, 'blk', axis=0, tiled=True)  15 us
  transfers between devices with their start and end apart: 3, of which 1 were waited for; matrix products, arithmetic and copies ran while one was open for 0% of the time, Pallas kernels for 21%

profile of v7, /device:TPU:1, one launch (start us, length us, event | category | flops | bytes accessed | tf_op | source)
XLA Modules:
  0.0 251.0 jit_solution(15131395861498387910)
XLA Ops:
  7.2 0.0 all-gather.2.cloned.1.call-start
  7.2 40.1 %fetch_rows.1 = (bf16[1024,256]{1,0:T(8,128)(2,1)}, bf16[1024,256]{1,0:T(8,128)(2,1)}, bf16[1024,256]{1,0:T(8,128)(2,1)}, s32[1,2048]{1,0:T(1,128)}, s32[1,1024]...) custom-call(s32[1,1024]{1,0:T(1,128)} %bitcast.8, ...), custom_call_target="tpu_custom_call" | custom-call | tf_op jit(solution)/shard_map/fetch_rows/pallas_call | solution.py:390
  47.3 0.0 all-gather.2.cloned.1.call-update
  47.4 1.6 collective-permute-start
  48.9 0.0 collective-permute-start.1
  48.9 52.4 %edge_counts.1 = (bf16[1024,16384]{1,0:T(8,128)(2,1)}, bf16[1024,512]{1,0:T(8,128)(2,1)}, f32[1024,1]{1,0:T(8,128)}) custom-call(s32[8]{0:T(128)} %count_ref.3, s32[8,1,6144]{2,1,0:T(1,128)} %get-tuple-element.30.fast_ref, s32[8,1,6144]{2,1,0:T(1,128)} %get-tuple-element.31.slow_ref, s32[8,1,128]{2,1,0:T(1,128)} %get-tuple-element.32.flag_ref), custom_call_target="tpu_custom_call" | custom-call | flops 80000000000 | bytes 40000000 | tf_op jit(solution)/shard_map/edge_counts/pallas_call | solution.py:158
  101.3 0.0 collective-permute-done.low_ref
  101.3 0.0 collective-permute-done.1.high_ref
  101.3 0.0 copy-start.8
  101.3 15.0 %all-gather.2.cloned.1.call-done.rows_ref = bf16[16384,256]{1,0:T(8,128)(2,1)} async-done(((bf16[1024,256]{1,0:T(8,128)(2,1)}), bf16[16384,256]{1,0:T(8,128)(2,1)}) %all-gather.2.cloned.1.call-update) | async-done | bytes 8388624 | tf_op jit(solution)/shard_map/all_gather | solution.py:972
  116.3 0.0 copy-done.7
  116.3 0.0 copy-done.8
  116.3 0.0 copy-start.4
  116.3 0.0 copy-start.5
  116.3 0.0 copy-start.6
  116.3 22.4 %forward_layer.1 = (bf16[1024,256]{1,0:T(8,128)(2,1)}, bf16[256,1024]{1,0:T(8,128)(2,1)}, bf16[512,256]{1,0:T(8,128)(2,1)}, f32[1024,256]{1,0:T(8,128)}, f32[8,72,256]{2,1,0:T(8,128)}) custom-call(bf16[1024,16384]{1,0:T(8,128)(2,1)} %get-tuple-element.33.counts_ref, bf16[16384,256]{1,0:T(8,128)(2,1)} %all-gather.2.cloned.1.call-done.rows_ref, ...), custom_call_target="tpu_custom_call" | custom-call | tf_op jit(solution)/shard_map/forward_layer/pallas_call | solution.py:658
  138.7 56.1 %reduce_sources.1 = (f32[1024,256]{1,0:T(8,128)}, f32[72,256]{1,0:T(8,128)}) custom-call(bf16[1024,16384]{1,0:T(8,128)(2,1)} %get-tuple-element.33.counts_ref, bf16[256,1024]{1,0:T(8,128)(2,1)} %get-tuple-element.40.grad_ref, f32[8,72,256]{2,1,0:T(8,128)} %get-tuple-element.41.weights_ref, bf16[512,256]{1,0:T(8,128)(2,1)} %get-tuple-element.42.halo_ref, ...), custom_call_target="tpu_custom_call" | custom-call | tf_op jit(solution)/shard_map/reduce_sources/pallas_call | solution.py:890
  194.9 1.2 copy-done
  196.1 0.9 copy-done.3
  197.0 43.7 %spread_grads.1 = (f32[1024,256]{1,0:T(8,128)S(1)}, f32[1024,256]{1,0:T(8,128)S(1)}, f32[512,256]{1,0:T(8,128)S(1)}, f32[8,128]{1,0:T(8,128)S(1)}) custom-call(f32[1024,256]{1,0:T(8,128)S(1)} %copy-done, bf16[1024,256]{1,0:T(8,128)(2,1)S(1)} %copy-done.1, bf16[1024,256]{1,0:T(8,128)(2,1)S(1)} %copy-done.2, s32[1,1024]{1,0:T(1,128)S(1)} %copy-done.6, ...), custom_call_target="tpu_custom_call" | custom-call | tf_op jit(solution)/shard_map/spread_grads/pallas_call | solution.py:557
  240.7 0.6 reshape.19
  241.3 0.8 fusion
  242.2 1.0 copy.20
  243.1 1.0 copy.21
  (10 shorter events, 0.0 us)
Async XLA Ops:
  7.2 109.1 %all-gather.2.cloned.1.call-start = ((), (), s32[]{:S(2)}) async-start(), calls=%async_computation | async-start | bytes 8912896 | tf_op jit(solution)/shard_map/all_gather | solution.py:972
  47.4 53.9 %collective-permute-start = (bf16[256,256]{1,0:T(8,128)(2,1)}, bf16[256,256]{1,0:T(8,128)(2,1)S(1)}, u32[]{:S(2)}, u32[]{:S(2)}) collective-permute-start(bf16[256,256]{1,0:T(8,128)(2,1)} %get-tuple-element.36), channel_id=1, source_target_pairs={{112,0},{0,16},{16,32},{32,48},{48,64},{64,80},{80,96},{96,112},{1... | collective-permute-start | bytes 393224 | tf_op jit(solution)/shard_map/ppermute | solution.py:934
  48.9 52.4 %collective-permute-start.1 = (bf16[256,256]{1,0:T(8,128)(2,1)}, bf16[256,256]{1,0:T(8,128)(2,1)S(1)}, u32[]{:S(2)}, u32[]{:S(2)}) collective-permute-start(bf16[256,256]{1,0:T(8,128)(2,1)} %get-tuple-element.37), channel_id=1, source_target_pairs={{16,0},{32,16},{48,32},{64,48},{80,64},{96,80},{112,96},{0,112},{1... | collective-permute-start | bytes 393224 | tf_op jit(solution)/shard_map/ppermute | solution.py:934
  101.3 15.0 %copy-start.7 = (bf16[256,256]{1,0:T(8,128)(2,1)}, bf16[256,256]{1,0:T(8,128)(2,1)S(1)}, u32[]{:S(2)}) copy-start(bf16[256,256]{1,0:T(8,128)(2,1)S(1)} %collective-permute-done.low_ref) | copy-start | bytes 393220
  101.3 15.0 %copy-start.8 = (bf16[256,256]{1,0:T(8,128)(2,1)}, bf16[256,256]{1,0:T(8,128)(2,1)S(1)}, u32[]{:S(2)}) copy-start(bf16[256,256]{1,0:T(8,128)(2,1)S(1)} %collective-permute-done.1.high_ref) | copy-start | bytes 393220
  116.3 78.5 %copy-start.1 = (bf16[1024,256]{1,0:T(8,128)(2,1)S(1)}, bf16[1024,256]{1,0:T(8,128)(2,1)}, u32[]{:S(2)}) copy-start(bf16[1024,256]{1,0:T(8,128)(2,1)} %get-tuple-element.45.qv_ref) | copy-start | bytes 1572868
  116.3 78.5 %copy-start.2 = (bf16[1024,256]{1,0:T(8,128)(2,1)S(1)}, bf16[1024,256]{1,0:T(8,128)(2,1)}, u32[]{:S(2)}) copy-start(bf16[1024,256]{1,0:T(8,128)(2,1)} %get-tuple-element.46.rv_ref) | copy-start | bytes 1572868
  116.3 78.6 %copy-start.4 = (s32[1024]{0:T(1024)S(1)}, s32[1024]{0:T(1024)}, u32[]{:S(2)}) copy-start(s32[1024]{0:T(1024)} %param.14) | copy-start | bytes 12292
  116.3 78.6 %copy-start.5 = (s32[1,2048]{1,0:T(1,128)S(1)}, s32[1,2048]{1,0:T(1,128)}, u32[]{:S(2)}) copy-start(s32[1,2048]{1,0:T(1,128)} %get-tuple-element.48.asked_ref) | copy-start | bytes 24580
  116.3 78.6 %copy-start.6 = (s32[1,1024]{1,0:T(1,128)S(1)}, s32[1,1024]{1,0:T(1,128)}, u32[]{:S(2)}) copy-start(s32[1,1024]{1,0:T(1,128)} %get-tuple-element.47.slot_ref) | copy-start | bytes 12292
  194.9 1.2 copy-start
  196.1 0.9 copy-start.3
Sparse Core Ops, SparseCore 0:
  47.5 68.7 all-gather.1

commit v8 on v7

--- a/solution.py
+++ b/solution.py
@@ -496,9 +496,19 @@
         lax.fori_loop(0, step, one, 0)
         return carry
 
+    half = devices // 2
+    core = lax.rem(dom, 2)
+    twin = (dom + 1 - 2 * core) * peers + blk
+
     def send_total(k, carry):
-        other = lax.rem(me + k, devices)
+        turn = lax.rem(dom // 2 * peers + blk + k, half)
+        other = (turn // peers * 2 + core) * peers + lax.rem(turn, peers)
         send(piece, whole.at[me], other, sems.at[4], sems.at[5])
+        return carry
+
+    def relay(z, carry):
+        group = pl.ds((z * 2 + core) * peers, peers)
+        send(whole.at[group], whole.at[group], twin, sems.at[9], sems.at[10])
         return carry
 
     def keep(src, dst):
@@ -517,16 +527,18 @@
     drain(rem_in.at[pl.ds(0, devices - 1)], sems.at[1])
     piece[:tall] = (jnp.sum(rem_in[...].astype(jnp.float32), axis=0) * rem_scale).astype(jnp.bfloat16)
     piece[tall:] = (jnp.sum(sums_in[...], axis=0) * scale).astype(jnp.bfloat16)
-    lax.fori_loop(1, devices, send_total, 0)
+    lax.fori_loop(1, half, send_total, 0)
     keep(piece, whole.at[me])
     drain(grads_in.at[pl.ds(0, slots - slot_cap)], sems.at[3])
+    drain(whole.at[pl.ds(0, half - 1)], sems.at[5])
+    lax.fori_loop(0, half // peers, relay, 0)
 
     def collect(r, carry):
         quot_ref[cut(r), :] = dot(pick_rows(asked_ref[...], r * size, size), grads_in[...])
         return carry
 
     lax.fori_loop(0, quot_ref.shape[0] // size, collect, 0)
-    drain(whole.at[pl.ds(0, devices - 1)], sems.at[5])
+    drain(whole.at[pl.ds(0, half)], sems.at[10])
 
     def lay(k, carry):
         for part in range(across):
@@ -541,7 +553,8 @@
         bias_ref[d : d + 1, :] = whole[d * peers, tall + 8 : tall + 16, :].astype(jnp.float32)[0:1]
     drain(rem_in.at[pl.ds(0, devices - 1)], sems.at[0])
     drain(grads_in.at[pl.ds(0, slots - slot_cap)], sems.at[2])
-    drain(whole.at[pl.ds(0, devices - 1)], sems.at[4])
+    drain(whole.at[pl.ds(0, half - 1)], sems.at[4])
+    drain(whole.at[pl.ds(0, half)], sems.at[9])
     drain(sums_in.at[pl.ds(0, peers - 1)], sems.at[7])
 
 
@@ -573,7 +586,7 @@
             pltpu.VMEM((peers, 16, wide), jnp.float32),
             pltpu.VMEM((tall + 16, wide), kind),
             pltpu.VMEM((devices, tall + 16, wide), kind),
-            pltpu.SemaphoreType.DMA((9,)),
+            pltpu.SemaphoreType.DMA((11,)),
         ],
         compiler_params=pltpu.CompilerParams(
             collective_id=2, has_side_effects=True, vmem_limit_bytes=40 << 20

time: 251 us -> 246 us (0.980)
  waiting for transfers between devices: 15 us -> 3.4 us
  Pallas kernels: 215 us -> 220 us
    pallas_call x1, Pallas kernels: 52.4 us -> 64 us  [build_counts(): pl.pallas_call(functools.partial(count_kernel, dump), grid=(blocks + 1,),...]
    all_gather x1, waiting for transfers between devices: 15 us -> 3.38 us  [per_device(): part_gathered = lax.all_gather(features, 'blk', axis=0, tiled=True)]
    pallas_call x1, Pallas kernels: 43.7 us -> 39.3 us  [spread_grads(): pl.pallas_call(functools.partial(spread_kernel, devices, rem_scale, scale...]
  transfers between devices with their start and end apart: 3 -> 3, of which waited for: 1 -> 1; matrix products, arithmetic and copies ran while one was open for 0% -> 0% of each run, Pallas kernels for 21% -> 26%
where the time goes in v8:
time: 246 us; the launch traced here: 245 us
  Pallas kernels  220 us (89%)
  between operations  14.2 us (6%)
  local copies, waits for them, and re-layouts  5.53 us (2%)
  waiting for transfers between devices  3.4 us (1%)
    pallas_call x1, Pallas kernels, build_counts(): pl.pallas_call(functools.partial(count_kernel, dump), grid=(blocks + 1,),...  64 us
    pallas_call x1, Pallas kernels, reduce_sources(): pl.pallas_call(reduce_kernel, out_shape=(jax.ShapeDtypeStruct((nodes, fea...  54.6 us
    pallas_call x1, Pallas kernels, fetch_rows(): pl.pallas_call(functools.partial(fetch_kernel, devices, dump), out_shape=...  40.1 us
    pallas_call x1, Pallas kernels, spread_grads(): pl.pallas_call(functools.partial(spread_kernel, devices, rem_scale, scale...  39.3 us
    pallas_call x1, Pallas kernels, forward(): pl.pallas_call(forward_kernel, grid=(steps,), out_shape=out_shape, in_spe...  22.4 us
  transfers between devices with their start and end apart: 3, of which 1 were waited for; matrix products, arithmetic and copies ran while one was open for 0% of the time, Pallas kernels for 26%

profile of v8, /device:TPU:1, one launch (start us, length us, event | category | flops | bytes accessed | tf_op | source)
XLA Modules:
  0.0 245.0 jit_solution(3972599864322545205)
XLA Ops:
  7.2 0.0 all-gather.2.cloned.1.call-start
  7.2 40.1 %fetch_rows.1 = (bf16[1024,256]{1,0:T(8,128)(2,1)}, bf16[1024,256]{1,0:T(8,128)(2,1)}, bf16[1024,256]{1,0:T(8,128)(2,1)}, s32[1,2048]{1,0:T(1,128)}, s32[1,1024]...) custom-call(s32[1,1024]{1,0:T(1,128)} %bitcast.8, ...), custom_call_target="tpu_custom_call" | custom-call | tf_op jit(solution)/shard_map/fetch_rows/pallas_call | solution.py:390
  47.3 0.0 all-gather.2.cloned.1.call-update
  47.4 1.6 collective-permute-start
  48.9 0.0 collective-permute-start.1
  48.9 64.0 %edge_counts.1 = (bf16[1024,16384]{1,0:T(8,128)(2,1)}, bf16[1024,512]{1,0:T(8,128)(2,1)}, f32[1024,1]{1,0:T(8,128)}) custom-call(s32[8]{0:T(128)} %count_ref.3, s32[8,1,6144]{2,1,0:T(1,128)} %get-tuple-element.30.fast_ref, s32[8,1,6144]{2,1,0:T(1,128)} %get-tuple-element.31.slow_ref, s32[8,1,128]{2,1,0:T(1,128)} %get-tuple-element.32.flag_ref), custom_call_target="tpu_custom_call" | custom-call | flops 80000000000 | bytes 40000000 | tf_op jit(solution)/shard_map/edge_counts/pallas_call | solution.py:158
  112.9 0.0 collective-permute-done.low_ref
  112.9 0.0 collective-permute-done.1.high_ref
  112.9 0.0 copy-start.8
  112.9 3.4 %all-gather.2.cloned.1.call-done.rows_ref = bf16[16384,256]{1,0:T(8,128)(2,1)} async-done(((bf16[1024,256]{1,0:T(8,128)(2,1)}), bf16[16384,256]{1,0:T(8,128)(2,1)}) %all-gather.2.cloned.1.call-update) | async-done | bytes 8388624 | tf_op jit(solution)/shard_map/all_gather | solution.py:985
  116.3 0.0 copy-done.7
  116.3 0.0 copy-done.8
  116.3 0.0 copy-start.4
  116.3 0.0 copy-start.5
  116.3 0.0 copy-start.6
  116.3 22.4 %forward_layer.1 = (bf16[1024,256]{1,0:T(8,128)(2,1)}, bf16[256,1024]{1,0:T(8,128)(2,1)}, bf16[512,256]{1,0:T(8,128)(2,1)}, f32[1024,256]{1,0:T(8,128)}, f32[8,72,256]{2,1,0:T(8,128)}) custom-call(bf16[1024,16384]{1,0:T(8,128)(2,1)} %get-tuple-element.33.counts_ref, bf16[16384,256]{1,0:T(8,128)(2,1)} %all-gather.2.cloned.1.call-done.rows_ref, ...), custom_call_target="tpu_custom_call" | custom-call | tf_op jit(solution)/shard_map/forward_layer/pallas_call | solution.py:671
  138.7 54.6 %reduce_sources.1 = (f32[1024,256]{1,0:T(8,128)}, f32[72,256]{1,0:T(8,128)}) custom-call(bf16[1024,16384]{1,0:T(8,128)(2,1)} %get-tuple-element.33.counts_ref, bf16[256,1024]{1,0:T(8,128)(2,1)} %get-tuple-element.40.grad_ref, f32[8,72,256]{2,1,0:T(8,128)} %get-tuple-element.41.weights_ref, bf16[512,256]{1,0:T(8,128)(2,1)} %get-tuple-element.42.halo_ref, ...), custom_call_target="tpu_custom_call" | custom-call | tf_op jit(solution)/shard_map/reduce_sources/pallas_call | solution.py:903
  193.4 1.2 copy-done
  194.6 0.9 copy-done.3
  195.5 39.3 %spread_grads.1 = (f32[1024,256]{1,0:T(8,128)S(1)}, f32[1024,256]{1,0:T(8,128)S(1)}, f32[512,256]{1,0:T(8,128)S(1)}, f32[8,128]{1,0:T(8,128)S(1)}) custom-call(f32[1024,256]{1,0:T(8,128)S(1)} %copy-done, bf16[1024,256]{1,0:T(8,128)(2,1)S(1)} %copy-done.1, bf16[1024,256]{1,0:T(8,128)(2,1)S(1)} %copy-done.2, s32[1,1024]{1,0:T(1,128)S(1)} %copy-done.6, ...), custom_call_target="tpu_custom_call" | custom-call | tf_op jit(solution)/shard_map/spread_grads/pallas_call | solution.py:570
  234.8 0.6 reshape.19
  235.4 0.8 fusion
  236.2 1.0 copy.20
  237.2 1.0 copy.21
  (10 shorter events, 0.0 us)
Async XLA Ops:
  7.2 109.1 %all-gather.2.cloned.1.call-start = ((), (), s32[]{:S(2)}) async-start(), calls=%async_computation | async-start | bytes 8912896 | tf_op jit(solution)/shard_map/all_gather | solution.py:985
  47.4 65.5 %collective-permute-start = (bf16[256,256]{1,0:T(8,128)(2,1)}, bf16[256,256]{1,0:T(8,128)(2,1)S(1)}, u32[]{:S(2)}, u32[]{:S(2)}) collective-permute-start(bf16[256,256]{1,0:T(8,128)(2,1)} %get-tuple-element.36), channel_id=1, source_target_pairs={{112,0},{0,16},{16,32},{32,48},{48,64},{64,80},{80,96},{96,112},{1... | collective-permute-start | bytes 393224 | tf_op jit(solution)/shard_map/ppermute | solution.py:947
  48.9 64.0 %collective-permute-start.1 = (bf16[256,256]{1,0:T(8,128)(2,1)}, bf16[256,256]{1,0:T(8,128)(2,1)S(1)}, u32[]{:S(2)}, u32[]{:S(2)}) collective-permute-start(bf16[256,256]{1,0:T(8,128)(2,1)} %get-tuple-element.37), channel_id=1, source_target_pairs={{16,0},{32,16},{48,32},{64,48},{80,64},{96,80},{112,96},{0,112},{1... | collective-permute-start | bytes 393224 | tf_op jit(solution)/shard_map/ppermute | solution.py:947
  112.9 3.4 %copy-start.7 = (bf16[256,256]{1,0:T(8,128)(2,1)}, bf16[256,256]{1,0:T(8,128)(2,1)S(1)}, u32[]{:S(2)}) copy-start(bf16[256,256]{1,0:T(8,128)(2,1)S(1)} %collective-permute-done.low_ref) | copy-start | bytes 393220
  112.9 3.4 %copy-start.8 = (bf16[256,256]{1,0:T(8,128)(2,1)}, bf16[256,256]{1,0:T(8,128)(2,1)S(1)}, u32[]{:S(2)}) copy-start(bf16[256,256]{1,0:T(8,128)(2,1)S(1)} %collective-permute-done.1.high_ref) | copy-start | bytes 393220
  116.3 77.0 %copy-start.1 = (bf16[1024,256]{1,0:T(8,128)(2,1)S(1)}, bf16[1024,256]{1,0:T(8,128)(2,1)}, u32[]{:S(2)}) copy-start(bf16[1024,256]{1,0:T(8,128)(2,1)} %get-tuple-element.45.qv_ref) | copy-start | bytes 1572868
  116.3 77.0 %copy-start.2 = (bf16[1024,256]{1,0:T(8,128)(2,1)S(1)}, bf16[1024,256]{1,0:T(8,128)(2,1)}, u32[]{:S(2)}) copy-start(bf16[1024,256]{1,0:T(8,128)(2,1)} %get-tuple-element.46.rv_ref) | copy-start | bytes 1572868
  116.3 77.1 %copy-start.4 = (s32[1024]{0:T(1024)S(1)}, s32[1024]{0:T(1024)}, u32[]{:S(2)}) copy-start(s32[1024]{0:T(1024)} %param.14) | copy-start | bytes 12292
  116.3 77.1 %copy-start.5 = (s32[1,2048]{1,0:T(1,128)S(1)}, s32[1,2048]{1,0:T(1,128)}, u32[]{:S(2)}) copy-start(s32[1,2048]{1,0:T(1,128)} %get-tuple-element.48.asked_ref) | copy-start | bytes 24580
  116.3 77.1 %copy-start.6 = (s32[1,1024]{1,0:T(1,128)S(1)}, s32[1,1024]{1,0:T(1,128)}, u32[]{:S(2)}) copy-start(s32[1,1024]{1,0:T(1,128)} %get-tuple-element.47.slot_ref) | copy-start | bytes 12292
  193.4 1.2 copy-start
  194.6 0.9 copy-start.3
Sparse Core Ops, SparseCore 0:
  47.5 68.7 all-gather.1

commit v9 on v8

--- a/solution.py
+++ b/solution.py
@@ -518,9 +518,8 @@
 
     lax.fori_loop(1, peers, send_sums, 0)
     lax.fori_loop(1, devices, send_rem, 0)
-    lax.fori_loop(0, devices // step, send_grads, 0)
+    lax.fori_loop(0, devices // step // 2, send_grads, 0)
     keep(rem_ref.at[tile(me)], rem_in.at[me])
-    keep(grads_ref.at[slot(me)], grads_in.at[slot(me)])
     keep(sums_ref.at[share(blk)], sums_in.at[blk, pl.ds(0, 8), :])
     keep(sums_ref.at[pl.ds(high, 8), pl.ds(0, wide)], sums_in.at[blk, pl.ds(8, 8), :])
     drain(sums_in.at[pl.ds(0, peers - 1)], sems.at[8])
@@ -529,9 +528,11 @@
     piece[tall:] = (jnp.sum(sums_in[...], axis=0) * scale).astype(jnp.bfloat16)
     lax.fori_loop(1, half, send_total, 0)
     keep(piece, whole.at[me])
-    drain(grads_in.at[pl.ds(0, slots - slot_cap)], sems.at[3])
+    lax.fori_loop(devices // step // 2, devices // step, send_grads, 0)
+    keep(grads_ref.at[slot(me)], grads_in.at[slot(me)])
     drain(whole.at[pl.ds(0, half - 1)], sems.at[5])
     lax.fori_loop(0, half // peers, relay, 0)
+    drain(grads_in.at[pl.ds(0, slots - slot_cap)], sems.at[3])
 
     def collect(r, carry):
         quot_ref[cut(r), :] = dot(pick_rows(asked_ref[...], r * size, size), grads_in[...])

time: 246 us -> 247 us (level)
  waiting for transfers between devices: 3.4 us -> 10 us
  Pallas kernels: 220 us -> 214 us
    all_gather x1, waiting for transfers between devices: 3.38 us -> 10 us  [per_device(): part_gathered = lax.all_gather(features, 'blk', axis=0, tiled=True)]
    pallas_call x1, Pallas kernels: 64 us -> 57.3 us  [build_counts(): pl.pallas_call(functools.partial(count_kernel, dump), grid=(blocks + 1,),...]
  transfers between devices with their start and end apart: 3 -> 3, of which waited for: 1 -> 1; matrix products, arithmetic and copies ran while one was open for 0% -> 0% of each run, Pallas kernels for 26% -> 23%
where the time goes in v9:
time: 247 us; the launch traced here: 246 us
  Pallas kernels  214 us (87%)
  between operations  14.2 us (6%)
  waiting for transfers between devices  10 us (4%)
  local copies, waits for them, and re-layouts  5.53 us (2%)
    pallas_call x1, Pallas kernels, build_counts(): pl.pallas_call(functools.partial(count_kernel, dump), grid=(blocks + 1,),...  57.3 us
    pallas_call x1, Pallas kernels, reduce_sources(): pl.pallas_call(reduce_kernel, out_shape=(jax.ShapeDtypeStruct((nodes, fea...  55.7 us
    pallas_call x1, Pallas kernels, fetch_rows(): pl.pallas_call(functools.partial(fetch_kernel, devices, dump), out_shape=...  40.1 us
    pallas_call x1, Pallas kernels, spread_grads(): pl.pallas_call(functools.partial(spread_kernel, devices, rem_scale, scale...  39 us
    pallas_call x1, Pallas kernels, forward(): pl.pallas_call(forward_kernel, grid=(steps,), out_shape=out_shape, in_spe...  22.4 us
    all_gather x1, waiting for transfers between devices, per_device(): part_gathered = lax.all_gather(features, 'blk', axis=0, tiled=True)  10 us
  transfers between devices with their start and end apart: 3, of which 1 were waited for; matrix products, arithmetic and copies ran while one was open for 0% of the time, Pallas kernels for 23%

profile of v9, /device:TPU:1, one launch (start us, length us, event | category | flops | bytes accessed | tf_op | source)
XLA Modules:
  0.0 245.8 jit_solution(14197415057981928500)
XLA Ops:
  7.2 0.0 all-gather.2.cloned.1.call-start
  7.2 40.1 %fetch_rows.1 = (bf16[1024,256]{1,0:T(8,128)(2,1)}, bf16[1024,256]{1,0:T(8,128)(2,1)}, bf16[1024,256]{1,0:T(8,128)(2,1)}, s32[1,2048]{1,0:T(1,128)}, s32[1,1024]...) custom-call(s32[1,1024]{1,0:T(1,128)} %bitcast.8, ...), custom_call_target="tpu_custom_call" | custom-call | tf_op jit(solution)/shard_map/fetch_rows/pallas_call | solution.py:390
  47.3 0.0 all-gather.2.cloned.1.call-update
  47.4 1.6 collective-permute-start
  48.9 0.0 collective-permute-start.1
  48.9 57.3 %edge_counts.1 = (bf16[1024,16384]{1,0:T(8,128)(2,1)}, bf16[1024,512]{1,0:T(8,128)(2,1)}, f32[1024,1]{1,0:T(8,128)}) custom-call(s32[8]{0:T(128)} %count_ref.3, s32[8,1,6144]{2,1,0:T(1,128)} %get-tuple-element.30.fast_ref, s32[8,1,6144]{2,1,0:T(1,128)} %get-tuple-element.31.slow_ref, s32[8,1,128]{2,1,0:T(1,128)} %get-tuple-element.32.flag_ref), custom_call_target="tpu_custom_call" | custom-call | flops 80000000000 | bytes 40000000 | tf_op jit(solution)/shard_map/edge_counts/pallas_call | solution.py:158
  106.2 0.0 collective-permute-done.low_ref
  106.3 0.0 collective-permute-done.1.high_ref
  106.3 0.0 copy-start.8
  106.3 10.0 %all-gather.2.cloned.1.call-done.rows_ref = bf16[16384,256]{1,0:T(8,128)(2,1)} async-done(((bf16[1024,256]{1,0:T(8,128)(2,1)}), bf16[16384,256]{1,0:T(8,128)(2,1)}) %all-gather.2.cloned.1.call-update) | async-done | bytes 8388624 | tf_op jit(solution)/shard_map/all_gather | solution.py:986
  116.3 0.0 copy-done.7
  116.3 0.0 copy-done.8
  116.3 0.0 copy-start.4
  116.3 0.0 copy-start.5
  116.3 0.0 copy-start.6
  116.3 22.4 %forward_layer.1 = (bf16[1024,256]{1,0:T(8,128)(2,1)}, bf16[256,1024]{1,0:T(8,128)(2,1)}, bf16[512,256]{1,0:T(8,128)(2,1)}, f32[1024,256]{1,0:T(8,128)}, f32[8,72,256]{2,1,0:T(8,128)}) custom-call(bf16[1024,16384]{1,0:T(8,128)(2,1)} %get-tuple-element.33.counts_ref, bf16[16384,256]{1,0:T(8,128)(2,1)} %all-gather.2.cloned.1.call-done.rows_ref, ...), custom_call_target="tpu_custom_call" | custom-call | tf_op jit(solution)/shard_map/forward_layer/pallas_call | solution.py:672
  138.7 55.7 %reduce_sources.1 = (f32[1024,256]{1,0:T(8,128)}, f32[72,256]{1,0:T(8,128)}) custom-call(bf16[1024,16384]{1,0:T(8,128)(2,1)} %get-tuple-element.33.counts_ref, bf16[256,1024]{1,0:T(8,128)(2,1)} %get-tuple-element.40.grad_ref, f32[8,72,256]{2,1,0:T(8,128)} %get-tuple-element.41.weights_ref, bf16[512,256]{1,0:T(8,128)(2,1)} %get-tuple-element.42.halo_ref, ...), custom_call_target="tpu_custom_call" | custom-call | tf_op jit(solution)/shard_map/reduce_sources/pallas_call | solution.py:904
  194.4 1.2 copy-done
  195.6 0.9 copy-done.3
  196.5 39.0 %spread_grads.1 = (f32[1024,256]{1,0:T(8,128)S(1)}, f32[1024,256]{1,0:T(8,128)S(1)}, f32[512,256]{1,0:T(8,128)S(1)}, f32[8,128]{1,0:T(8,128)S(1)}) custom-call(f32[1024,256]{1,0:T(8,128)S(1)} %copy-done, bf16[1024,256]{1,0:T(8,128)(2,1)S(1)} %copy-done.1, bf16[1024,256]{1,0:T(8,128)(2,1)S(1)} %copy-done.2, s32[1,1024]{1,0:T(1,128)S(1)} %copy-done.6, ...), custom_call_target="tpu_custom_call" | custom-call | tf_op jit(solution)/shard_map/spread_grads/pallas_call | solution.py:571
  235.6 0.6 reshape.19
  236.2 0.8 fusion
  237.0 1.0 copy.20
  238.0 1.0 copy.21
  (10 shorter events, 0.0 us)
Async XLA Ops:
  7.2 109.1 %all-gather.2.cloned.1.call-start = ((), (), s32[]{:S(2)}) async-start(), calls=%async_computation | async-start | bytes 8912896 | tf_op jit(solution)/shard_map/all_gather | solution.py:986
  47.4 58.9 %collective-permute-start = (bf16[256,256]{1,0:T(8,128)(2,1)}, bf16[256,256]{1,0:T(8,128)(2,1)S(1)}, u32[]{:S(2)}, u32[]{:S(2)}) collective-permute-start(bf16[256,256]{1,0:T(8,128)(2,1)} %get-tuple-element.36), channel_id=1, source_target_pairs={{112,0},{0,16},{16,32},{32,48},{48,64},{64,80},{80,96},{96,112},{1... | collective-permute-start | bytes 393224 | tf_op jit(solution)/shard_map/ppermute | solution.py:948
  48.9 57.4 %collective-permute-start.1 = (bf16[256,256]{1,0:T(8,128)(2,1)}, bf16[256,256]{1,0:T(8,128)(2,1)S(1)}, u32[]{:S(2)}, u32[]{:S(2)}) collective-permute-start(bf16[256,256]{1,0:T(8,128)(2,1)} %get-tuple-element.37), channel_id=1, source_target_pairs={{16,0},{32,16},{48,32},{64,48},{80,64},{96,80},{112,96},{0,112},{1... | collective-permute-start | bytes 393224 | tf_op jit(solution)/shard_map/ppermute | solution.py:948
  106.2 10.1 %copy-start.7 = (bf16[256,256]{1,0:T(8,128)(2,1)}, bf16[256,256]{1,0:T(8,128)(2,1)S(1)}, u32[]{:S(2)}) copy-start(bf16[256,256]{1,0:T(8,128)(2,1)S(1)} %collective-permute-done.low_ref) | copy-start | bytes 393220
  106.3 10.0 %copy-start.8 = (bf16[256,256]{1,0:T(8,128)(2,1)}, bf16[256,256]{1,0:T(8,128)(2,1)S(1)}, u32[]{:S(2)}) copy-start(bf16[256,256]{1,0:T(8,128)(2,1)S(1)} %collective-permute-done.1.high_ref) | copy-start | bytes 393220
  116.3 78.1 %copy-start.1 = (bf16[1024,256]{1,0:T(8,128)(2,1)S(1)}, bf16[1024,256]{1,0:T(8,128)(2,1)}, u32[]{:S(2)}) copy-start(bf16[1024,256]{1,0:T(8,128)(2,1)} %get-tuple-element.45.qv_ref) | copy-start | bytes 1572868
  116.3 78.1 %copy-start.2 = (bf16[1024,256]{1,0:T(8,128)(2,1)S(1)}, bf16[1024,256]{1,0:T(8,128)(2,1)}, u32[]{:S(2)}) copy-start(bf16[1024,256]{1,0:T(8,128)(2,1)} %get-tuple-element.46.rv_ref) | copy-start | bytes 1572868
  116.3 78.1 %copy-start.4 = (s32[1024]{0:T(1024)S(1)}, s32[1024]{0:T(1024)}, u32[]{:S(2)}) copy-start(s32[1024]{0:T(1024)} %param.14) | copy-start | bytes 12292
  116.3 78.1 %copy-start.5 = (s32[1,2048]{1,0:T(1,128)S(1)}, s32[1,2048]{1,0:T(1,128)}, u32[]{:S(2)}) copy-start(s32[1,2048]{1,0:T(1,128)} %get-tuple-element.48.asked_ref) | copy-start | bytes 24580
  116.3 78.1 %copy-start.6 = (s32[1,1024]{1,0:T(1,128)S(1)}, s32[1,1024]{1,0:T(1,128)}, u32[]{:S(2)}) copy-start(s32[1,1024]{1,0:T(1,128)} %get-tuple-element.47.slot_ref) | copy-start | bytes 12292
  194.4 1.2 copy-start
  195.6 0.9 copy-start.3
Sparse Core Ops, SparseCore 0:
  47.5 68.7 all-gather.1
